TPU v7x, 32 devices: a whole 2x2x4 slice. The times are simulated.
32 devices in a mesh: dp: 4 (over y, core), seq: 8 (over z, x).
Axes of the slice: x: 2, y: 2, z: 4, core: 2. Of those that a mesh axis runs over, the one named last changes fastest.
Arguments:
- inputs: bfloat16 [20480, 512], P(('dp', 'seq')), may hold values from -6 to 6
- cotangent: bfloat16 [20480, 512], P(('dp', 'seq')), may hold values from -6 to 6
- block_segment: int32 [160], P('dp'), may hold values from 0 to 39, as said below
- segment_parent: int32 [160], P('dp'), may hold values from -1 to 39, as said below
- query_weight: bfloat16 [512, 512], P(('dp', 'seq')), may hold values from -0.5 to 0.5
- key_weight: bfloat16 [512, 512], P(('dp', 'seq')), may hold values from -0.25 to 0.25
- value_weight: bfloat16 [512, 512], P(('dp', 'seq')), may hold values from -0.25 to 0.25
- output_weight: bfloat16 [512, 512], P(('dp', 'seq')), may hold values from -1 to 1
- gate_weight: bfloat16 [512, 512], P(('dp', 'seq')), may hold values from -0.25 to 0.25
- gate_bias: bfloat16 [512], P(('dp', 'seq')), may hold values from -3 to 3
- up_weight: bfloat16 [512, 2048], P(('dp', 'seq')), may hold values from -0.25 to 0.25
- up_bias: bfloat16 [2048], P(('dp', 'seq')), may hold values from -3 to 3
- down_weight: bfloat16 [2048, 512], P(('dp', 'seq')), may hold values from -0.125 to 0.125
- down_bias: bfloat16 [512], P(('dp', 'seq')), may hold values from -3 to 3
- carry_weight: bfloat16 [512, 512], P(('dp', 'seq')), may hold values from -0.25 to 0.25
- carry_bias: bfloat16 [512], P(('dp', 'seq')), may hold values from -3 to 3
- first_gain: bfloat16 [512], P(('dp', 'seq')), may hold values from 0.25 to 1.75
- first_shift: bfloat16 [512], P(('dp', 'seq')), may hold values from -2 to 2
- second_gain: bfloat16 [512], P(('dp', 'seq')), may hold values from 0.25 to 1.75
- second_shift: bfloat16 [512], P(('dp', 'seq')), may hold values from -2 to 2
Outputs:
- output: bfloat16 [20480, 512], P(('dp', 'seq'))
- input_grad: float32 [20480, 512], P(('dp', 'seq'))
- query_weight_grad: float32 [512, 512], P(('dp', 'seq'))
- key_weight_grad: float32 [512, 512], P(('dp', 'seq'))
- value_weight_grad: float32 [512, 512], P(('dp', 'seq'))
- output_weight_grad: float32 [512, 512], P(('dp', 'seq'))
- gate_weight_grad: float32 [512, 512], P(('dp', 'seq'))
- gate_bias_grad: float32 [512], P(('dp', 'seq'))
- up_weight_grad: float32 [512, 2048], P(('dp', 'seq'))
- up_bias_grad: float32 [2048], P(('dp', 'seq'))
- down_weight_grad: float32 [2048, 512], P(('dp', 'seq'))
- down_bias_grad: float32 [512], P(('dp', 'seq'))
- carry_weight_grad: float32 [512, 512], P(('dp', 'seq'))
- carry_bias_grad: float32 [512], P(('dp', 'seq'))
- first_gain_grad: float32 [512], P(('dp', 'seq'))
- first_shift_grad: float32 [512], P(('dp', 'seq'))
- second_gain_grad: float32 [512], P(('dp', 'seq'))
- second_shift_grad: float32 [512], P(('dp', 'seq'))
Inputs may be any that keep to these rules, and one draw needn't show every extreme that they name: `segment_parent`: entry s of a dp group's 40 entries is the parent of segment s of that group, or -1 for a root. The group's segments form 2 trees of 20 segments: a chain of 8 from the root, 4 children of the chain's last segment, and 2 children of each of those. `block_segment`: each dp group's 40 entries are a permutation of its segment numbers; entry j names the segment held in slot j, on the device of index j // 5 along seq.
All inputs are finite; a program needn't handle non-finite values.
Results may differ from a plain program's by a relative error of at most 0.035.
Values may be sent and summed in bfloat16 or wider, within the bound.
No kernel may reach another device: no remote copies, remote signals or barrier semaphores. Data moves between devices by JAX's collectives and lax.ppermute only.
A program may use at most 256 MiB of HBM per device.

v0:
```python
import functools

import jax
import jax.numpy as jnp
from jax import lax
from jax.experimental import pallas as pl
from jax.experimental.pallas import tpu as pltpu
from jax.sharding import PartitionSpec as P

HD = 64
BLK = 128
DEPTH = 10
PAIR = 2 * HD
PLACES = 4
TREE_BLOCKS = 20
TRUNK = 8

EPSILON = 1e-05
NEGATIVE = -1e30
BOTH = ("dp", "seq")
VMEM_BYTES = 60 * 1024 * 1024


def normalize(values, norm_gain, norm_shift):
    center = values - jnp.mean(values, axis=-1, keepdims=True)
    spread = jnp.mean(center * center, axis=-1, keepdims=True)
    return center * lax.rsqrt(spread + EPSILON) * norm_gain + norm_shift


def matmul(left_side, right_side):
    return jnp.dot(left_side, right_side, preferred_element_type=jnp.float32)


def inner_rows(left_side, right_side):
    return lax.dot_general(
        left_side, right_side, (((0,), (0,)), ((), ())), preferred_element_type=jnp.float32
    )


def against(left_side, right_side):
    return lax.dot_general(
        left_side, right_side, (((1,), (1,)), ((), ())), preferred_element_type=jnp.float32
    )


def column_sums(values):
    return jnp.sum(values.astype(jnp.float32), axis=0)


def lookup(lookup_table, wanted):
    entries = jnp.arange(lookup_table.shape[0], dtype=jnp.int32)
    matches = wanted[..., None] == entries
    located = jnp.sum(jnp.where(matches, lookup_table, jnp.int32(0)), axis=-1, dtype=jnp.int32)
    return jnp.where(wanted >= 0, located, jnp.int32(-1))


def ancestor_slots(block_segment, segment_parent, own_segments):
    entries = jnp.arange(block_segment.shape[0], dtype=jnp.int32)
    placed = block_segment[None, :] == entries[:, None]
    slot_of = jnp.sum(jnp.where(placed, entries[None, :], jnp.int32(0)), axis=1, dtype=jnp.int32)
    current = own_segments
    lineage = []
    for depth_step in range(DEPTH):
        lineage.append(current)
        current = lookup(segment_parent, current)
    lineage = jnp.stack(lineage, axis=-1)
    usable = lineage >= 0
    return (jnp.where(usable, lookup(slot_of, lineage), jnp.int32(0)), usable)


def stack_heads(rows):
    lane = lax.broadcasted_iota(jnp.int32, rows.shape, 1)
    low = lane < HD
    zero = jnp.zeros_like(rows)
    return jnp.concatenate([jnp.where(low, rows, zero), jnp.where(low, zero, rows)], axis=0)


def unstack_heads(rows):
    half = rows.shape[0] // 2
    lane = lax.broadcasted_iota(jnp.int32, (half, rows.shape[1]), 1)
    return jnp.where(lane < HD, rows[:half], rows[half:])


def make_bias(levels, bias_ref):
    row = lax.broadcasted_iota(jnp.int32, (BLK, DEPTH * BLK), 0)
    col = lax.broadcasted_iota(jnp.int32, (BLK, DEPTH * BLK), 1)
    limit = jnp.where(col < BLK, row + 1, levels * BLK)
    bias = jnp.where(col < limit, jnp.float32(0.0), jnp.float32(NEGATIVE))
    bias_ref[:BLK, :] = bias
    bias_ref[BLK:, :] = bias


class Levels:
    def __init__(self, slots_ref, sources, targets, arrivals):
        self.slots_ref = slots_ref
        self.pairs = tuple(zip(sources, targets))
        self.arrivals = arrivals

    def copies(self, slot):
        turn = slot % 2
        for level in range(DEPTH):
            start = pl.multiple_of(self.slots_ref[slot, level] * BLK, BLK)
            for index, (source, target) in enumerate(self.pairs):
                place = target.at[turn, level * BLK : (level + 1) * BLK, :]
                yield pltpu.make_async_copy(
                    source.at[pl.ds(start, BLK), :], place, self.arrivals.at[turn, index, level]
                )

    def start(self, slot):
        for copy in self.copies(slot):
            copy.start()

    def step(self, slot, count):
        @pl.when(slot + 1 < count)
        def ahead():
            self.start(slot + 1)

        for copy in self.copies(slot):
            copy.wait()


def forward_kernel(
    slots_ref, query_ref, key_source, value_source, mixed_ref, logsum_ref, key_here, value_here, bias_ref, arrivals
):
    width = query_ref.shape[1]
    count = query_ref.shape[0] // BLK
    levels = Levels(slots_ref, (key_source, value_source), (key_here, value_here), arrivals)
    levels.start(0)

    def one_slot(slot, carry):
        rows = pl.ds(pl.multiple_of(slot * BLK, BLK), BLK)
        make_bias(slots_ref[slot, DEPTH], bias_ref)
        levels.step(slot, count)
        turn = slot % 2
        lane = lax.broadcasted_iota(jnp.int32, (BLK, PAIR), 1)
        logsums = jnp.zeros((BLK, PAIR), jnp.float32)
        for pair in range(width // PAIR):
            cols = slice(pair * PAIR, (pair + 1) * PAIR)
            stacked = stack_heads(query_ref[rows, cols])
            scores = against(stacked, key_here[turn, :, cols]) + bias_ref[...]
            highest = jnp.max(scores, axis=-1, keepdims=True)
            raised = jnp.exp(scores - highest)
            total = jnp.sum(raised, axis=-1, keepdims=True)
            mixed = matmul(raised.astype(jnp.bfloat16), value_here[turn, :, cols]) / total
            mixed_ref[rows, cols] = unstack_heads(mixed).astype(jnp.bfloat16)
            logsum = highest + jnp.log(total)
            logsums = jnp.where(lane == 2 * pair, logsum[:BLK], logsums)
            logsums = jnp.where(lane == 2 * pair + 1, logsum[BLK:], logsums)
        logsum_ref[rows, :] = logsums
        return carry

    lax.fori_loop(0, count, one_slot, 0)


def backward_kernel(
    slots_ref,
    compact_ref,
    used_ref,
    seen_ref,
    query_ref,
    key_source,
    value_source,
    logsum_ref,
    mixed_ref,
    mixed_grad_ref,
    normed_source,
    weight_ref,
    query_grad_ref,
    grads_ref,
    lanes_ref,
    shared_ref,
    key_here,
    value_here,
    bias_ref,
    normed_here,
    key_sums,
    value_sums,
    stage,
    zero_block,
    arrivals,
    normed_arrivals,
    departures,
):
    width = query_ref.shape[1]
    count = query_ref.shape[0] // BLK
    places = used_ref.shape[1] - 1
    used_count = used_ref[0, places]
    levels = Levels(slots_ref, (key_source, value_source), (key_here, value_here), arrivals)
    levels.start(0)

    def normed_copy(place):
        source = pl.ds(pl.multiple_of(used_ref[0, place] * BLK, BLK), BLK)
        target = normed_here.at[place * BLK : (place + 1) * BLK, :]
        return pltpu.make_async_copy(normed_source.at[source, :], target, normed_arrivals.at[place])

    for place in range(places):

        @pl.when(place < used_count)
        def fetch():
            normed_copy(place).start()

        @pl.when(place >= used_count)
        def clear():
            normed_here[place * BLK : (place + 1) * BLK, :] = jnp.zeros((BLK, normed_here.shape[1]), jnp.bfloat16)

    zero_block[...] = jnp.zeros_like(zero_block)
    for slot in range(shared_ref.shape[0]):

        @pl.when(seen_ref[0, slot] == 0)
        def none():
            pltpu.make_async_copy(zero_block, shared_ref.at[slot], departures.at[slot]).start()

    key_sums[...] = jnp.zeros_like(key_sums)
    value_sums[...] = jnp.zeros_like(value_sums)

    def one_slot(slot, carry):
        rows = pl.ds(pl.multiple_of(slot * BLK, BLK), BLK)
        make_bias(slots_ref[slot, DEPTH], bias_ref)
        levels.step(slot, count)
        turn = slot % 2
        for pair in range(width // PAIR):
            cols = slice(pair * PAIR, (pair + 1) * PAIR)
            stacked = stack_heads(query_ref[rows, cols])
            grad_rows = mixed_grad_ref[rows, cols]
            grad_stacked = stack_heads(grad_rows)
            products = grad_rows.astype(jnp.float32) * mixed_ref[rows, cols].astype(jnp.float32)
            row_dot = jnp.sum(stack_heads(products), axis=-1, keepdims=True)
            logsum = jnp.concatenate(
                [logsum_ref[rows, 2 * pair : 2 * pair + 1], logsum_ref[rows, 2 * pair + 1 : 2 * pair + 2]], axis=0
            )
            key_rows = key_here[turn, :, cols]
            shares = jnp.exp(against(stacked, key_rows) + bias_ref[...] - logsum)
            share_grad = against(grad_stacked, value_here[turn, :, cols])
            score_grad = (shares * (share_grad - row_dot)).astype(jnp.bfloat16)
            query_grad = unstack_heads(matmul(score_grad, key_rows)) * (HD ** (-0.5))
            query_grad_ref[rows, cols] = query_grad.astype(jnp.bfloat16)
            key_part = inner_rows(stacked, score_grad)
            value_part = inner_rows(grad_stacked, shares.astype(jnp.bfloat16))
            for level in range(DEPTH):
                start = pl.multiple_of(compact_ref[slot, level] * BLK, BLK)
                here = slice(level * BLK, (level + 1) * BLK)
                key_sums[cols, pl.ds(start, BLK)] += key_part[:, here]
                value_sums[cols, pl.ds(start, BLK)] += value_part[:, here]
        return carry

    lax.fori_loop(0, count, one_slot, 0)

    for place in range(places):

        @pl.when(place < used_count)
        def arrived():
            normed_copy(place).wait()

    grads_ref[...] = jnp.zeros_like(grads_ref)
    lanes_ref[...] = jnp.zeros_like(lanes_ref)

    def some_places(step, carry):
        here = pl.ds(pl.multiple_of(step * (PLACES * BLK), PLACES * BLK), PLACES * BLK)
        shared = None
        for part, part_sums in enumerate((key_sums, value_sums)):
            lines = slice(part * width, (part + 1) * width)
            block = part_sums[:, here]
            tiles = [block[:, start : start + BLK] for start in range(0, PLACES * BLK, BLK)]
            lanes_ref[lines, :] += functools.reduce(lambda left, right: left + right, tiles)
            block = block.astype(jnp.bfloat16)
            product = matmul(weight_ref[:, lines], block)
            shared = product if shared is None else shared + product
            grads_ref[lines, :] += matmul(block, normed_here[here, :])
        for index in range(PLACES):
            place = step * PLACES + index
            stage[place] = shared[:, index * BLK : (index + 1) * BLK].astype(jnp.bfloat16)

            @pl.when(place < used_count)
            def leave():
                slot = used_ref[0, place]
                pltpu.make_async_copy(stage.at[place], shared_ref.at[slot], departures.at[slot]).start()

        return carry

    lax.fori_loop(0, (used_count + PLACES - 1) // PLACES, some_places, 0)
    for slot in range(shared_ref.shape[0]):
        pltpu.make_async_copy(zero_block, shared_ref.at[slot], departures.at[slot]).wait()


def about(cost):
    return pl.CostEstimate(flops=int(cost * 1e9), bytes_accessed=int(cost * 1e6), transcendentals=0)


def in_vmem():
    return pl.BlockSpec(memory_space=pltpu.VMEM)


def in_smem():
    return pl.BlockSpec(memory_space=pltpu.SMEM)


def anywhere():
    return pl.BlockSpec(memory_space=pl.ANY)


def level_scratch(width):
    return [
        pltpu.VMEM((2, DEPTH * BLK, width), jnp.bfloat16),
        pltpu.VMEM((2, DEPTH * BLK, width), jnp.bfloat16),
        pltpu.VMEM((2 * BLK, DEPTH * BLK), jnp.float32),
    ]


def attend(slots, query_rows, key_group, value_group):
    rows, width = query_rows.shape
    return pl.pallas_call(
        forward_kernel,
        cost_estimate=about(18),
        out_shape=(
            jax.ShapeDtypeStruct((rows, width), jnp.bfloat16),
            jax.ShapeDtypeStruct((rows, PAIR), jnp.float32),
        ),
        in_specs=[in_smem(), in_vmem(), anywhere(), anywhere()],
        out_specs=(in_vmem(), in_vmem()),
        scratch_shapes=level_scratch(width) + [pltpu.SemaphoreType.DMA((2, 2, DEPTH))],
        compiler_params=pltpu.CompilerParams(vmem_limit_bytes=VMEM_BYTES),
    )(slots, query_rows, key_group, value_group)


def attend_backward(tables, query_rows, key_group, value_group, logsum, mixed, mixed_grad, normed_group, both_weight):
    rows, width = query_rows.shape
    blocks = normed_group.shape[0] // BLK
    places = tables[2].shape[1] - 1
    return pl.pallas_call(
        backward_kernel,
        cost_estimate=about(32),
        out_shape=(
            jax.ShapeDtypeStruct((rows, width), jnp.bfloat16),
            jax.ShapeDtypeStruct((2 * width, width), jnp.float32),
            jax.ShapeDtypeStruct((2 * width, BLK), jnp.float32),
            jax.ShapeDtypeStruct((blocks, width, BLK), jnp.bfloat16),
        ),
        in_specs=[in_smem()] * 4
        + [in_vmem(), anywhere(), anywhere(), in_vmem(), in_vmem(), in_vmem(), anywhere(), in_vmem()],
        out_specs=(in_vmem(), in_vmem(), in_vmem(), anywhere()),
        scratch_shapes=level_scratch(width)
        + [
            pltpu.VMEM((places * BLK, width), jnp.bfloat16),
            pltpu.VMEM((width, places * BLK), jnp.float32),
            pltpu.VMEM((width, places * BLK), jnp.float32),
            pltpu.VMEM((places, width, BLK), jnp.bfloat16),
            pltpu.VMEM((width, BLK), jnp.bfloat16),
            pltpu.SemaphoreType.DMA((2, 2, DEPTH)),
            pltpu.SemaphoreType.DMA((places,)),
            pltpu.SemaphoreType.DMA((blocks,)),
        ],
        compiler_params=pltpu.CompilerParams(vmem_limit_bytes=VMEM_BYTES),
    )(*tables, query_rows, key_group, value_group, logsum, mixed, mixed_grad, normed_group, both_weight)


def used_places(relative_slot, usable, group_blocks):
    block_count = relative_slot.shape[0]
    most = group_blocks // TREE_BLOCKS * TRUNK + 2 * block_count
    places = min(-(-most // PLACES) * PLACES, -(-group_blocks // PLACES) * PLACES)
    entries = jnp.arange(group_blocks, dtype=jnp.int32)
    hits = (relative_slot[:, :, None] == entries) & usable[:, :, None]
    seen = jnp.any(hits, axis=(0, 1))
    earlier = (entries[None, :] < entries[:, None]) & seen[None, :]
    place_of = jnp.sum(earlier, axis=1, dtype=jnp.int32)
    compact = jnp.sum(jnp.where(hits, place_of, jnp.int32(0)), axis=-1, dtype=jnp.int32)
    wanted = jnp.arange(places, dtype=jnp.int32)
    matches = (place_of[None, :] == wanted[:, None]) & seen[None, :]
    used = jnp.sum(jnp.where(matches, entries, jnp.int32(0)), axis=1, dtype=jnp.int32)
    seen = seen.astype(jnp.int32)
    used = jnp.concatenate([used, jnp.sum(seen, dtype=jnp.int32).reshape(1)])
    return compact, used.reshape(1, -1), seen.reshape(1, -1)


def project(pieces, vectors, key_weight, value_weight, group_rows, step, carried, query_weight=None):
    count = len(pieces)
    rows, width = pieces[0].shape
    weights = [key_weight, value_weight] + ([] if query_weight is None else [query_weight])
    extra = [] if carried is None else list(carried)

    def body(*refs):
        piece_refs, vectors_ref = refs[:count], refs[count]
        weight_refs = refs[count + 1 : count + 1 + len(weights)]
        outs = refs[count + 1 + len(weights) + len(extra) :]
        normed_ref, key_ref, value_ref = outs[:3]
        gain = vectors_ref[GAIN_ONE : GAIN_ONE + 1, :]
        shift = vectors_ref[SHIFT_ONE : SHIFT_ONE + 1, :]
        for index, piece in enumerate(piece_refs):
            here = slice(index * rows, (index + 1) * rows)
            normed = normalize(piece[...].astype(jnp.float32), gain, shift).astype(jnp.bfloat16)
            normed_ref[here, :] = normed
            key_ref[here, :] = matmul(normed, weight_refs[0][...]).astype(jnp.bfloat16)
            value_ref[here, :] = matmul(normed, weight_refs[1][...]).astype(jnp.bfloat16)
            if index == 0 and len(outs) > 3:
                outs[3][...] = normed
                queries = matmul(normed, weight_refs[2][...]).astype(jnp.bfloat16)
                outs[4][...] = (queries.astype(jnp.float32) * (HD ** (-0.5))).astype(jnp.bfloat16)

    block = pl.BlockSpec((count * rows, width), lambda index: (step, 0))
    whole = jax.ShapeDtypeStruct((group_rows, width), jnp.bfloat16)
    own = [] if query_weight is None else [jax.ShapeDtypeStruct((rows, width), jnp.bfloat16)] * 2
    first = count + 1 + len(weights)
    return pl.pallas_call(
        body,
        cost_estimate=about(4),
        grid=(1,),
        out_shape=[whole] * 3 + own,
        in_specs=[in_vmem()] * first + [pl.BlockSpec(memory_space=pl.ANY)] * len(extra),
        out_specs=[block] * 3 + [in_vmem()] * len(own),
        input_output_aliases={first + index: index for index in range(len(extra))},
        compiler_params=pltpu.CompilerParams(vmem_limit_bytes=VMEM_BYTES),
    )(*pieces, vectors, *weights, *extra)


class Axis:
    def __init__(self, name, size, stride):
        self.name = name
        self.size = size
        self.stride = stride

    def position(self):
        return lax.axis_index(self.name) // self.stride % self.size

    def rotate(self, values, shift):
        pairs = []
        for index in range(lax.axis_size(self.name)):
            here = index // self.stride % self.size
            there = (here + shift) % self.size
            pairs.append((index, index + (there - here) * self.stride))
        return lax.ppermute(values, self.name, pairs)


def axes():
    seq = lax.axis_size("seq")
    dp = lax.axis_size("dp")
    along_z = 4 if seq % 4 == 0 else 1
    cores = 2 if dp % 2 == 0 else 1
    return (
        Axis("seq", along_z, seq // along_z),
        Axis("seq", seq // along_z, 1),
        Axis("dp", dp // cores, cores),
        Axis("dp", cores, 1),
    )


def relative_devices():
    axis_z, axis_x, axis_y, axis_core = axes()

    def place(axis, dim):
        back = lax.broadcasted_iota(jnp.int32, (axis_core.size, axis_y.size, axis_x.size, axis_z.size), dim)
        return (axis.position() - back + axis.size) % axis.size

    dp_index = place(axis_y, 1) * axis_core.size + place(axis_core, 0)
    seq_index = place(axis_z, 3) * axis_x.size + place(axis_x, 2)
    return (dp_index * lax.axis_size("seq") + seq_index).reshape(-1)


def scatter_devices():
    axis_z, axis_x, axis_y, axis_core = axes()
    entries = relative_devices().reshape(-1, axis_x.size, axis_z.size)
    return jnp.swapaxes(entries, 1, 2).reshape(-1)


def add_low(left_side, right_side):
    return (left_side.astype(jnp.float32) + right_side.astype(jnp.float32)).astype(jnp.bfloat16)


def add_three(first, second, third):
    total = first.astype(jnp.float32) + second.astype(jnp.float32) + third.astype(jnp.float32)
    return total.astype(jnp.bfloat16)


def tied(values, after):
    return lax.optimization_barrier((values, after))[0]


def ring_scatter(entry, axis):
    running = entry(axis.size - 1)
    for back in range(axis.size - 1, 0, -1):
        running = add_low(axis.rotate(running, -1), entry(back - 1))
    return running


def pair_scatter(keep, send, axis):
    arrived = axis.rotate(send, -1)
    return lambda index: add_low(arrived[index], keep[index])


GATE_B, DOWN_B, CARRY_B, GAIN_ONE, SHIFT_ONE, GAIN_TWO, SHIFT_TWO, UP_B = range(8)
VECTOR_ROWS = 16
MIDDLE_ROWS = 640


def pack_kernel(devices, place_ref, *refs):
    early_sources, late_sources, vector_refs, (early_ref, late_ref) = refs[:4], refs[4:8], refs[8:16], refs[16:]
    width = early_ref.shape[1]
    for target, sources in ((early_ref, early_sources), (late_ref, late_sources)):
        start = 0
        for source in sources:
            rows = source.shape[0]
            for column in range(0, source.shape[1], width):
                target[start : start + rows, :] = source[:, column : column + width]
                start += rows
    block = jnp.zeros((VECTOR_ROWS, width), jnp.float32)
    line = lax.broadcasted_iota(jnp.int32, block.shape, 0)
    for index, source in enumerate(vector_refs):
        count = source.shape[1]
        feature = lax.broadcasted_iota(jnp.int32, (count, width), 0) + place_ref[0] * count
        column = lax.broadcasted_iota(jnp.int32, (count, width), 1)
        for part in range(count * devices // width):
            spot = jnp.where(feature == column + part * width, jnp.float32(1.0), jnp.float32(0.0))
            spread = matmul(source[...], spot.astype(jnp.bfloat16))
            block += jnp.where(line == index + part, spread, jnp.float32(0.0))
    early_ref[early_ref.shape[0] - VECTOR_ROWS :, :] = block.astype(jnp.bfloat16)


def unpack_kernel(place_ref, mine_ref, other_ref, query_ref, key_ref, value_ref, gate_ref, vectors_ref):
    half = mine_ref.shape[0]
    rows = (mine_ref.shape[1] - VECTOR_ROWS) // 4
    vectors = jnp.zeros(vectors_ref.shape, jnp.float32)
    for index in range(2 * half):
        source = (mine_ref if index < half else other_ref).at[index % half]
        target = pl.ds(pl.multiple_of(place_ref[index] * rows, rows), rows)
        for part, weight_ref in enumerate((query_ref, key_ref, value_ref, gate_ref)):
            weight_ref[target, :] = source[part * rows : (part + 1) * rows, :]
        vectors += source[4 * rows :, :].astype(jnp.float32)
    vectors_ref[...] = vectors


def unpack_late(place_ref, line_sources, plane_sources, output_ref, up_ref, down_ref, carry_ref):
    part_size = line_sources[0].shape[0]
    devices = part_size * len(line_sources)
    width = output_ref.shape[1]
    rows = output_ref.shape[0] // devices
    down_rows = down_ref.shape[0] // devices
    for index in range(devices):
        source = line_sources[index // part_size].at[index % part_size]
        target = pl.ds(pl.multiple_of(place_ref[0, index] * rows, rows), rows)
        output_ref[target, :] = source[:rows, :]
        for part in range(up_ref.shape[1] // width):
            up_ref[target, part * width : (part + 1) * width] = source[(part + 1) * rows : (part + 2) * rows, :]
        source = plane_sources[index // part_size].at[index % part_size]
        target = pl.ds(pl.multiple_of(place_ref[1, index] * down_rows, down_rows), down_rows)
        down_ref[target, :] = source[:down_rows, :]
        target = pl.ds(pl.multiple_of(place_ref[1, index] * rows, rows), rows)
        carry_ref[target, :] = source[down_rows:, :]


def spread_rows(place_ref, grad_ref, keep_ref, send_ref, start, rows):
    half = keep_ref.shape[0]
    for index in range(2 * half):
        source = pl.ds(pl.multiple_of(place_ref[index] * rows, rows), rows)
        target = (keep_ref if index < half else send_ref).at[index % half]
        target[start : start + rows, :] = grad_ref[source, :].astype(jnp.bfloat16)


def middle_kernel(
    place_ref,
    attended_ref,
    input_ref,
    normed_ref,
    cotangent_ref,
    gate_weight_ref,
    vectors_ref,
    *refs,
):
    late_refs, refs = refs[:8], refs[8:]
    output_ref, middle_grad_ref, attended_grad_ref, gate_pre_ref, block_ref, keep_ref, send_ref = refs[:7]
    output_weight, up_weight, down_weight, carry_weight, hidden, up_pre_grads = refs[7:13]
    update_grads, normed_second, carry_pre_grads, branch_grads, up_grad, down_grad, square_grads = refs[13:]
    unpack_late(
        place_ref,
        late_refs[:4],
        late_refs[4:],
        output_weight,
        up_weight,
        down_weight,
        carry_weight,
    )
    width = output_ref.shape[1]
    hidden_width = up_weight.shape[1]
    wide = hidden_width // width

    def vector(line):
        return vectors_ref[line : line + 1, :]

    up_bias = jnp.concatenate([vector(UP_B + part) for part in range(wide)], axis=1)

    def column_lines(values):
        return jnp.sum(values.astype(jnp.float32), axis=0, keepdims=True)

    def some_rows(step, totals):
        rows = pl.ds(pl.multiple_of(step * MIDDLE_ROWS, MIDDLE_ROWS), MIDDLE_ROWS)
        gate_open = jax.nn.sigmoid(matmul(normed_ref[rows, :], gate_weight_ref[...]) + vector(GATE_B))
        branch = matmul(attended_ref[rows, :], output_weight[...])
        middle = input_ref[rows, :].astype(jnp.float32) + gate_open * branch
        centered = middle - jnp.mean(middle, axis=-1, keepdims=True)
        scale = lax.rsqrt(jnp.mean(centered * centered, axis=-1, keepdims=True) + EPSILON)
        hat = centered * scale
        normed = (hat * vector(GAIN_TWO) + vector(SHIFT_TWO)).astype(jnp.bfloat16)
        up_pre = matmul(normed, up_weight[...]) + up_bias
        up_open = jax.nn.sigmoid(up_pre)
        hidden_rows = (up_pre * up_open).astype(jnp.bfloat16)
        update = matmul(hidden_rows, down_weight[...]) + vector(DOWN_B)
        carry_open = jax.nn.sigmoid(matmul(normed, carry_weight[...]) + vector(CARRY_B))
        output_ref[rows, :] = (middle + carry_open * update).astype(jnp.bfloat16)

        grad_out = cotangent_ref[rows, :].astype(jnp.float32)
        update_grad = (carry_open * grad_out).astype(jnp.bfloat16)
        carry_pre_grad = (grad_out * update * carry_open * (1.0 - carry_open)).astype(jnp.bfloat16)
        slope = up_open * (1.0 + up_pre * (1.0 - up_open))
        up_pre_grad = (against(update_grad, down_weight[...]) * slope).astype(jnp.bfloat16)
        norm_grad = against(up_pre_grad, up_weight[...]) + against(carry_pre_grad, carry_weight[...])
        pull = norm_grad * vector(GAIN_TWO)
        middle_grad = grad_out + scale * (
            pull - jnp.mean(pull, axis=-1, keepdims=True) - hat * jnp.mean(pull * hat, axis=-1, keepdims=True)
        )
        middle_grad_ref[rows, :] = middle_grad
        branch_grad = (gate_open * middle_grad).astype(jnp.bfloat16)
        gate_pre_grad = (middle_grad * branch * gate_open * (1.0 - gate_open)).astype(jnp.bfloat16)
        gate_pre_ref[rows, :] = gate_pre_grad
        attended_grad_ref[rows, :] = against(branch_grad, output_weight[...]).astype(jnp.bfloat16)

        hidden[rows, :] = hidden_rows
        up_pre_grads[rows, :] = up_pre_grad
        update_grads[rows, :] = update_grad
        normed_second[rows, :] = normed
        carry_pre_grads[rows, :] = carry_pre_grad
        branch_grads[rows, :] = branch_grad
        lines = (gate_pre_grad, update_grad, carry_pre_grad, norm_grad * hat, norm_grad, up_pre_grad)
        return tuple(total + column_lines(line) for total, line in zip(totals, lines))

    start = (jnp.zeros((1, width), jnp.float32),) * 5 + (jnp.zeros((1, hidden_width), jnp.float32),)
    totals = lax.fori_loop(0, output_ref.shape[0] // MIDDLE_ROWS, some_rows, start)
    line = lax.broadcasted_iota(jnp.int32, block_ref.shape, 0)
    block = jnp.zeros(block_ref.shape, jnp.float32)
    for place, total in zip((GATE_B, DOWN_B, CARRY_B, GAIN_TWO, SHIFT_TWO), totals):
        block = jnp.where(line == place, total, block)
    for part in range(wide):
        block = jnp.where(line == UP_B + part, totals[5][:, part * width : (part + 1) * width], block)
    block_ref[...] = block

    target_ref = place_ref.at[2]
    rows = width // (2 * keep_ref.shape[0])
    place = 0
    for part in range(wide):
        grad = up_grad.at[part]
        grad[...] = inner_rows(normed_second[...], up_pre_grads[:, part * width : (part + 1) * width])
        spread_rows(target_ref, grad, keep_ref, send_ref, place, rows)
        place += rows
    for part in range(wide):
        here = slice(part * width, (part + 1) * width)
        down_grad[here, :] = inner_rows(hidden[:, here], update_grads[...])
    spread_rows(target_ref, down_grad, keep_ref, send_ref, place, wide * rows)
    place += wide * rows
    pairs = ((normed_second, carry_pre_grads), (attended_ref, branch_grads), (normed_ref, gate_pre_ref))
    for index, (left_ref, right_ref) in enumerate(pairs):
        grad = square_grads.at[index]
        grad[...] = inner_rows(left_ref[...], right_ref[...])
        spread_rows(target_ref, grad, keep_ref, send_ref, place, rows)
        place += rows


def second_grads_kernel(
    place_ref,
    both_grads_ref,
    normed_ref,
    query_grad_ref,
    gate_pre_ref,
    lanes_ref,
    query_weight_ref,
    key_weight_ref,
    value_weight_ref,
    gate_weight_ref,
    vectors_ref,
    block_ref,
    keep_ref,
    send_ref,
    grads,
):
    width = keep_ref.shape[2]
    rows = width // (2 * keep_ref.shape[0])
    grads[0] = inner_rows(normed_ref[...], query_grad_ref[...])
    grads[1] = jnp.transpose(both_grads_ref[:width, :])
    grads[2] = jnp.transpose(both_grads_ref[width:, :])
    for index in range(3):
        spread_rows(place_ref, grads.at[index], keep_ref, send_ref, index * rows, rows)
    gate_grad = inner_rows(normed_ref[...], gate_pre_ref[...])

    def line_sums(ref):
        return jnp.sum(ref[...].astype(jnp.float32), axis=0, keepdims=True)

    def as_line(column):
        return jnp.transpose(jnp.broadcast_to(column, (width, BLK)))[:1, :]

    lines = (
        line_sums(query_grad_ref),
        jnp.sum(jnp.transpose(lanes_ref[:width, :]), axis=0, keepdims=True),
        jnp.sum(jnp.transpose(lanes_ref[width:, :]), axis=0, keepdims=True),
        line_sums(gate_pre_ref),
    )
    weighted = jnp.zeros((width, width), jnp.float32)
    shifted = jnp.zeros((width, width), jnp.float32)
    weight_refs = (query_weight_ref, key_weight_ref, value_weight_ref, gate_weight_ref)
    for weight_ref, line, grad in zip(weight_refs, lines, (grads[0], grads[1], grads[2], gate_grad)):
        weight = weight_ref[...].astype(jnp.float32)
        weighted += weight * grad
        shifted += weight * line
    shift_line = as_line(jnp.sum(shifted, axis=1, keepdims=True))
    gain_line = (
        as_line(jnp.sum(weighted, axis=1, keepdims=True)) - vectors_ref[SHIFT_ONE : SHIFT_ONE + 1, :] * shift_line
    ) / vectors_ref[GAIN_ONE : GAIN_ONE + 1, :]
    place = lax.broadcasted_iota(jnp.int32, block_ref.shape, 0)
    block = jnp.where(place == GAIN_ONE, gain_line, block_ref[...])
    block = jnp.where(place == SHIFT_ONE, shift_line, block).astype(jnp.bfloat16)
    for index in range(keep_ref.shape[0]):
        keep_ref[index, 3 * rows :, :] = block
        send_ref[index, 3 * rows :, :] = block


def input_grad_kernel(input_ref, local_ref, middle_grad_ref, vectors_ref, *refs):
    shared_refs, output_ref = refs[:-1], refs[-1]
    blocks = [sum(ref[index].astype(jnp.float32) for ref in shared_refs) for index in range(shared_refs[0].shape[0])]
    shared = jnp.concatenate([jnp.transpose(block) for block in blocks])
    values = input_ref[...].astype(jnp.float32)
    centered = values - jnp.mean(values, axis=-1, keepdims=True)
    scale = lax.rsqrt(jnp.mean(centered * centered, axis=-1, keepdims=True) + EPSILON)
    hat = centered * scale
    pull = (local_ref[...] + shared) * vectors_ref[GAIN_ONE : GAIN_ONE + 1, :]
    output_ref[...] = middle_grad_ref[...] + scale * (
        pull - jnp.mean(pull, axis=-1, keepdims=True) - hat * jnp.mean(pull * hat, axis=-1, keepdims=True)
    )


def local_call(kernel, cost, outs, smem, args, scratch=()):
    return pl.pallas_call(
        kernel,
        cost_estimate=about(cost),
        out_shape=outs,
        in_specs=[in_smem()] + [in_vmem()] * len(args),
        out_specs=jax.tree.map(lambda out: in_vmem(), outs),
        scratch_shapes=list(scratch),
        compiler_params=pltpu.CompilerParams(vmem_limit_bytes=VMEM_BYTES),
    )(smem, *args)


def joined(pieces, axis):
    return pieces[0] if len(pieces) == 1 else jnp.concatenate(pieces, axis=axis)


def shards(
    inputs,
    cotangent,
    block_segment,
    segment_parent,
    query_weight,
    key_weight,
    value_weight,
    output_weight,
    gate_weight,
    gate_bias,
    up_weight,
    up_bias,
    down_weight,
    down_bias,
    carry_weight,
    carry_bias,
    first_gain,
    first_shift,
    second_gain,
    second_shift,
):
    width = inputs.shape[1]
    devices = lax.axis_size(BOTH)
    block_count = inputs.shape[0] // BLK
    group_blocks = block_segment.shape[0]

    axis_z, axis_x, axis_y, axis_core = axes()
    rows_each = query_weight.shape[0]
    sizes = (axis_z.size, axis_x.size, axis_y.size, axis_core.size)
    direct = sizes == (4, 2, 2, 2) and rows_each % 16 == 0
    places = relative_devices()
    targets = scatter_devices()
    device = lax.axis_index(BOTH)
    vectors = (gate_bias, down_bias, carry_bias, first_gain, first_shift, second_gain, second_shift, up_bias)
    early_set = (query_weight, key_weight, value_weight, gate_weight)
    late_set = (output_weight, up_weight, down_weight, carry_weight)
    low = jnp.bfloat16

    def struct(*shape, dtype=low):
        return jax.ShapeDtypeStruct(shape, dtype)

    def take(source, start, piece):
        rows = piece.shape[0]
        parts = piece.shape[1] // width
        blocks = [
            source[:, start + part * rows : start + (part + 1) * rows].reshape(devices * rows, width)
            for part in range(parts)
        ]
        return joined(blocks, 1), start + parts * rows

    def flat_rows(pieces):
        return [piece[:, start : start + width] for piece in pieces for start in range(0, piece.shape[1], width)]

    if direct:
        early_count = 4 * rows_each + VECTOR_ROWS
        late_count = sum(piece.shape[0] * piece.shape[1] // width for piece in late_set)
        early, late = local_call(
            functools.partial(pack_kernel, devices),
            0.1,
            (struct(early_count, width), struct(late_count, width)),
            device.reshape(1),
            early_set + late_set + tuple(vector.reshape(1, -1) for vector in vectors),
        )
        late_line = [late]
        late_line.append(axis_z.rotate(late, 1))
        early_line = [axis_z.rotate(early, back) for back in range(1, 4)]
        x_zero = axis_x.rotate(inputs, 1)
        z_one = axis_z.rotate(inputs, 1)
        late_line[1], early_line, x_zero, z_one = lax.optimization_barrier((late_line[1], early_line, x_zero, z_one))
        z_two = axis_z.rotate(z_one, 1)
        x_one = axis_x.rotate(z_one, 1)
        early_line = jnp.stack([early] + list(early_line))
        early_other = axis_x.rotate(early_line, 1)
        late_line.append(axis_z.rotate(late_line[1], 1))
        early_other, z_two, x_one, late_line[2] = lax.optimization_barrier((early_other, z_two, x_one, late_line[2]))
        z_three = axis_z.rotate(z_two, 1)
        x_two = axis_x.rotate(z_two, 1)
        early_plane = jnp.stack([early_line, early_other])
        early_other = axis_y.rotate(early_plane, 1)
        late_line.append(axis_z.rotate(late_line[2], 1))
        early_other, z_three, x_two, late_line[3] = lax.optimization_barrier(
            (early_other, z_three, x_two, late_line[3])
        )
        x_three = axis_x.rotate(z_three, 1)
        early_all = jnp.stack([early_plane, early_other]).reshape(devices // 2, early_count, width)
        early_other = axis_core.rotate(early_all, 1)
        late_half = late_count // 2
        late_x = jnp.stack([rows[:late_half] for rows in late_line])
        late_y = jnp.stack([rows[late_half:] for rows in late_line])
        late_x_other = axis_x.rotate(late_x, 1)
        late_y_other = axis_y.rotate(late_y, 1)
        input_pieces = [[inputs, x_zero], [z_one, x_one], [z_two, x_two], [z_three, x_three]]
        square = struct(width, width)
        full_query, full_key, full_value, full_gate, vector_rows = local_call(
            unpack_kernel,
            3,
            (square, square, square, square, struct(VECTOR_ROWS, width, dtype=jnp.float32)),
            places,
            (early_all, early_other),
        )
    else:
        early_rows = lax.all_gather(jnp.concatenate(early_set), BOTH)
        late_rows = lax.all_gather(jnp.concatenate(flat_rows(late_set)), BOTH)
        place = 0
        full_query, place = take(early_rows, place, query_weight)
        full_key, place = take(early_rows, place, key_weight)
        full_value, place = take(early_rows, place, value_weight)
        full_gate, place = take(early_rows, place, gate_weight)
        place = 0
        full_output, place = take(late_rows, place, output_weight)
        full_up, place = take(late_rows, place, up_weight)
        full_down, place = take(late_rows, place, down_weight)
        full_carry, place = take(late_rows, place, carry_weight)
        lines = [lax.all_gather(vector, BOTH, tiled=True).reshape(-1, width) for vector in vectors]
        lines = jnp.concatenate(lines).astype(jnp.float32)
        vector_rows = jnp.pad(lines, ((0, VECTOR_ROWS - lines.shape[0]), (0, 0)))
        input_pieces = []
        along_z = inputs
        for step_z in range(axis_z.size):
            along_x = along_z
            row = []
            for step_x in range(axis_x.size):
                row.append(along_x)
                along_x = axis_x.rotate(along_x, 1) if step_x + 1 < axis_x.size else None
            input_pieces.append(row)
            along_z = axis_z.rotate(along_z, 1) if step_z + 1 < axis_z.size else None

    carried = None
    for step, row in enumerate(input_pieces):
        if direct and step == 3:
            x_three, late_x_other, late_y_other, carried = lax.optimization_barrier(
                (row[1], late_x_other, late_y_other, carried)
            )
            row = [row[0], x_three]
            late_x = jnp.stack([late_x, late_x_other])
            late_y = jnp.stack([late_y, late_y_other])
            late_x_other = axis_y.rotate(late_x, 1)
            late_y_other = axis_x.rotate(late_y, 1)
        asked = full_query if step == 0 else None
        done = project(row, vector_rows, full_key, full_value, group_blocks * BLK, step, carried, asked)
        carried = done[:3]
        if step == 0:
            normed_low, query_low = done[3:]
    normed_group, key_group, value_group = carried

    gate_b, down_b, carry_b, gain_one, shift_one, gain_two, shift_two = [vector_rows[line] for line in range(UP_B)]
    up_b = vector_rows[UP_B : UP_B + up_weight.shape[1] // width].reshape(-1)

    own_start = lax.axis_index("seq") * block_count
    own_segments = lax.dynamic_slice_in_dim(block_segment, own_start, block_count)
    ancestor_slot, usable = ancestor_slots(block_segment, segment_parent, own_segments)
    owner = ancestor_slot // block_count
    away_z = (axis_z.position() - owner // axis_x.size) % axis_z.size
    away_x = (axis_x.position() - owner % axis_x.size) % axis_x.size
    relative_slot = (away_z * axis_x.size + away_x) * block_count + ancestor_slot % block_count
    tables = used_places(relative_slot, usable, group_blocks)
    slots = jnp.concatenate(
        [relative_slot, jnp.sum(usable, axis=-1, keepdims=True, dtype=jnp.int32)], axis=-1
    )

    values_in = inputs.astype(jnp.float32)
    attended_low, logsum = attend(slots, query_low, key_group, value_group)

    if direct:
        attended_low, late_x_other, late_y_other = lax.optimization_barrier((attended_low, late_x_other, late_y_other))
        late_parts = []
        for mine in ((late_x, late_x_other), (late_y, late_y_other)):
            for piece in list(mine) + [axis_core.rotate(part, 1) for part in mine]:
                late_parts.append(piece.reshape(devices // 4, late_half, width))
        other_places = jnp.transpose(places.reshape(2, 2, 2, 4), (0, 2, 1, 3)).reshape(-1)
        rows = inputs.shape[0]
        first_rows = late_count + rows_each
        hidden_width = up_weight.shape[1]
        half = struct(devices // 2, first_rows, width)
        tall, short = pltpu.VMEM((rows, hidden_width), low), pltpu.VMEM((rows, width), low)
        output, middle_grad, attended_grad, gate_pre_grad, block, first_keep, first_send = local_call(
            middle_kernel,
            28,
            (
                struct(rows, width),
                struct(rows, width, dtype=jnp.float32),
                struct(rows, width),
                struct(rows, width),
                struct(VECTOR_ROWS, width, dtype=jnp.float32),
                half,
                half,
            ),
            jnp.stack([places, other_places, targets]),
            (
                attended_low,
                inputs,
                normed_low,
                cotangent,
                full_gate,
                vector_rows,
            )
            + tuple(late_parts),
            (
                pltpu.VMEM((width, width), low),
                pltpu.VMEM((width, hidden_width), low),
                pltpu.VMEM((hidden_width, width), low),
                pltpu.VMEM((width, width), low),
                tall,
                tall,
                short,
                short,
                short,
                short,
                pltpu.VMEM((hidden_width // width, width, width), jnp.float32),
                pltpu.VMEM((hidden_width, width), jnp.float32),
                pltpu.VMEM((3, width, width), jnp.float32),
            ),
        )
        near = (2, 4, 2, first_rows, width)
        first_entry = pair_scatter(first_keep.reshape(near), first_send.reshape(near), axis_core)
        first_keep, first_send = first_entry(0), first_entry(1)
        attended_grad, first_keep, first_send = lax.optimization_barrier((attended_grad, first_keep, first_send))
        first_arrived = axis_y.rotate(first_send, -1)
    else:
        gate_open = jax.nn.sigmoid(matmul(normed_low, full_gate) + gate_b)
        branch = matmul(attended_low, full_output)
        middle = values_in + gate_open * branch
        normed_second = normalize(middle, gain_two, shift_two).astype(jnp.bfloat16)
        up_pre = matmul(normed_second, full_up) + up_b
        up_sigmoid = jax.nn.sigmoid(up_pre)
        hidden_low = (up_pre * up_sigmoid).astype(jnp.bfloat16)
        update = matmul(hidden_low, full_down) + down_b
        carry_open = jax.nn.sigmoid(matmul(normed_second, full_carry) + carry_b)
        output = (middle + carry_open * update).astype(jnp.bfloat16)

        grad_out = cotangent.astype(jnp.float32)
        update_grad = (carry_open * grad_out).astype(jnp.bfloat16)
        carry_pre_grad = (grad_out * update * carry_open * (1.0 - carry_open)).astype(jnp.bfloat16)
        grad_down_bias = column_sums(update_grad)
        grad_carry_bias = column_sums(carry_pre_grad)
        silu_slope = up_sigmoid * (1.0 + up_pre * (1.0 - up_sigmoid))
        up_pre_grad = (against(update_grad, full_down) * silu_slope).astype(jnp.bfloat16)
        grad_up_bias = column_sums(up_pre_grad)
        second_norm_grad = against(up_pre_grad, full_up) + against(carry_pre_grad, full_carry)
        second_pull = jax.vjp(normalize, middle, gain_two, shift_two)[1]
        middle_part, grad_second_gain, grad_second_shift = second_pull(second_norm_grad)
        middle_grad = grad_out + middle_part

        branch_grad = (gate_open * middle_grad).astype(jnp.bfloat16)
        gate_pre_grad = (middle_grad * branch * gate_open * (1.0 - gate_open)).astype(jnp.bfloat16)
        grad_gate_bias = column_sums(gate_pre_grad)
        attended_grad = against(branch_grad, full_output).astype(jnp.bfloat16)
        zero_line = jnp.zeros((width,), jnp.float32)
        local_lines = (
            grad_gate_bias,
            grad_down_bias,
            grad_carry_bias,
            zero_line,
            zero_line,
            grad_second_gain,
            grad_second_shift,
            grad_up_bias,
        )
        block = jnp.concatenate([line.reshape(-1, width) for line in local_lines])
        block = jnp.pad(block, ((0, VECTOR_ROWS - block.shape[0]), (0, 0)))
    backward = attend_backward(
        (slots,) + tables,
        query_low,
        key_group,
        value_group,
        logsum,
        attended_low,
        attended_grad,
        normed_group,
        jnp.concatenate([full_key, full_value], axis=1),
    )
    if direct:
        backward, first_arrived = lax.optimization_barrier((backward, first_arrived))

        def first_y(back):
            return add_low(first_arrived[back], first_keep[back])

        first_z = axis_z.rotate(first_y(3), -1)
    query_rows_grad, both_grads, lanes, shared_rows = backward

    shared_parts = [
        shared_rows[start : start + block_count] for start in range(0, group_blocks, block_count)
    ]

    if direct:
        second_rows = 3 * rows_each + VECTOR_ROWS
        half = struct(devices // 2, second_rows, width)
        second_keep, second_send = local_call(
            second_grads_kernel,
            0.1,
            (half, half),
            places,
            (
                both_grads,
                normed_low,
                query_rows_grad,
                gate_pre_grad,
                lanes,
                full_query,
                full_key,
                full_value,
                full_gate,
                vector_rows,
                block,
            ),
            (pltpu.VMEM((3, width, width), jnp.float32),),
        )
        near = (2, 2, 4, second_rows, width)
        second_entry = pair_scatter(second_keep.reshape(near), second_send.reshape(near), axis_core)
        barrier = lax.optimization_barrier
        first_z = axis_z.rotate(add_low(first_z, first_y(2)), -1)
        x_three = axis_x.rotate(shared_parts[7], -1)
        second_keep, second_send = second_entry(0), second_entry(1)
        x_three, first_z, second_keep, second_send = barrier((x_three, first_z, second_keep, second_send))

        second_arrived = axis_y.rotate(second_send, -1)
        x_two = axis_x.rotate(tied(shared_parts[5], x_three), -1)
        z_three = axis_z.rotate(add_low(x_three, shared_parts[6]), -1)
        first_z = axis_z.rotate(add_low(first_z, first_y(1)), -1)
        x_two, z_three, first_z, second_arrived = barrier((x_two, z_three, first_z, second_arrived))

        second_y = add_low(second_arrived, second_keep)
        second_x = axis_x.rotate(second_y[1], -1)
        x_one = axis_x.rotate(tied(shared_parts[3], x_two), -1)
        z_two = axis_z.rotate(add_three(x_two, shared_parts[4], z_three), -1)
        x_one, z_two, second_x = barrier((x_one, z_two, second_x))

        first_half = add_low(first_z, first_y(0))
        first_x = axis_x.rotate(tied(first_half[1], x_one), -1)
        second_half = add_low(second_x, second_y[0])
        second_z = [axis_z.rotate(second_half[back], -back) for back in range(1, 4)]
        x_zero = axis_x.rotate(tied(shared_parts[1], x_one), -1)
        z_one = axis_z.rotate(add_three(x_one, shared_parts[2], z_two), -1)
        shared = (x_zero, z_one, shared_parts[0])
        first_sum = first_x.astype(jnp.float32) + first_half[0].astype(jnp.float32)
        second_sum = sum(piece.astype(jnp.float32) for piece in [second_half[0]] + second_z)
        weight_sum = jnp.concatenate([first_sum, second_sum])
    else:
        grad_key = jnp.transpose(both_grads[:width])
        grad_value = jnp.transpose(both_grads[width:])
        grad_query = inner_rows(normed_low, query_rows_grad)
        grad_gate = inner_rows(normed_low, gate_pre_grad)
        both_sums = jnp.sum(lanes, axis=1)
        weights = [weight.astype(jnp.float32) for weight in (full_query, full_key, full_value, full_gate)]
        line_sums = (column_sums(query_rows_grad), both_sums[:width], both_sums[width:], grad_gate_bias)
        shift_line = sum(jnp.sum(weight * line, axis=1) for weight, line in zip(weights, line_sums))
        weighted = sum(
            jnp.sum(weight * grad, axis=1)
            for weight, grad in zip(weights, (grad_query, grad_key, grad_value, grad_gate))
        )
        block = block.at[GAIN_ONE].set((weighted - shift_one * shift_line) / gain_one).at[SHIFT_ONE].set(shift_line)
        grads = (
            (inner_rows(normed_second, up_pre_grad), up_weight),
            (inner_rows(hidden_low, update_grad), down_weight),
            (inner_rows(normed_second, carry_pre_grad), carry_weight),
            (inner_rows(attended_low, branch_grad), output_weight),
            (grad_gate, gate_weight),
            (grad_query, query_weight),
            (grad_key, key_weight),
            (grad_value, value_weight),
        )
        pack = [
            cut.astype(low).reshape(devices, piece.shape[0], width)
            for grad, piece in grads
            for cut in flat_rows((grad,))
        ]
        pack.append(jnp.broadcast_to(block.astype(low), (devices, VECTOR_ROWS, width)))
        pack = jnp.concatenate(pack, axis=1)
        pack = jnp.pad(pack, ((0, 0), (0, -pack.shape[1] % 16), (0, 0)))
        weight_sum = lax.psum_scatter(pack, BOTH, scatter_dimension=0, tiled=True)[0].astype(jnp.float32)

        def over_x(step_z):
            return ring_scatter(lambda step_x: shared_parts[step_z * axis_x.size + step_x], axis_x)

        shared = (ring_scatter(over_x, axis_z),)

    def own(start, piece):
        rows = piece.shape[0]
        parts = piece.shape[1] // width
        blocks = [weight_sum[start + part * rows : start + (part + 1) * rows] for part in range(parts)]
        return joined(blocks, 1), start + parts * rows

    local_grad = against(query_rows_grad, full_query) + against(gate_pre_grad, full_gate)
    rows = inputs.shape[0]
    input_grad = pl.pallas_call(
        input_grad_kernel,
        cost_estimate=about(3),
        out_shape=struct(rows, width, dtype=jnp.float32),
        compiler_params=pltpu.CompilerParams(vmem_limit_bytes=VMEM_BYTES),
    )(inputs, local_grad, middle_grad, vector_rows, *shared)

    place = 0
    own_up, place = own(place, up_weight)
    own_down, place = own(place, down_weight)
    own_carry, place = own(place, carry_weight)
    own_output, place = own(place, output_weight)
    own_gate, place = own(place, gate_weight)
    own_query, place = own(place, query_weight)
    own_key, place = own(place, key_weight)
    own_value, place = own(place, value_weight)
    vector_out = []
    for index, vector in enumerate(vectors):
        count = vector.shape[0]
        lines = weight_sum[place + index : place + index + count * devices // width].reshape(-1)
        vector_out.append(lax.dynamic_slice_in_dim(lines, device * count, count))
    gate_bg, down_bg, carry_bg, gain_one_g, shift_one_g, gain_two_g, shift_two_g, up_bg = vector_out
    return (
        output,
        input_grad,
        own_query,
        own_key,
        own_value,
        own_output,
        own_gate,
        gate_bg,
        own_up,
        up_bg,
        own_down,
        down_bg,
        own_carry,
        carry_bg,
        gain_one_g,
        shift_one_g,
        gain_two_g,
        shift_two_g,
    )


def solution(mesh):
    rows = P(BOTH, None)
    line = P(BOTH)
    matrix_or_line = (rows,) * 5 + (line, rows, line, rows, line, rows) + (line,) * 5
    return jax.shard_map(
        shards,
        mesh=mesh,
        in_specs=(rows, rows, P("dp"), P("dp")) + matrix_or_line,
        out_specs=(rows, rows) + matrix_or_line,
        check_vma=False,
    )
```

profile of v0, /device:TPU:28, one launch (start us, length us, event | category | flops | bytes accessed | tf_op | source)
XLA Modules:
  0.0 317.1 jit_solution(10256988508878713410)
XLA Ops:
  0.7 1.9 shard_map.331
  2.8 1.7 collective-permute-start.2
  4.4 1.5 collective-permute-start.4
  5.9 2.5 collective-permute-start.5
  19.1 1.9 collective-permute-start.3
  21.7 7.1 %collective-permute-done.3 = bf16[80,512]{1,0:T(8,128)(2,1)S(1)} collective-permute-done((bf16[80,512]{1,0:T(8,128)(2,1)}, bf16[80,512]{1,0:T(8,128)(2,1)S(1)}, u32[]{:S(2)}, u32[]{:S(2)}) %collective-permute-start.3) | collective-permute-done | bytes 81952 | tf_op jit(solution)/shard_map/ppermute | solution.py:429
  29.7 3.0 collective-permute-start.7
  32.7 1.5 collective-permute-start.8
  37.7 12.7 %collective-permute-done.9 = bf16[160,512]{1,0:T(8,128)(2,1)S(1)} collective-permute-done((bf16[160,512]{1,0:T(8,128)(2,1)S(1)}, bf16[160,512]{1,0:T(8,128)(2,1)S(1)}, u32[]{:S(2)}, u32[]{:S(2)}) %collective-permute-start.9) | collective-permute-done | bytes 163872 | tf_op jit(solution)/shard_map/ppermute | solution.py:429
  50.4 5.7 %collective-permute-done.6 = bf16[4,80,512]{2,1,0:T(8,128)(2,1)S(1)} collective-permute-done((bf16[4,80,512]{2,1,0:T(8,128)(2,1)S(1)}, bf16[4,80,512]{2,1,0:T(8,128)(2,1)S(1)}, u32[]{:S(2)}, u32[]{:S(2)}) %collective-permute-start.6) | collective-permute-done | bytes 327712 | tf_op jit(solution)/shard_map/ppermute | solution.py:429
  56.7 1.5 collective-permute-start.12
  59.6 15.7 %collective-permute-done.13 = bf16[160,512]{1,0:T(8,128)(2,1)} collective-permute-done((bf16[160,512]{1,0:T(8,128)(2,1)S(1)}, bf16[160,512]{1,0:T(8,128)(2,1)}, u32[]{:S(2)}, u32[]{:S(2)}) %collective-permute-start.13) | collective-permute-done | bytes 163872 | tf_op jit(solution)/shard_map/ppermute | solution.py:429
  79.4 1.5 collective-permute-start.16
  82.7 3.2 shard_map.332
  85.9 5.6 %shard_map.333 = (bf16[5120,512]{1,0:T(8,128)(2,1)}, bf16[5120,512]{1,0:T(8,128)(2,1)}, bf16[5120,512]{1,0:T(8,128)(2,1)}, bf16[640,512]{1,0:T(8,128)(2,1)}, bf16[640,512]{1,0:T(8,128)(2,1)}) custom-call(bf16[640,512]{1,0:T(8,128)(2,1)} %input_ref.3, bf16[640,512]{1,0:T(8,128)(2,1)} %copy-done.22, f32[16,512]{1,0:T(8,128)} %get-tuple-element.112.refs_2_.vectors_ref, ...), custom_call_target="tpu_custom_call" | custom-call | flops 4000000000 | bytes 4000000 | tf_op jit(solution)/shard_map/pallas_call | solution.py:402
  91.4 4.9 %shard_map.334 = (bf16[5120,512]{1,0:T(8,128)(2,1)}, bf16[5120,512]{1,0:T(8,128)(2,1)}, bf16[5120,512]{1,0:T(8,128)(2,1)}) custom-call(bf16[640,512]{1,0:T(8,128)(2,1)} %copy-done.8, bf16[640,512]{1,0:T(8,128)(2,1)} %copy-done.10, f32[16,512]{1,0:T(8,128)} %get-tuple-element.112.refs_2_.vectors_ref, ...), custom_call_target="tpu_custom_call", output_to_operand_aliasing={{0}: (5, {}), {1}: (6, {}), {2}: (7, {})} | custom-call | flops 4000000000 | bytes 4000000 | tf_op jit(solution)/shard_map/pallas_call | solution.py:402
  96.3 4.9 %shard_map.335 = (bf16[5120,512]{1,0:T(8,128)(2,1)}, bf16[5120,512]{1,0:T(8,128)(2,1)}, bf16[5120,512]{1,0:T(8,128)(2,1)}) custom-call(bf16[640,512]{1,0:T(8,128)(2,1)} %copy-done.9, bf16[640,512]{1,0:T(8,128)(2,1)} %copy-done.13, f32[16,512]{1,0:T(8,128)} %get-tuple-element.112.refs_2_.vectors_ref, ...), custom_call_target="tpu_custom_call", output_to_operand_aliasing={{0}: (5, {}), {1}: (6, {}), {2}: (7, {})} | custom-call | flops 4000000000 | bytes 4000000 | tf_op jit(solution)/shard_map/pallas_call | solution.py:402
  101.2 2.4 collective-permute-done.15.refs_1_
  105.3 1.6 collective-permute-start.19
  107.1 4.8 %shard_map.336 = (bf16[5120,512]{1,0:T(8,128)(2,1)}, bf16[5120,512]{1,0:T(8,128)(2,1)}, bf16[5120,512]{1,0:T(8,128)(2,1)}) custom-call(bf16[640,512]{1,0:T(8,128)(2,1)} %copy-done.11, bf16[640,512]{1,0:T(8,128)(2,1)} %copy-done.14, f32[16,512]{1,0:T(8,128)} %get-tuple-element.112.refs_2_.vectors_ref, ...), custom_call_target="tpu_custom_call", output_to_operand_aliasing={{0}: (5, {}), {1}: (6, {}), {2}: (7, {})} | custom-call | flops 4000000000 | bytes 4000000 | tf_op jit(solution)/shard_map/pallas_call | solution.py:402
  111.9 17.8 %shard_map.337 = (bf16[640,512]{1,0:T(8,128)(2,1)}, f32[640,128]{1,0:T(8,128)}) custom-call(s32[5,11]{1,0:T(8,128)} %pad_add_fusion.slots_ref, bf16[640,512]{1,0:T(8,128)(2,1)} %get-tuple-element.116.query_ref, bf16[5120,512]{1,0:T(8,128)(2,1)} %get-tuple-element.134.key_source, bf16[5120,512]{1,0:T(8,128)(2,1)} %get-tuple-element.135.value_source), custom_call_target="tpu_custom_call" | custom-call | flops 17999998976 | bytes 18000000 | tf_op jit(solution)/shard_map/pallas_call | solution.py:311
  133.2 21.6 %shard_map.338 = (bf16[640,512]{1,0:T(8,128)(2,1)}, f32[640,512]{1,0:T(8,128)}, bf16[640,512]{1,0:T(8,128)(2,1)}, bf16[640,512]{1,0:T(8,128)(2,1)}, f32[16,512]{...) custom-call(s32[3,32]{1,0:T(4,128)} %pad_add_fusion.1.place_ref, ...), custom_call_target="tpu_custom_call" | custom-call | flops 28000000000 | bytes 28000000 | tf_op jit(solution)/shard_map/pallas_call | solution.py:735
  156.1 1.2 add_bitcast_fusion.used_ref
  158.8 1.1 pad_maximum_fusion.1.weight_ref
  159.9 2.0 fusion.70
  161.9 2.1 fusion
  164.0 2.2 collective-permute-start.25
  166.2 33.6 %shard_map.339 = (bf16[640,512]{1,0:T(8,128)(2,1)}, f32[1024,512]{1,0:T(8,128)}, f32[1024,128]{1,0:T(8,128)}, bf16[40,512,128]{2,1,0:T(8,128)(2,1)}) custom-call(s32[5,11]{1,0:T(8,128)} %pad_add_fusion.slots_ref, s32[5,10]{1,0:T(8,128)} %select_reduce_fusion.compact_ref, s32[1,29]{1,0:T(1,128)} %add_bitcast_fusion.used_ref, ...), custom_call_target="tpu_custom_call" | custom-call | flops 32000000000 | bytes 32000000 | tf_op jit(solution)/shard_map/pallas_call | solution.py:329
  199.9 6.4 %shard_map.340 = (bf16[16,64,512]{2,1,0:T(8,128)(2,1)}, bf16[16,64,512]{2,1,0:T(8,128)(2,1)}) custom-call(s32[32]{0:T(128)} %fusion.32.place_ref, f32[1024,512]{1,0:T(8,128)} %get-tuple-element.162.both_grads_ref, bf16[640,512]{1,0:T(8,128)(2,1)} %get-tuple-element.140.normed_ref, bf16[640,512]{1,0:T(8,128)(2,1)} %get-tuple-element.156.query_grad_ref, ...), custom_call_target="tpu_custom_call" | custom-call | flops 100000000 | bytes 100000 | tf_op jit(solution)/shard_map/pallas_call | solution.py:735
  206.3 1.2 collective-permute-start.29
  208.4 3.1 fusion.69
  211.4 8.6 %collective-permute-done.27 = bf16[2,176,512]{2,1,0:T(8,128)(2,1)} collective-permute-done((bf16[2,176,512]{2,1,0:T(8,128)(2,1)S(1)}, bf16[2,176,512]{2,1,0:T(8,128)(2,1)}, u32[]{:S(2)}, u32[]{:S(2)}) %collective-permute-start.27) | collective-permute-done | bytes 360480 | tf_op jit(solution)/shard_map/ppermute | solution.py:429
  221.3 1.5 fusion.2
  222.8 5.0 %collective-permute-done.26 = bf16[5,512,128]{2,1,0:T(8,128)(2,1)S(1)} collective-permute-done((bf16[5,512,128]{2,1,0:T(8,128)(2,1)S(1)}, bf16[5,512,128]{2,1,0:T(8,128)(2,1)S(1)}, u32[]{:S(2)}, u32[]{:S(2)}) %collective-permute-start.26) | collective-permute-done | bytes 655392 | tf_op jit(solution)/shard_map/ppermute | solution.py:429
  227.8 4.7 %collective-permute-done.28 = bf16[2,176,512]{2,1,0:T(8,128)(2,1)S(1)} collective-permute-done((bf16[2,176,512]{2,1,0:T(8,128)(2,1)S(1)}, bf16[2,176,512]{2,1,0:T(8,128)(2,1)S(1)}, u32[]{:S(2)}, u32[]{:S(2)}) %collective-permute-start.28) | collective-permute-done | bytes 360480 | tf_op jit(solution)/shard_map/ppermute | solution.py:429
  232.5 1.4 add_convert_fusion.2
  236.1 1.6 convolution_add_fusion.local_ref
  237.7 20.5 %collective-permute-done.32 = bf16[2,176,512]{2,1,0:T(8,128)(2,1)S(1)} collective-permute-done((bf16[2,176,512]{2,1,0:T(8,128)(2,1)S(1)}, bf16[2,176,512]{2,1,0:T(8,128)(2,1)S(1)}, u32[]{:S(2)}, u32[]{:S(2)}) %collective-permute-start.32) | collective-permute-done | bytes 360480 | tf_op jit(solution)/shard_map/ppermute | solution.py:429
  258.3 1.3 add_convert_fusion.1
  259.7 1.4 collective-permute-start.34
  262.2 17.7 %collective-permute-done.36 = bf16[4,64,512]{2,1,0:T(8,128)(2,1)S(1)} collective-permute-done((bf16[4,64,512]{2,1,0:T(8,128)(2,1)S(1)}, bf16[4,64,512]{2,1,0:T(8,128)(2,1)S(1)}, u32[]{:S(2)}, u32[]{:S(2)}) %collective-permute-start.36) | collective-permute-done | bytes 262176 | tf_op jit(solution)/shard_map/ppermute | solution.py:429
  279.9 1.7 collective-permute-start.42
  281.8 4.3 %collective-permute-start.40 = (bf16[64,512]{1,0:T(8,128)(2,1)S(1)}, bf16[64,512]{1,0:T(8,128)(2,1)S(1)}, u32[]{:S(2)}, u32[]{:S(2)}) collective-permute-start(bf16[64,512]{1,0:T(8,128)(2,1)S(1)} %get-tuple-element.221), channel_id=1, source_target_pairs={{0,4},{1,5},{2,6},{3,7},{4,0},{5,1},{6,2},{7,3},{8,12},{9,13},{10,... | collective-permute-start | bytes 196616 | tf_op jit(solution)/shard_map/ppermute | solution.py:429
  286.1 1.3 add_convert_fusion
  287.4 2.1 collective-permute-start.38
  289.8 1.6 collective-permute-done.40
  291.3 12.5 %collective-permute-done.41 = bf16[64,512]{1,0:T(8,128)(2,1)S(1)} collective-permute-done((bf16[64,512]{1,0:T(8,128)(2,1)S(1)}, bf16[64,512]{1,0:T(8,128)(2,1)S(1)}, u32[]{:S(2)}, u32[]{:S(2)}) %collective-permute-start.41) | collective-permute-done | bytes 65568 | tf_op jit(solution)/shard_map/ppermute | solution.py:429
  312.3 4.7 %shard_map.341 = f32[640,512]{1,0:T(8,128)} custom-call(bf16[640,512]{1,0:T(8,128)(2,1)} %input_ref.3, f32[640,512]{1,0:T(8,128)} %convolution_add_fusion.local_ref, f32[640,512]{1,0:T(8,128)} %get-tuple-element.158.middle_grad_ref, f32[16,512]{1,0:T(8,128)} %get-tuple-element.112.refs_2_.vectors_ref, bf16[5,512,128]{2,1,0:T(8,128)(2,1)} %copy-done.25, ...), custom_call_target="tpu_custom_call" | custom-call | flops 3000000000 | bytes 3000000 | tf_op jit(solution)/shard_map/pallas_call | solution.py:1135
  (230 shorter events, 46.2 us)
Async XLA Ops:
  0.7 35.7 %copy-start.21 = (s32[40]{0:T(128)S(1)}, s32[40]{0:T(128)}, u32[]{:S(2)}) copy-start(s32[40]{0:T(128)} %param.22) | copy-start | bytes 484
  2.5 16.6 %collective-permute-start.1 = (bf16[80,512]{1,0:T(8,128)(2,1)}, bf16[80,512]{1,0:T(8,128)(2,1)S(1)}, u32[]{:S(2)}, u32[]{:S(2)}) collective-permute-start(bf16[80,512]{1,0:T(8,128)(2,1)} %get-tuple-element.101), channel_id=1, source_target_pairs={{0,2},{1,3},{2,4},{3,5},{4,6},{5,7},{6,0},{7,1},{8,10},{9,11},{10,... | collective-permute-start | bytes 245768 | tf_op jit(solution)/shard_map/ppermute | solution.py:429
  2.8 19.0 %collective-permute-start.2 = (bf16[80,512]{1,0:T(8,128)(2,1)}, bf16[80,512]{1,0:T(8,128)(2,1)S(1)}, u32[]{:S(2)}, u32[]{:S(2)}) collective-permute-start(bf16[80,512]{1,0:T(8,128)(2,1)} %get-tuple-element.101), channel_id=1, source_target_pairs={{0,4},{1,5},{2,6},{3,7},{4,0},{5,1},{6,2},{7,3},{8,12},{9,13},{10,... | collective-permute-start | bytes 245768 | tf_op jit(solution)/shard_map/ppermute | solution.py:429
  4.4 24.4 %collective-permute-start.4 = (bf16[640,512]{1,0:T(8,128)(2,1)}, bf16[640,512]{1,0:T(8,128)(2,1)S(1)}, u32[]{:S(2)}, u32[]{:S(2)}) collective-permute-start(bf16[640,512]{1,0:T(8,128)(2,1)} %input_ref.3), channel_id=1, source_target_pairs={{0,1},{1,0},{2,3},{3,2},{4,5},{5,4},{6,7},{7,6},{8,9},{9,8},{10,11... | collective-permute-start | bytes 1966088 | tf_op jit(solution)/shard_map/ppermute | solution.py:429
  5.9 23.7 %collective-permute-start.5 = (bf16[640,512]{1,0:T(8,128)(2,1)}, bf16[640,512]{1,0:T(8,128)(2,1)S(1)}, u32[]{:S(2)}, u32[]{:S(2)}) collective-permute-start(bf16[640,512]{1,0:T(8,128)(2,1)} %input_ref.3), channel_id=1, source_target_pairs={{0,2},{1,3},{2,4},{3,5},{4,6},{5,7},{6,0},{7,1},{8,10},{9,11},{10,... | collective-permute-start | bytes 1966088 | tf_op jit(solution)/shard_map/ppermute | solution.py:429
  8.4 20.4 %collective-permute-start = (bf16[160,512]{1,0:T(8,128)(2,1)}, bf16[160,512]{1,0:T(8,128)(2,1)S(1)}, u32[]{:S(2)}, u32[]{:S(2)}) collective-permute-start(bf16[160,512]{1,0:T(8,128)(2,1)} %get-tuple-element.100), channel_id=1, source_target_pairs={{0,2},{1,3},{2,4},{3,5},{4,6},{5,7},{6,0},{7,1},{8,10},{9,11},{10,... | collective-permute-start | bytes 491528 | tf_op jit(solution)/shard_map/ppermute | solution.py:429
  19.1 9.7 %collective-permute-start.3 = (bf16[80,512]{1,0:T(8,128)(2,1)}, bf16[80,512]{1,0:T(8,128)(2,1)S(1)}, u32[]{:S(2)}, u32[]{:S(2)}) collective-permute-start(bf16[80,512]{1,0:T(8,128)(2,1)} %get-tuple-element.101), channel_id=1, source_target_pairs={{0,6},{1,7},{2,0},{3,1},{4,2},{5,3},{6,4},{7,5},{8,14},{9,15},{10,... | collective-permute-start | bytes 245768 | tf_op jit(solution)/shard_map/ppermute | solution.py:429
  29.7 28.6 %copy-start.8 = (bf16[640,512]{1,0:T(8,128)(2,1)}, bf16[640,512]{1,0:T(8,128)(2,1)S(1)}, u32[]{:S(2)}) copy-start(bf16[640,512]{1,0:T(8,128)(2,1)S(1)} %collective-permute-done.5.refs_0_) | copy-start | bytes 1966084
  29.7 26.4 %collective-permute-start.7 = (bf16[640,512]{1,0:T(8,128)(2,1)S(1)}, bf16[640,512]{1,0:T(8,128)(2,1)S(1)}, u32[]{:S(2)}, u32[]{:S(2)}) collective-permute-start(bf16[640,512]{1,0:T(8,128)(2,1)S(1)} %collective-permute-done.5.refs_0_), channel_id=1, source_target_pairs={{0,2},{1,3},{2,4},{3,5},{4,6},{5,7},{6,0},{7,1},{8,10},{9,11},{10,... | collective-permute-start | bytes 1966088 | tf_op jit(solution)/shard_map/ppermute | solution.py:429
  32.7 23.4 %collective-permute-start.8 = (bf16[640,512]{1,0:T(8,128)(2,1)S(1)}, bf16[640,512]{1,0:T(8,128)(2,1)S(1)}, u32[]{:S(2)}, u32[]{:S(2)}) collective-permute-start(bf16[640,512]{1,0:T(8,128)(2,1)S(1)} %collective-permute-done.5.refs_0_), channel_id=1, source_target_pairs={{0,1},{1,0},{2,3},{3,2},{4,5},{5,4},{6,7},{7,6},{8,9},{9,8},{10,11... | collective-permute-start | bytes 1966088 | tf_op jit(solution)/shard_map/ppermute | solution.py:429
  35.1 21.0 %collective-permute-start.6 = (bf16[4,80,512]{2,1,0:T(8,128)(2,1)S(1)}, bf16[4,80,512]{2,1,0:T(8,128)(2,1)S(1)}, u32[]{:S(2)}, u32[]{:S(2)}) collective-permute-start(bf16[4,80,512]{2,1,0:T(8,128)(2,1)S(1)} %get-tuple-element.218), channel_id=1, source_target_pairs={{0,1},{1,0},{2,3},{3,2},{4,5},{5,4},{6,7},{7,6},{8,9},{9,8},{10,11... | collective-permute-start | bytes 983048 | tf_op jit(solution)/shard_map/ppermute | solution.py:429
  35.7 14.6 %collective-permute-start.9 = (bf16[160,512]{1,0:T(8,128)(2,1)S(1)}, bf16[160,512]{1,0:T(8,128)(2,1)S(1)}, u32[]{:S(2)}, u32[]{:S(2)}) collective-permute-start(bf16[160,512]{1,0:T(8,128)(2,1)S(1)} %collective-permute-done), channel_id=1, source_target_pairs={{0,2},{1,3},{2,4},{3,5},{4,6},{5,7},{6,0},{7,1},{8,10},{9,11},{10,... | collective-permute-start | bytes 491528 | tf_op jit(solution)/shard_map/ppermute | solution.py:429
  56.1 20.4 %copy-start.9 = (bf16[640,512]{1,0:T(8,128)(2,1)}, bf16[640,512]{1,0:T(8,128)(2,1)S(1)}, u32[]{:S(2)}) copy-start(bf16[640,512]{1,0:T(8,128)(2,1)S(1)} %collective-permute-done.7.refs_0_) | copy-start | bytes 1966084
  56.1 19.2 %collective-permute-start.11 = (bf16[640,512]{1,0:T(8,128)(2,1)S(1)}, bf16[640,512]{1,0:T(8,128)(2,1)S(1)}, u32[]{:S(2)}, u32[]{:S(2)}) collective-permute-start(bf16[640,512]{1,0:T(8,128)(2,1)S(1)} %collective-permute-done.7.refs_0_), channel_id=1, source_target_pairs={{0,2},{1,3},{2,4},{3,5},{4,6},{5,7},{6,0},{7,1},{8,10},{9,11},{10,... | collective-permute-start | bytes 1966088 | tf_op jit(solution)/shard_map/ppermute | solution.py:429
  56.7 18.6 %collective-permute-start.12 = (bf16[640,512]{1,0:T(8,128)(2,1)S(1)}, bf16[640,512]{1,0:T(8,128)(2,1)S(1)}, u32[]{:S(2)}, u32[]{:S(2)}) collective-permute-start(bf16[640,512]{1,0:T(8,128)(2,1)S(1)} %collective-permute-done.7.refs_0_), channel_id=1, source_target_pairs={{0,1},{1,0},{2,3},{3,2},{4,5},{5,4},{6,7},{7,6},{8,9},{9,8},{10,11... | collective-permute-start | bytes 1966088 | tf_op jit(solution)/shard_map/ppermute | solution.py:429
  58.3 17.0 %collective-permute-start.10 = (bf16[2,4,80,512]{3,2,1,0:T(8,128)(2,1)S(1)}, bf16[2,4,80,512]{3,2,1,0:T(8,128)(2,1)S(1)}, u32[]{:S(2)}, u32[]{:S(2)}) collective-permute-start(bf16[2,4,80,512]{3,2,1,0:T(8,128)(2,1)S(1)} %get-tuple-element.205), channel_id=1, source_target_pairs={{0,16},{8,24},{16,0},{24,8},{1,17},{9,25},{17,1},{25,9},{2,18},{10... | collective-permute-start | bytes 1966088 | tf_op jit(solution)/shard_map/ppermute | solution.py:429
  58.9 16.4 %collective-permute-start.13 = (bf16[160,512]{1,0:T(8,128)(2,1)S(1)}, bf16[160,512]{1,0:T(8,128)(2,1)}, u32[]{:S(2)}, u32[]{:S(2)}) collective-permute-start(bf16[160,512]{1,0:T(8,128)(2,1)S(1)} %copy-done.19), channel_id=1, source_target_pairs={{0,2},{1,3},{2,4},{3,5},{4,6},{5,7},{6,0},{7,1},{8,10},{9,11},{10,... | collective-permute-start | bytes 491528 | tf_op jit(solution)/shard_map/ppermute | solution.py:429
  76.5 6.2 %collective-permute-start.14 = (bf16[16,80,512]{2,1,0:T(8,128)(2,1)S(1)}, bf16[16,80,512]{2,1,0:T(8,128)(2,1)}, u32[]{:S(2)}, u32[]{:S(2)}) collective-permute-start(bf16[16,80,512]{2,1,0:T(8,128)(2,1)S(1)} %bitcast.165), channel_id=1, source_target_pairs={{0,8},{8,0},{16,24},{24,16},{1,9},{9,1},{17,25},{25,17},{2,10},{10... | collective-permute-start | bytes 3932168 | tf_op jit(solution)/shard_map/ppermute | solution.py:429
  79.4 21.8 %collective-permute-start.16 = (bf16[4,80,512]{2,1,0:T(8,128)(2,1)}, bf16[4,80,512]{2,1,0:T(8,128)(2,1)S(1)}, u32[]{:S(2)}, u32[]{:S(2)}) collective-permute-start(bf16[4,80,512]{2,1,0:T(8,128)(2,1)} %get-tuple-element.216), channel_id=1, source_target_pairs={{0,1},{1,0},{2,3},{3,2},{4,5},{5,4},{6,7},{7,6},{8,9},{9,8},{10,11... | collective-permute-start | bytes 983048 | tf_op jit(solution)/shard_map/ppermute | solution.py:429
  81.7 19.6 %collective-permute-start.17 = (bf16[4,80,512]{2,1,0:T(8,128)(2,1)}, bf16[4,80,512]{2,1,0:T(8,128)(2,1)}, u32[]{:S(2)}, u32[]{:S(2)}) collective-permute-start(bf16[4,80,512]{2,1,0:T(8,128)(2,1)} %get-tuple-element.214), channel_id=1, source_target_pairs={{0,16},{8,24},{16,0},{24,8},{1,17},{9,25},{17,1},{25,9},{2,18},{10... | collective-permute-start | bytes 983048 | tf_op jit(solution)/shard_map/ppermute | solution.py:429
  82.2 21.4 %collective-permute-start.15 = (bf16[640,512]{1,0:T(8,128)(2,1)S(1)}, bf16[640,512]{1,0:T(8,128)(2,1)S(1)}, u32[]{:S(2)}, u32[]{:S(2)}) collective-permute-start(bf16[640,512]{1,0:T(8,128)(2,1)S(1)} %copy-done.12), channel_id=1, source_target_pairs={{0,1},{1,0},{2,3},{3,2},{4,5},{5,4},{6,7},{7,6},{8,9},{9,8},{10,11... | collective-permute-start | bytes 1966088 | tf_op jit(solution)/shard_map/ppermute | solution.py:429
  103.7 26.1 %collective-permute-start.18 = (bf16[2,4,80,512]{3,2,1,0:T(8,128)(2,1)S(1)}, bf16[2,4,80,512]{3,2,1,0:T(8,128)(2,1)}, u32[]{:S(2)}, u32[]{:S(2)}) collective-permute-start(bf16[2,4,80,512]{3,2,1,0:T(8,128)(2,1)S(1)} %pad_maximum_fusion.3), channel_id=1, source_target_pairs={{0,16},{8,24},{16,0},{24,8},{1,17},{9,25},{17,1},{25,9},{2,18},{10... | collective-permute-start | bytes 1966088 | tf_op jit(solution)/shard_map/ppermute | solution.py:429
  104.3 27.6 %collective-permute-start.20 = (bf16[2,4,80,512]{3,2,1,0:T(8,128)(2,1)S(1)}, bf16[2,4,80,512]{3,2,1,0:T(8,128)(2,1)}, u32[]{:S(2)}, u32[]{:S(2)}) collective-permute-start(bf16[2,4,80,512]{3,2,1,0:T(8,128)(2,1)S(1)} %pad_maximum_fusion.3), channel_id=1, source_target_pairs={{0,8},{8,0},{16,24},{24,16},{1,9},{9,1},{17,25},{25,17},{2,10},{10... | collective-permute-start | bytes 1966088 | tf_op jit(solution)/shard_map/ppermute | solution.py:429
  105.3 24.5 %collective-permute-start.19 = (bf16[2,4,80,512]{3,2,1,0:T(8,128)(2,1)S(1)}, bf16[2,4,80,512]{3,2,1,0:T(8,128)(2,1)}, u32[]{:S(2)}, u32[]{:S(2)}) collective-permute-start(bf16[2,4,80,512]{3,2,1,0:T(8,128)(2,1)S(1)} %pad_maximum_fusion.4), channel_id=1, source_target_pairs={{0,1},{1,0},{2,3},{3,2},{4,5},{5,4},{6,7},{7,6},{8,9},{9,8},{10,11... | collective-permute-start | bytes 1966088 | tf_op jit(solution)/shard_map/ppermute | solution.py:429
  106.9 25.0 %collective-permute-start.22 = (bf16[2,4,80,512]{3,2,1,0:T(8,128)(2,1)S(1)}, bf16[2,4,80,512]{3,2,1,0:T(8,128)(2,1)}, u32[]{:S(2)}, u32[]{:S(2)}) collective-permute-start(bf16[2,4,80,512]{3,2,1,0:T(8,128)(2,1)S(1)} %pad_maximum_fusion.4), channel_id=1, source_target_pairs={{0,8},{8,0},{16,24},{24,16},{1,9},{9,1},{17,25},{25,17},{2,10},{10... | collective-permute-start | bytes 1966088 | tf_op jit(solution)/shard_map/ppermute | solution.py:429
  129.8 2.4 collective-permute-start.21
  130.2 3.1 collective-permute-start.23
  133.2 25.5 %copy-start = (bf16[512,512]{1,0:T(8,128)(2,1)S(1)}, bf16[512,512]{1,0:T(8,128)(2,1)}, u32[]{:S(2)}) copy-start(bf16[512,512]{1,0:T(8,128)(2,1)} %get-tuple-element.113.refs_3_.key_weight_ref) | copy-start | bytes 1572868
  133.2 25.5 %copy-start.1 = (bf16[512,512]{1,0:T(8,128)(2,1)S(1)}, bf16[512,512]{1,0:T(8,128)(2,1)}, u32[]{:S(2)}) copy-start(bf16[512,512]{1,0:T(8,128)(2,1)} %get-tuple-element.114.refs_4_.value_weight_ref) | copy-start | bytes 1572868
  154.9 7.0 %collective-permute-start.24 = (bf16[2,4,2,176,512]{4,3,2,1,0:T(8,128)(2,1)}, bf16[2,4,2,176,512]{4,3,2,1,0:T(8,128)(2,1)S(1)}, u32[]{:S(2)}, u32[]{:S(2)}) collective-permute-start(bf16[2,4,2,176,512]{4,3,2,1,0:T(8,128)(2,1)} %bitcast.186), channel_id=1, source_target_pairs={{0,8},{8,0},{16,24},{24,16},{1,9},{9,1},{17,25},{25,17},{2,10},{10... | collective-permute-start | bytes 8650760 | tf_op jit(solution)/shard_map/ppermute | solution.py:429
  164.0 35.8 %collective-permute-start.25 = (bf16[4,2,176,512]{3,2,1,0:T(8,128)(2,1)}, bf16[4,2,176,512]{3,2,1,0:T(8,128)(2,1)S(1)}, u32[]{:S(2)}, u32[]{:S(2)}) collective-permute-start(bf16[4,2,176,512]{3,2,1,0:T(8,128)(2,1)} %get-tuple-element.155), channel_id=1, source_target_pairs={{0,16},{8,24},{16,0},{24,8},{1,17},{9,25},{17,1},{25,9},{2,18},{10... | collective-permute-start | bytes 4325384 | tf_op jit(solution)/shard_map/ppermute | solution.py:429
  206.3 15.0 %collective-permute-start.29 = (bf16[2,2,4,64,512]{4,3,2,1,0:T(8,128)(2,1)}, bf16[2,2,4,64,512]{4,3,2,1,0:T(8,128)(2,1)}, u32[]{:S(2)}, u32[]{:S(2)}) collective-permute-start(bf16[2,2,4,64,512]{4,3,2,1,0:T(8,128)(2,1)} %bitcast.187), channel_id=1, source_target_pairs={{0,8},{8,0},{16,24},{24,16},{1,9},{9,1},{17,25},{25,17},{2,10},{10... | collective-permute-start | bytes 3145736 | tf_op jit(solution)/shard_map/ppermute | solution.py:429
  207.6 12.4 %collective-permute-start.27 = (bf16[2,176,512]{2,1,0:T(8,128)(2,1)S(1)}, bf16[2,176,512]{2,1,0:T(8,128)(2,1)}, u32[]{:S(2)}, u32[]{:S(2)}) collective-permute-start(bf16[2,176,512]{2,1,0:T(8,128)(2,1)S(1)} %fusion.8), channel_id=1, source_target_pairs={{0,6},{1,7},{2,0},{3,1},{4,2},{5,3},{6,4},{7,5},{8,14},{9,15},{10,... | collective-permute-start | bytes 1081352 | tf_op jit(solution)/shard_map/ppermute | solution.py:429
  211.4 16.4 %collective-permute-start.26 = (bf16[5,512,128]{2,1,0:T(8,128)(2,1)S(1)}, bf16[5,512,128]{2,1,0:T(8,128)(2,1)S(1)}, u32[]{:S(2)}, u32[]{:S(2)}) collective-permute-start(bf16[5,512,128]{2,1,0:T(8,128)(2,1)S(1)} %get-tuple-element.192), channel_id=1, source_target_pairs={{0,1},{1,0},{2,3},{3,2},{4,5},{5,4},{6,7},{7,6},{8,9},{9,8},{10,11... | collective-permute-start | bytes 1966088 | tf_op jit(solution)/shard_map/ppermute | solution.py:429
  221.1 11.3 %collective-permute-start.28 = (bf16[2,176,512]{2,1,0:T(8,128)(2,1)S(1)}, bf16[2,176,512]{2,1,0:T(8,128)(2,1)S(1)}, u32[]{:S(2)}, u32[]{:S(2)}) collective-permute-start(bf16[2,176,512]{2,1,0:T(8,128)(2,1)S(1)} %fusion.6), channel_id=1, source_target_pairs={{0,6},{1,7},{2,0},{3,1},{4,2},{5,3},{6,4},{7,5},{8,14},{9,15},{10,... | collective-permute-start | bytes 1081352 | tf_op jit(solution)/shard_map/ppermute | solution.py:429
  233.8 24.4 %collective-permute-start.31 = (bf16[5,512,128]{2,1,0:T(8,128)(2,1)S(1)}, bf16[5,512,128]{2,1,0:T(8,128)(2,1)S(1)}, u32[]{:S(2)}, u32[]{:S(2)}) collective-permute-start(bf16[5,512,128]{2,1,0:T(8,128)(2,1)S(1)} %add_convert_fusion.2), channel_id=1, source_target_pairs={{0,6},{1,7},{2,0},{3,1},{4,2},{5,3},{6,4},{7,5},{8,14},{9,15},{10,... | collective-permute-start | bytes 1966088 | tf_op jit(solution)/shard_map/ppermute | solution.py:429
  233.9 24.4 %collective-permute-start.30 = (bf16[5,512,128]{2,1,0:T(8,128)(2,1)S(1)}, bf16[5,512,128]{2,1,0:T(8,128)(2,1)S(1)}, u32[]{:S(2)}, u32[]{:S(2)}) collective-permute-start(bf16[5,512,128]{2,1,0:T(8,128)(2,1)S(1)} %get-tuple-element.168), channel_id=1, source_target_pairs={{0,1},{1,0},{2,3},{3,2},{4,5},{5,4},{6,7},{7,6},{8,9},{9,8},{10,11... | collective-permute-start | bytes 1966088 | tf_op jit(solution)/shard_map/ppermute | solution.py:429
  234.8 23.4 %collective-permute-start.32 = (bf16[2,176,512]{2,1,0:T(8,128)(2,1)S(1)}, bf16[2,176,512]{2,1,0:T(8,128)(2,1)S(1)}, u32[]{:S(2)}, u32[]{:S(2)}) collective-permute-start(bf16[2,176,512]{2,1,0:T(8,128)(2,1)S(1)} %fusion.5), channel_id=1, source_target_pairs={{0,6},{1,7},{2,0},{3,1},{4,2},{5,3},{6,4},{7,5},{8,14},{9,15},{10,... | collective-permute-start | bytes 1081352 | tf_op jit(solution)/shard_map/ppermute | solution.py:429
  234.9 23.4 %collective-permute-start.33 = (bf16[2,4,64,512]{3,2,1,0:T(8,128)(2,1)S(1)}, bf16[2,4,64,512]{3,2,1,0:T(8,128)(2,1)S(1)}, u32[]{:S(2)}, u32[]{:S(2)}) collective-permute-start(bf16[2,4,64,512]{3,2,1,0:T(8,128)(2,1)S(1)} %get-tuple-element.170), channel_id=1, source_target_pairs={{0,16},{8,24},{16,0},{24,8},{1,17},{9,25},{17,1},{25,9},{2,18},{10... | collective-permute-start | bytes 1572872 | tf_op jit(solution)/shard_map/ppermute | solution.py:429
  259.6 20.2 %collective-permute-start.35 = (bf16[5,512,128]{2,1,0:T(8,128)(2,1)S(1)}, bf16[5,512,128]{2,1,0:T(8,128)(2,1)S(1)}, u32[]{:S(2)}, u32[]{:S(2)}) collective-permute-start(bf16[5,512,128]{2,1,0:T(8,128)(2,1)S(1)} %add_convert_fusion.1), channel_id=1, source_target_pairs={{0,6},{1,7},{2,0},{3,1},{4,2},{5,3},{6,4},{7,5},{8,14},{9,15},{10,... | collective-permute-start | bytes 1966088 | tf_op jit(solution)/shard_map/ppermute | solution.py:429
  259.7 20.2 %collective-permute-start.34 = (bf16[5,512,128]{2,1,0:T(8,128)(2,1)S(1)}, bf16[5,512,128]{2,1,0:T(8,128)(2,1)S(1)}, u32[]{:S(2)}, u32[]{:S(2)}) collective-permute-start(bf16[5,512,128]{2,1,0:T(8,128)(2,1)S(1)} %get-tuple-element.172), channel_id=1, source_target_pairs={{0,1},{1,0},{2,3},{3,2},{4,5},{5,4},{6,7},{7,6},{8,9},{9,8},{10,11... | collective-permute-start | bytes 1966088 | tf_op jit(solution)/shard_map/ppermute | solution.py:429
  261.3 18.6 %collective-permute-start.36 = (bf16[4,64,512]{2,1,0:T(8,128)(2,1)S(1)}, bf16[4,64,512]{2,1,0:T(8,128)(2,1)S(1)}, u32[]{:S(2)}, u32[]{:S(2)}) collective-permute-start(bf16[4,64,512]{2,1,0:T(8,128)(2,1)S(1)} %slice_bitcast_fusion.5), channel_id=1, source_target_pairs={{0,1},{1,0},{2,3},{3,2},{4,5},{5,4},{6,7},{7,6},{8,9},{9,8},{10,11... | collective-permute-start | bytes 786440 | tf_op jit(solution)/shard_map/ppermute | solution.py:429
  279.9 29.3 %collective-permute-start.42 = (bf16[176,512]{1,0:T(8,128)(2,1)S(1)}, bf16[176,512]{1,0:T(8,128)(2,1)S(1)}, u32[]{:S(2)}, u32[]{:S(2)}) collective-permute-start(bf16[176,512]{1,0:T(8,128)(2,1)S(1)} %slice_bitcast_fusion.7), channel_id=1, source_target_pairs={{0,1},{1,0},{2,3},{3,2},{4,5},{5,4},{6,7},{7,6},{8,9},{9,8},{10,11... | collective-permute-start | bytes 540680 | tf_op jit(solution)/shard_map/ppermute | solution.py:429
  281.7 7.8 %collective-permute-start.39 = (bf16[64,512]{1,0:T(8,128)(2,1)S(1)}, bf16[64,512]{1,0:T(8,128)(2,1)S(1)}, u32[]{:S(2)}, u32[]{:S(2)}) collective-permute-start(bf16[64,512]{1,0:T(8,128)(2,1)S(1)} %get-tuple-element.219), channel_id=1, source_target_pairs={{0,6},{1,7},{2,0},{3,1},{4,2},{5,3},{6,4},{7,5},{8,14},{9,15},{10,... | collective-permute-start | bytes 196616 | tf_op jit(solution)/shard_map/ppermute | solution.py:429
  281.8 9.6 %collective-permute-start.40 = (bf16[64,512]{1,0:T(8,128)(2,1)S(1)}, bf16[64,512]{1,0:T(8,128)(2,1)S(1)}, u32[]{:S(2)}, u32[]{:S(2)}) collective-permute-start(bf16[64,512]{1,0:T(8,128)(2,1)S(1)} %get-tuple-element.221), channel_id=1, source_target_pairs={{0,4},{1,5},{2,6},{3,7},{4,0},{5,1},{6,2},{7,3},{8,12},{9,13},{10,... | collective-permute-start | bytes 196616 | tf_op jit(solution)/shard_map/ppermute | solution.py:429
  286.1 17.7 %collective-permute-start.41 = (bf16[64,512]{1,0:T(8,128)(2,1)S(1)}, bf16[64,512]{1,0:T(8,128)(2,1)S(1)}, u32[]{:S(2)}, u32[]{:S(2)}) collective-permute-start(bf16[64,512]{1,0:T(8,128)(2,1)S(1)} %get-tuple-element.220), channel_id=1, source_target_pairs={{0,2},{1,3},{2,4},{3,5},{4,6},{5,7},{6,0},{7,1},{8,10},{9,11},{10,... | collective-permute-start | bytes 196616 | tf_op jit(solution)/shard_map/ppermute | solution.py:429
  287.4 23.8 %collective-permute-start.38 = (bf16[5,512,128]{2,1,0:T(8,128)(2,1)S(1)}, bf16[5,512,128]{2,1,0:T(8,128)(2,1)S(1)}, u32[]{:S(2)}, u32[]{:S(2)}) collective-permute-start(bf16[5,512,128]{2,1,0:T(8,128)(2,1)S(1)} %add_convert_fusion), channel_id=1, source_target_pairs={{0,6},{1,7},{2,0},{3,1},{4,2},{5,3},{6,4},{7,5},{8,14},{9,15},{10,... | collective-permute-start | bytes 1966088 | tf_op jit(solution)/shard_map/ppermute | solution.py:429
  289.5 21.7 %collective-permute-start.37 = (bf16[5,512,128]{2,1,0:T(8,128)(2,1)S(1)}, bf16[5,512,128]{2,1,0:T(8,128)(2,1)S(1)}, u32[]{:S(2)}, u32[]{:S(2)}) collective-permute-start(bf16[5,512,128]{2,1,0:T(8,128)(2,1)S(1)} %get-tuple-element.177), channel_id=1, source_target_pairs={{0,1},{1,0},{2,3},{3,2},{4,5},{5,4},{6,7},{7,6},{8,9},{9,8},{10,11... | collective-permute-start | bytes 1966088 | tf_op jit(solution)/shard_map/ppermute | solution.py:429
  (21 other events, 100.6 us)
where the time goes:
time: 322 us; the launch traced here: 317 us
  waiting for transfers between devices  115 us (36%)
  Pallas kernels  109 us (34%)
  starting transfers between devices  39.2 us (12%)
  other arithmetic  30.3 us (9%)
  local copies, waits for them, and re-layouts  19.3 us (6%)
    ppermute x43, waiting for transfers between devices, rotate(): return lax.ppermute(values, self.name, pairs)  115 us
    ppermute x43, starting transfers between devices, rotate(): return lax.ppermute(values, self.name, pairs)  39.2 us
    pallas_call x1, Pallas kernels, attend_backward(): pl.pallas_call(backward_kernel, cost_estimate=about(32), out_shape=(jax.S...  33.6 us
    pallas_call x4, Pallas kernels, local_call(): pl.pallas_call(kernel, cost_estimate=about(cost), out_shape=outs, in_spec...  33.1 us
    pallas_call x4, Pallas kernels, project(): pl.pallas_call(body, cost_estimate=about(4), grid=(1,), out_shape=[whole]...  20.2 us
    pallas_call x1, Pallas kernels, attend(): pl.pallas_call(forward_kernel, cost_estimate=about(18), out_shape=(jax.Sh...  17.8 us
    reduce_sum x10, other arithmetic, lookup(): jnp.sum(jnp.where(matches, lookup_table, jnp.int32(0)), axis=-1, dtype=jn...  7.79 us
    convert_element_type x9, other arithmetic, add_low(): (left_side.astype(jnp.float32) + right_side.astype(jnp.float32)).astype(j...  6.7 us
  transfers between devices with their start and end apart: 43, of which 14 were waited for; matrix products, arithmetic and copies ran while one was open for 14% of the time, Pallas kernels for 24%

commit v1 on v0

--- a/solution.py
+++ b/solution.py
@@ -168,21 +168,13 @@
     query_grad_ref,
     grads_ref,
     lanes_ref,
-    shared_ref,
-    key_here,
-    value_here,
-    bias_ref,
-    normed_here,
-    key_sums,
-    value_sums,
-    stage,
-    zero_block,
-    arrivals,
-    normed_arrivals,
-    departures,
+    *refs,
 ):
     width = query_ref.shape[1]
     count = query_ref.shape[0] // BLK
+    shared_refs = refs[:-11]
+    key_here, value_here, bias_ref, normed_here, key_sums, value_sums = refs[-11:-5]
+    stage, zero_block, arrivals, normed_arrivals, departures = refs[-5:]
     places = used_ref.shape[1] - 1
     used_count = used_ref[0, places]
     levels = Levels(slots_ref, (key_source, value_source), (key_here, value_here), arrivals)
@@ -204,11 +196,12 @@
             normed_here[place * BLK : (place + 1) * BLK, :] = jnp.zeros((BLK, normed_here.shape[1]), jnp.bfloat16)
 
     zero_block[...] = jnp.zeros_like(zero_block)
-    for slot in range(shared_ref.shape[0]):
+    for slot in range(count * len(shared_refs)):
 
         @pl.when(seen_ref[0, slot] == 0)
         def none():
-            pltpu.make_async_copy(zero_block, shared_ref.at[slot], departures.at[slot]).start()
+            target = shared_refs[slot // count].at[slot % count]
+            pltpu.make_async_copy(zero_block, target, departures.at[slot]).start()
 
     key_sums[...] = jnp.zeros_like(key_sums)
     value_sums[...] = jnp.zeros_like(value_sums)
@@ -270,16 +263,20 @@
             place = step * PLACES + index
             stage[place] = shared[:, index * BLK : (index + 1) * BLK].astype(jnp.bfloat16)
 
-            @pl.when(place < used_count)
-            def leave():
-                slot = used_ref[0, place]
-                pltpu.make_async_copy(stage.at[place], shared_ref.at[slot], departures.at[slot]).start()
+            slot = used_ref[0, jnp.minimum(place, used_count - 1)]
+            for piece, shared_ref in enumerate(shared_refs):
+
+                @pl.when((place < used_count) & (slot // count == piece))
+                def leave():
+                    target = shared_ref.at[slot - piece * count]
+                    pltpu.make_async_copy(stage.at[place], target, departures.at[slot]).start()
 
         return carry
 
     lax.fori_loop(0, (used_count + PLACES - 1) // PLACES, some_places, 0)
-    for slot in range(shared_ref.shape[0]):
-        pltpu.make_async_copy(zero_block, shared_ref.at[slot], departures.at[slot]).wait()
+    for slot in range(count * len(shared_refs)):
+        target = shared_refs[slot // count].at[slot % count]
+        pltpu.make_async_copy(zero_block, target, departures.at[slot]).wait()
 
 
 def about(cost):
@@ -325,6 +322,7 @@
 def attend_backward(tables, query_rows, key_group, value_group, logsum, mixed, mixed_grad, normed_group, both_weight):
     rows, width = query_rows.shape
     blocks = normed_group.shape[0] // BLK
+    pieces = normed_group.shape[0] // rows
     places = tables[2].shape[1] - 1
     return pl.pallas_call(
         backward_kernel,
@@ -333,11 +331,11 @@
             jax.ShapeDtypeStruct((rows, width), jnp.bfloat16),
             jax.ShapeDtypeStruct((2 * width, width), jnp.float32),
             jax.ShapeDtypeStruct((2 * width, BLK), jnp.float32),
-            jax.ShapeDtypeStruct((blocks, width, BLK), jnp.bfloat16),
-        ),
+        )
+        + (jax.ShapeDtypeStruct((rows // BLK, width, BLK), jnp.bfloat16),) * pieces,
         in_specs=[in_smem()] * 4
         + [in_vmem(), anywhere(), anywhere(), in_vmem(), in_vmem(), in_vmem(), anywhere(), in_vmem()],
-        out_specs=(in_vmem(), in_vmem(), in_vmem(), anywhere()),
+        out_specs=(in_vmem(),) * 3 + (anywhere(),) * pieces,
         scratch_shapes=level_scratch(width)
         + [
             pltpu.VMEM((places * BLK, width), jnp.bfloat16),
@@ -371,7 +369,7 @@
     return compact, used.reshape(1, -1), seen.reshape(1, -1)
 
 
-def project(pieces, vectors, key_weight, value_weight, group_rows, step, carried, query_weight=None):
+def project(pieces, vectors, key_weight, value_weight, group_rows, first, carried, query_weight=None):
     count = len(pieces)
     rows, width = pieces[0].shape
     weights = [key_weight, value_weight] + ([] if query_weight is None else [query_weight])
@@ -380,33 +378,57 @@
     def body(*refs):
         piece_refs, vectors_ref = refs[:count], refs[count]
         weight_refs = refs[count + 1 : count + 1 + len(weights)]
-        outs = refs[count + 1 + len(weights) + len(extra) :]
-        normed_ref, key_ref, value_ref = outs[:3]
+        outs = refs[count + 1 + len(weights) + len(extra) : -4]
+        piece_here, made, arrivals, departures = refs[-4:]
         gain = vectors_ref[GAIN_ONE : GAIN_ONE + 1, :]
         shift = vectors_ref[SHIFT_ONE : SHIFT_ONE + 1, :]
-        for index, piece in enumerate(piece_refs):
-            here = slice(index * rows, (index + 1) * rows)
-            normed = normalize(piece[...].astype(jnp.float32), gain, shift).astype(jnp.bfloat16)
-            normed_ref[here, :] = normed
-            key_ref[here, :] = matmul(normed, weight_refs[0][...]).astype(jnp.bfloat16)
-            value_ref[here, :] = matmul(normed, weight_refs[1][...]).astype(jnp.bfloat16)
+
+        def fetch(index):
+            return pltpu.make_async_copy(piece_refs[index], piece_here.at[index % 2], arrivals.at[index])
+
+        def leave(index, kind):
+            target = outs[kind].at[(first + index) * rows : (first + index + 1) * rows, :]
+            return pltpu.make_async_copy(made.at[index % 2, kind], target, departures.at[index, kind])
+
+        for index in range(min(2, count)):
+            fetch(index).start()
+        for index in range(count):
+            fetch(index).wait()
+            normed = normalize(piece_here[index % 2].astype(jnp.float32), gain, shift).astype(jnp.bfloat16)
+            if index + 2 < count:
+                fetch(index + 2).start()
+            if index >= 2:
+                for kind in range(3):
+                    leave(index - 2, kind).wait()
+            made[index % 2, 0] = normed
+            leave(index, 0).start()
+            for kind in (1, 2):
+                made[index % 2, kind] = matmul(normed, weight_refs[kind - 1][...]).astype(jnp.bfloat16)
+                leave(index, kind).start()
             if index == 0 and len(outs) > 3:
                 outs[3][...] = normed
                 queries = matmul(normed, weight_refs[2][...]).astype(jnp.bfloat16)
                 outs[4][...] = (queries.astype(jnp.float32) * (HD ** (-0.5))).astype(jnp.bfloat16)
-
-    block = pl.BlockSpec((count * rows, width), lambda index: (step, 0))
+        for index in range(max(0, count - 2), count):
+            for kind in range(3):
+                leave(index, kind).wait()
+
     whole = jax.ShapeDtypeStruct((group_rows, width), jnp.bfloat16)
     own = [] if query_weight is None else [jax.ShapeDtypeStruct((rows, width), jnp.bfloat16)] * 2
-    first = count + 1 + len(weights)
+    inputs = count + 1 + len(weights)
     return pl.pallas_call(
         body,
-        cost_estimate=about(4),
-        grid=(1,),
+        cost_estimate=about(1 + 1.6 * count),
         out_shape=[whole] * 3 + own,
-        in_specs=[in_vmem()] * first + [pl.BlockSpec(memory_space=pl.ANY)] * len(extra),
-        out_specs=[block] * 3 + [in_vmem()] * len(own),
-        input_output_aliases={first + index: index for index in range(len(extra))},
+        in_specs=[anywhere()] * count + [in_vmem()] * (1 + len(weights)) + [anywhere()] * len(extra),
+        out_specs=[anywhere()] * 3 + [in_vmem()] * len(own),
+        scratch_shapes=[
+            pltpu.VMEM((2, rows, width), jnp.bfloat16),
+            pltpu.VMEM((2, 3, rows, width), jnp.bfloat16),
+            pltpu.SemaphoreType.DMA((count,)),
+            pltpu.SemaphoreType.DMA((count, 3)),
+        ],
+        input_output_aliases={inputs + index: index for index in range(len(extra))},
         compiler_params=pltpu.CompilerParams(vmem_limit_bytes=VMEM_BYTES),
     )(*pieces, vectors, *weights, *extra)
 
@@ -480,21 +502,20 @@
     return running
 
 
-def pair_scatter(keep, send, axis):
-    arrived = axis.rotate(send, -1)
-    return lambda index: add_low(arrived[index], keep[index])
-
-
 GATE_B, DOWN_B, CARRY_B, GAIN_ONE, SHIFT_ONE, GAIN_TWO, SHIFT_TWO, UP_B = range(8)
 VECTOR_ROWS = 16
 MIDDLE_ROWS = 640
 
 
 def pack_kernel(devices, place_ref, *refs):
-    early_sources, late_sources, vector_refs, (early_ref, late_ref) = refs[:4], refs[4:8], refs[8:16], refs[16:]
+    early_sources, late_sources, vector_refs, (early_ref, all_ref) = refs[:4], refs[4:8], refs[8:16], refs[16:]
     width = early_ref.shape[1]
-    for target, sources in ((early_ref, early_sources), (late_ref, late_sources)):
-        start = 0
+    early_count = early_ref.shape[0]
+    for target, start, sources in (
+        (early_ref, 0, early_sources),
+        (all_ref, 0, early_sources),
+        (all_ref, early_count, late_sources),
+    ):
         for source in sources:
             rows = source.shape[0]
             for column in range(0, source.shape[1], width):
@@ -510,7 +531,8 @@
             spot = jnp.where(feature == column + part * width, jnp.float32(1.0), jnp.float32(0.0))
             spread = matmul(source[...], spot.astype(jnp.bfloat16))
             block += jnp.where(line == index + part, spread, jnp.float32(0.0))
-    early_ref[early_ref.shape[0] - VECTOR_ROWS :, :] = block.astype(jnp.bfloat16)
+    early_ref[early_count - VECTOR_ROWS :, :] = block.astype(jnp.bfloat16)
+    all_ref[early_count - VECTOR_ROWS : early_count, :] = block.astype(jnp.bfloat16)
 
 
 def unpack_kernel(place_ref, mine_ref, other_ref, query_ref, key_ref, value_ref, gate_ref, vectors_ref):
@@ -545,11 +567,11 @@
         carry_ref[target, :] = source[down_rows:, :]
 
 
-def spread_rows(place_ref, grad_ref, keep_ref, send_ref, start, rows):
-    half = keep_ref.shape[0]
-    for index in range(2 * half):
+def spread_rows(place_ref, grad_ref, pack_refs, start, rows):
+    size = pack_refs[0].shape[0]
+    for index in range(size * len(pack_refs)):
         source = pl.ds(pl.multiple_of(place_ref[index] * rows, rows), rows)
-        target = (keep_ref if index < half else send_ref).at[index % half]
+        target = pack_refs[index // size].at[index % size]
         target[start : start + rows, :] = grad_ref[source, :].astype(jnp.bfloat16)
 
 
@@ -564,9 +586,10 @@
     *refs,
 ):
     late_refs, refs = refs[:8], refs[8:]
-    output_ref, middle_grad_ref, attended_grad_ref, gate_pre_ref, block_ref, keep_ref, send_ref = refs[:7]
-    output_weight, up_weight, down_weight, carry_weight, hidden, up_pre_grads = refs[7:13]
-    update_grads, normed_second, carry_pre_grads, branch_grads, up_grad, down_grad, square_grads = refs[13:]
+    output_ref, middle_grad_ref, attended_grad_ref, gate_pre_ref, block_ref = refs[:5]
+    pack_refs = refs[5:9]
+    output_weight, up_weight, down_weight, carry_weight, hidden, up_pre_grads = refs[9:15]
+    update_grads, normed_second, carry_pre_grads, branch_grads, up_grad, down_grad, square_grads = refs[15:]
     unpack_late(
         place_ref,
         late_refs[:4],
@@ -640,23 +663,23 @@
     block_ref[...] = block
 
     target_ref = place_ref.at[2]
-    rows = width // (2 * keep_ref.shape[0])
+    rows = width // (4 * pack_refs[0].shape[0])
     place = 0
     for part in range(wide):
         grad = up_grad.at[part]
         grad[...] = inner_rows(normed_second[...], up_pre_grads[:, part * width : (part + 1) * width])
-        spread_rows(target_ref, grad, keep_ref, send_ref, place, rows)
+        spread_rows(target_ref, grad, pack_refs, place, rows)
         place += rows
     for part in range(wide):
         here = slice(part * width, (part + 1) * width)
         down_grad[here, :] = inner_rows(hidden[:, here], update_grads[...])
-    spread_rows(target_ref, down_grad, keep_ref, send_ref, place, wide * rows)
+    spread_rows(target_ref, down_grad, pack_refs, place, wide * rows)
     place += wide * rows
     pairs = ((normed_second, carry_pre_grads), (attended_ref, branch_grads), (normed_ref, gate_pre_ref))
     for index, (left_ref, right_ref) in enumerate(pairs):
         grad = square_grads.at[index]
         grad[...] = inner_rows(left_ref[...], right_ref[...])
-        spread_rows(target_ref, grad, keep_ref, send_ref, place, rows)
+        spread_rows(target_ref, grad, pack_refs, place, rows)
         place += rows
 
 
@@ -673,17 +696,16 @@
     gate_weight_ref,
     vectors_ref,
     block_ref,
-    keep_ref,
-    send_ref,
-    grads,
+    *refs,
 ):
-    width = keep_ref.shape[2]
-    rows = width // (2 * keep_ref.shape[0])
+    pack_refs, grads = refs[:4], refs[4]
+    width = pack_refs[0].shape[2]
+    rows = width // (4 * pack_refs[0].shape[0])
     grads[0] = inner_rows(normed_ref[...], query_grad_ref[...])
     grads[1] = jnp.transpose(both_grads_ref[:width, :])
     grads[2] = jnp.transpose(both_grads_ref[width:, :])
     for index in range(3):
-        spread_rows(place_ref, grads.at[index], keep_ref, send_ref, index * rows, rows)
+        spread_rows(place_ref, grads.at[index], pack_refs, index * rows, rows)
     gate_grad = inner_rows(normed_ref[...], gate_pre_ref[...])
 
     def line_sums(ref):
@@ -712,9 +734,9 @@
     place = lax.broadcasted_iota(jnp.int32, block_ref.shape, 0)
     block = jnp.where(place == GAIN_ONE, gain_line, block_ref[...])
     block = jnp.where(place == SHIFT_ONE, shift_line, block).astype(jnp.bfloat16)
-    for index in range(keep_ref.shape[0]):
-        keep_ref[index, 3 * rows :, :] = block
-        send_ref[index, 3 * rows :, :] = block
+    for pack_ref in pack_refs:
+        for index in range(pack_ref.shape[0]):
+            pack_ref[index, 3 * rows :, :] = block
 
 
 def input_grad_kernel(input_ref, local_ref, middle_grad_ref, vectors_ref, *refs):
@@ -801,28 +823,43 @@
     def flat_rows(pieces):
         return [piece[:, start : start + width] for piece in pieces for start in range(0, piece.shape[1], width)]
 
+    own_start = lax.axis_index("seq") * block_count
+    own_segments = lax.dynamic_slice_in_dim(block_segment, own_start, block_count)
+    ancestor_slot, usable = ancestor_slots(block_segment, segment_parent, own_segments)
+    owner = ancestor_slot // block_count
+    away_z = (axis_z.position() - owner // axis_x.size) % axis_z.size
+    away_x = (axis_x.position() - owner % axis_x.size) % axis_x.size
+    relative_slot = (away_z * axis_x.size + away_x) * block_count + ancestor_slot % block_count
+    tables = used_places(relative_slot, usable, group_blocks)
+    slots = jnp.concatenate(
+        [relative_slot, jnp.sum(usable, axis=-1, keepdims=True, dtype=jnp.int32)], axis=-1
+    )
+
     if direct:
         early_count = 4 * rows_each + VECTOR_ROWS
         late_count = sum(piece.shape[0] * piece.shape[1] // width for piece in late_set)
-        early, late = local_call(
+        early, both = local_call(
             functools.partial(pack_kernel, devices),
             0.1,
-            (struct(early_count, width), struct(late_count, width)),
+            (struct(early_count, width), struct(early_count + late_count, width)),
             device.reshape(1),
             early_set + late_set + tuple(vector.reshape(1, -1) for vector in vectors),
         )
-        late_line = [late]
-        late_line.append(axis_z.rotate(late, 1))
-        early_line = [axis_z.rotate(early, back) for back in range(1, 4)]
+        both_one = axis_z.rotate(both, 1)
+        early_line = [axis_z.rotate(early, back) for back in range(2, 4)]
         x_zero = axis_x.rotate(inputs, 1)
         z_one = axis_z.rotate(inputs, 1)
-        late_line[1], early_line, x_zero, z_one = lax.optimization_barrier((late_line[1], early_line, x_zero, z_one))
+        both_one, early_line, x_zero, z_one = lax.optimization_barrier((both_one, early_line, x_zero, z_one))
+        early_line = [both_one[:early_count]] + list(early_line)
+        late_line = [both[early_count:], both_one[early_count:]]
         z_two = axis_z.rotate(z_one, 1)
         x_one = axis_x.rotate(z_one, 1)
         early_line = jnp.stack([early] + list(early_line))
         early_other = axis_x.rotate(early_line, 1)
         late_line.append(axis_z.rotate(late_line[1], 1))
-        early_other, z_two, x_one, late_line[2] = lax.optimization_barrier((early_other, z_two, x_one, late_line[2]))
+        early_other, z_two, x_one, late_line[2], slots, tables = lax.optimization_barrier(
+            (early_other, z_two, x_one, late_line[2], slots, tables)
+        )
         z_three = axis_z.rotate(z_two, 1)
         x_two = axis_x.rotate(z_two, 1)
         early_plane = jnp.stack([early_line, early_other])
@@ -834,11 +871,6 @@
         x_three = axis_x.rotate(z_three, 1)
         early_all = jnp.stack([early_plane, early_other]).reshape(devices // 2, early_count, width)
         early_other = axis_core.rotate(early_all, 1)
-        late_half = late_count // 2
-        late_x = jnp.stack([rows[:late_half] for rows in late_line])
-        late_y = jnp.stack([rows[late_half:] for rows in late_line])
-        late_x_other = axis_x.rotate(late_x, 1)
-        late_y_other = axis_y.rotate(late_y, 1)
         input_pieces = [[inputs, x_zero], [z_one, x_one], [z_two, x_two], [z_three, x_three]]
         square = struct(width, width)
         full_query, full_key, full_value, full_gate, vector_rows = local_call(
@@ -848,6 +880,12 @@
             places,
             (early_all, early_other),
         )
+        late_line, full_key = lax.optimization_barrier((late_line, full_key))
+        late_half = late_count // 2
+        late_x = jnp.stack([rows[:late_half] for rows in late_line])
+        late_y = jnp.stack([rows[late_half:] for rows in late_line])
+        late_x_other = axis_x.rotate(late_x, 1)
+        late_y_other = axis_y.rotate(late_y, 1)
     else:
         early_rows = lax.all_gather(jnp.concatenate(early_set), BOTH)
         late_rows = lax.all_gather(jnp.concatenate(flat_rows(late_set)), BOTH)
@@ -875,38 +913,27 @@
             input_pieces.append(row)
             along_z = axis_z.rotate(along_z, 1) if step_z + 1 < axis_z.size else None
 
-    carried = None
-    for step, row in enumerate(input_pieces):
-        if direct and step == 3:
-            x_three, late_x_other, late_y_other, carried = lax.optimization_barrier(
-                (row[1], late_x_other, late_y_other, carried)
-            )
-            row = [row[0], x_three]
-            late_x = jnp.stack([late_x, late_x_other])
-            late_y = jnp.stack([late_y, late_y_other])
-            late_x_other = axis_y.rotate(late_x, 1)
-            late_y_other = axis_x.rotate(late_y, 1)
-        asked = full_query if step == 0 else None
-        done = project(row, vector_rows, full_key, full_value, group_blocks * BLK, step, carried, asked)
-        carried = done[:3]
-        if step == 0:
-            normed_low, query_low = done[3:]
+    both_weight = jnp.concatenate([full_key, full_value], axis=1)
+
+    group_rows = group_blocks * BLK
+    pieces = [piece for row in input_pieces for piece in row]
+    near = len(pieces) - 1 if direct else len(pieces)
+    *carried, normed_low, query_low = project(
+        pieces[:near], vector_rows, full_key, full_value, group_rows, 0, None, full_query
+    )
+    if direct:
+        late_y_other, late_x_other, x_three, carried, both_weight = lax.optimization_barrier(
+            (late_y_other, late_x_other, pieces[near], carried, both_weight)
+        )
+        late_x = jnp.stack([late_x, late_x_other])
+        late_y = jnp.stack([late_y, late_y_other])
+        late_x_other = axis_y.rotate(late_x, 1)
+        late_y_other = axis_x.rotate(late_y, 1)
+        carried = project([x_three], vector_rows, full_key, full_value, group_rows, near, carried)
     normed_group, key_group, value_group = carried
 
     gate_b, down_b, carry_b, gain_one, shift_one, gain_two, shift_two = [vector_rows[line] for line in range(UP_B)]
     up_b = vector_rows[UP_B : UP_B + up_weight.shape[1] // width].reshape(-1)
-
-    own_start = lax.axis_index("seq") * block_count
-    own_segments = lax.dynamic_slice_in_dim(block_segment, own_start, block_count)
-    ancestor_slot, usable = ancestor_slots(block_segment, segment_parent, own_segments)
-    owner = ancestor_slot // block_count
-    away_z = (axis_z.position() - owner // axis_x.size) % axis_z.size
-    away_x = (axis_x.position() - owner % axis_x.size) % axis_x.size
-    relative_slot = (away_z * axis_x.size + away_x) * block_count + ancestor_slot % block_count
-    tables = used_places(relative_slot, usable, group_blocks)
-    slots = jnp.concatenate(
-        [relative_slot, jnp.sum(usable, axis=-1, keepdims=True, dtype=jnp.int32)], axis=-1
-    )
 
     values_in = inputs.astype(jnp.float32)
     attended_low, logsum = attend(slots, query_low, key_group, value_group)
@@ -921,9 +948,9 @@
         rows = inputs.shape[0]
         first_rows = late_count + rows_each
         hidden_width = up_weight.shape[1]
-        half = struct(devices // 2, first_rows, width)
+        quarter = struct(devices // 4, first_rows, width)
         tall, short = pltpu.VMEM((rows, hidden_width), low), pltpu.VMEM((rows, width), low)
-        output, middle_grad, attended_grad, gate_pre_grad, block, first_keep, first_send = local_call(
+        output, middle_grad, attended_grad, gate_pre_grad, block, *first = local_call(
             middle_kernel,
             28,
             (
@@ -932,9 +959,8 @@
                 struct(rows, width),
                 struct(rows, width),
                 struct(VECTOR_ROWS, width, dtype=jnp.float32),
-                half,
-                half,
-            ),
+            )
+            + (quarter,) * 4,
             jnp.stack([places, other_places, targets]),
             (
                 attended_low,
@@ -961,9 +987,9 @@
                 pltpu.VMEM((3, width, width), jnp.float32),
             ),
         )
-        near = (2, 4, 2, first_rows, width)
-        first_entry = pair_scatter(first_keep.reshape(near), first_send.reshape(near), axis_core)
-        first_keep, first_send = first_entry(0), first_entry(1)
+        first = [pack.reshape(4, 2, first_rows, width) for pack in first]
+        first_core = [axis_core.rotate(first[2 + index], -1) for index in range(2)]
+        first_keep, first_send = [add_low(first_core[index], first[index]) for index in range(2)]
         attended_grad, first_keep, first_send = lax.optimization_barrier((attended_grad, first_keep, first_send))
         first_arrived = axis_y.rotate(first_send, -1)
     else:
@@ -1017,7 +1043,7 @@
         attended_low,
         attended_grad,
         normed_group,
-        jnp.concatenate([full_key, full_value], axis=1),
+        both_weight,
     )
     if direct:
         backward, first_arrived = lax.optimization_barrier((backward, first_arrived))
@@ -1026,19 +1052,17 @@
             return add_low(first_arrived[back], first_keep[back])
 
         first_z = axis_z.rotate(first_y(3), -1)
-    query_rows_grad, both_grads, lanes, shared_rows = backward
-
-    shared_parts = [
-        shared_rows[start : start + block_count] for start in range(0, group_blocks, block_count)
-    ]
+    query_rows_grad, both_grads, lanes = backward[:3]
+
+    shared_parts = backward[3:]
 
     if direct:
         second_rows = 3 * rows_each + VECTOR_ROWS
-        half = struct(devices // 2, second_rows, width)
-        second_keep, second_send = local_call(
+        quarter = struct(devices // 4, second_rows, width)
+        second = local_call(
             second_grads_kernel,
             0.1,
-            (half, half),
+            (quarter,) * 4,
             places,
             (
                 both_grads,
@@ -1055,15 +1079,15 @@
             ),
             (pltpu.VMEM((3, width, width), jnp.float32),),
         )
-        near = (2, 2, 4, second_rows, width)
-        second_entry = pair_scatter(second_keep.reshape(near), second_send.reshape(near), axis_core)
+        second = [pack.reshape(2, 4, second_rows, width) for pack in second]
         barrier = lax.optimization_barrier
         first_z = axis_z.rotate(add_low(first_z, first_y(2)), -1)
         x_three = axis_x.rotate(shared_parts[7], -1)
-        second_keep, second_send = second_entry(0), second_entry(1)
-        x_three, first_z, second_keep, second_send = barrier((x_three, first_z, second_keep, second_send))
-
-        second_arrived = axis_y.rotate(second_send, -1)
+        x_three, first_z, second = barrier((x_three, first_z, second))
+
+        second_core = [axis_core.rotate(second[2 + index], -1) for index in range(2)]
+        second_keep = add_low(second_core[0], second[0])
+        second_arrived = axis_y.rotate(add_low(second_core[1], second[1]), -1)
         x_two = axis_x.rotate(tied(shared_parts[5], x_three), -1)
         z_three = axis_z.rotate(add_low(x_three, shared_parts[6]), -1)
         first_z = axis_z.rotate(add_low(first_z, first_y(1)), -1)
@@ -1131,11 +1155,10 @@
         return joined(blocks, 1), start + parts * rows
 
     local_grad = against(query_rows_grad, full_query) + against(gate_pre_grad, full_gate)
-    rows = inputs.shape[0]
     input_grad = pl.pallas_call(
         input_grad_kernel,
         cost_estimate=about(3),
-        out_shape=struct(rows, width, dtype=jnp.float32),
+        out_shape=struct(block_count * BLK, width, dtype=jnp.float32),
         compiler_params=pltpu.CompilerParams(vmem_limit_bytes=VMEM_BYTES),
     )(inputs, local_grad, middle_grad, vector_rows, *shared)
 

time: 322 us -> 308 us (0.957)
  local copies, waits for them, and re-layouts: 19.3 us -> 14.4 us
  waiting for transfers between devices: 115 us -> 111 us
  other arithmetic: 30.3 us -> 26.5 us
    slice x3 -> x2, local copies, waits for them, and re-layouts: 5.11 us -> 0.02 us  [shards(): late_line = [both[early_count:], both_one[early_count:]]]
    ppermute x43 -> x44, waiting for transfers between devices: 115 us -> 111 us  [rotate(): return lax.ppermute(values, self.name, pairs)]
    pallas_call x4 -> x2, Pallas kernels: 20.2 us -> 18.6 us  [project(): pl.pallas_call(body, cost_estimate=about(1 + 1.6 * count), out_shape=[who...]
    convert_element_type x9 -> x10, other arithmetic: 6.7 us -> 7.5 us  [add_low(): (left_side.astype(jnp.float32) + right_side.astype(jnp.float32)).astype(j...]
    ppermute x43 -> x44, starting transfers between devices: 39.2 us -> 39.3 us  [rotate(): return lax.ppermute(values, self.name, pairs)]
  transfers between devices with their start and end apart: 43 -> 44, of which waited for: 14 -> 16; matrix products, arithmetic and copies ran while one was open for 14% -> 12% of each run, Pallas kernels for 24% -> 27%
where the time goes in v1:
time: 308 us; the launch traced here: 304 us
  waiting for transfers between devices  111 us (36%)
  Pallas kernels  109 us (35%)
  starting transfers between devices  39.3 us (13%)
  other arithmetic  26.5 us (9%)
  local copies, waits for them, and re-layouts  14.4 us (5%)
    ppermute x44, waiting for transfers between devices, rotate(): return lax.ppermute(values, self.name, pairs)  111 us
    ppermute x44, starting transfers between devices, rotate(): return lax.ppermute(values, self.name, pairs)  39.3 us
    pallas_call x1, Pallas kernels, attend_backward(): pl.pallas_call(backward_kernel, cost_estimate=about(32), out_shape=(jax.S...  34.3 us
    pallas_call x4, Pallas kernels, local_call(): pl.pallas_call(kernel, cost_estimate=about(cost), out_shape=outs, in_spec...  32.8 us
    pallas_call x1, Pallas kernels, attend(): pl.pallas_call(forward_kernel, cost_estimate=about(18), out_shape=(jax.Sh...  18.8 us
    pallas_call x2, Pallas kernels, project(): pl.pallas_call(body, cost_estimate=about(1 + 1.6 * count), out_shape=[who...  18.6 us
    reduce_sum x10, other arithmetic, lookup(): jnp.sum(jnp.where(matches, lookup_table, jnp.int32(0)), axis=-1, dtype=jn...  7.79 us
    convert_element_type x10, other arithmetic, add_low(): (left_side.astype(jnp.float32) + right_side.astype(jnp.float32)).astype(j...  7.5 us
  transfers between devices with their start and end apart: 44, of which 16 were waited for; matrix products, arithmetic and copies ran while one was open for 12% of the time, Pallas kernels for 27%

profile of v1, /device:TPU:28, one launch (start us, length us, event | category | flops | bytes accessed | tf_op | source)
XLA Modules:
  0.0 304.4 jit_solution(1760670816174252117)
XLA Ops:
  0.7 1.9 shard_map.331
  3.4 1.5 collective-permute-start.3
  4.9 3.4 %collective-permute-start.4 = (bf16[640,512]{1,0:T(8,128)(2,1)}, bf16[640,512]{1,0:T(8,128)(2,1)S(1)}, u32[]{:S(2)}, u32[]{:S(2)}) collective-permute-start(bf16[640,512]{1,0:T(8,128)(2,1)} %input_ref.3), channel_id=1, source_target_pairs={{0,2},{1,3},{2,4},{3,5},{4,6},{5,7},{6,0},{7,1},{8,10},{9,11},{10,... | collective-permute-start | bytes 1966088 | tf_op jit(solution)/shard_map/ppermute | solution.py:451
  22.5 7.5 %collective-permute-done = bf16[240,512]{1,0:T(8,128)(2,1)S(1)} collective-permute-done((bf16[240,512]{1,0:T(8,128)(2,1)}, bf16[240,512]{1,0:T(8,128)(2,1)S(1)}, u32[]{:S(2)}, u32[]{:S(2)}) %collective-permute-start) | collective-permute-done | bytes 245792 | tf_op jit(solution)/shard_map/ppermute | solution.py:451
  30.0 1.2 collective-permute-start.6
  31.9 1.0 fusion.65
  32.9 1.4 collective-permute-start.5
  35.6 1.2 add_bitcast_fusion.used_ref
  37.7 11.9 %collective-permute-done.8 = bf16[160,512]{1,0:T(8,128)(2,1)S(1)} collective-permute-done((bf16[160,512]{1,0:T(8,128)(2,1)S(1)}, bf16[160,512]{1,0:T(8,128)(2,1)S(1)}, u32[]{:S(2)}, u32[]{:S(2)}) %collective-permute-start.8) | collective-permute-done | bytes 163872 | tf_op jit(solution)/shard_map/ppermute | solution.py:451
  49.6 3.5 %collective-permute-done.5 = bf16[4,80,512]{2,1,0:T(8,128)(2,1)S(1)} collective-permute-done((bf16[4,80,512]{2,1,0:T(8,128)(2,1)S(1)}, bf16[4,80,512]{2,1,0:T(8,128)(2,1)S(1)}, u32[]{:S(2)}, u32[]{:S(2)}) %collective-permute-start.5) | collective-permute-done | bytes 327712 | tf_op jit(solution)/shard_map/ppermute | solution.py:451
  54.6 2.0 collective-permute-start.10
  56.7 1.4 collective-permute-start.11
  58.1 2.6 collective-permute-start.12
  61.6 11.5 %collective-permute-done.12 = bf16[160,512]{1,0:T(8,128)(2,1)S(1)} collective-permute-done((bf16[160,512]{1,0:T(8,128)(2,1)S(1)}, bf16[160,512]{1,0:T(8,128)(2,1)S(1)}, u32[]{:S(2)}, u32[]{:S(2)}) %collective-permute-start.12) | collective-permute-done | bytes 163872 | tf_op jit(solution)/shard_map/ppermute | solution.py:451
  74.7 1.9 collective-permute-start.16
  77.1 3.2 %shard_map.332 = (bf16[512,512]{1,0:T(8,128)(2,1)}, bf16[512,512]{1,0:T(8,128)(2,1)}, bf16[512,512]{1,0:T(8,128)(2,1)}, bf16[512,512]{1,0:T(8,128)(2,1)}, f32[16,512]{1,0:T(8,128)}) custom-call(s32[32]{0:T(128)} %fusion.30.place_ref, bf16[16,80,512]{2,1,0:T(8,128)(2,1)} %bitcast.145, bf16[16,80,512]{2,1,0:T(8,128)(2,1)} %collective-permute-done.13.other_ref), custom_call_target="tpu_custom_call" | custom-call | flops 3000000000 | bytes 3000000 | tf_op jit(solution)/shard_map/pallas_call | solution.py:757
  80.4 1.6 collective-permute-start.14
  82.1 2.0 collective-permute-start.15
  84.1 14.2 %shard_map.333 = (bf16[5120,512]{1,0:T(8,128)(2,1)}, bf16[5120,512]{1,0:T(8,128)(2,1)}, bf16[5120,512]{1,0:T(8,128)(2,1)}, bf16[640,512]{1,0:T(8,128)(2,1)}, bf16[640,512]{1,0:T(8,128)(2,1)}) custom-call(bf16[640,512]{1,0:T(8,128)(2,1)} %input_ref.3, bf16[640,512]{1,0:T(8,128)(2,1)} %copy-done.21, bf16[640,512]{1,0:T(8,128)(2,1)} %copy-done.22, ...), custom_call_target="tpu_custom_call" | custom-call | flops 12199999488 | bytes 12200000 | tf_op jit(solution)/shard_map/pallas_call | solution.py:419
  98.3 1.1 pad_maximum_fusion.1.weight_ref
  99.5 1.3 collective-permute-start.17
  100.9 1.8 collective-permute-start.18
  102.9 4.4 %shard_map.334 = (bf16[5120,512]{1,0:T(8,128)(2,1)}, bf16[5120,512]{1,0:T(8,128)(2,1)}, bf16[5120,512]{1,0:T(8,128)(2,1)}) custom-call(bf16[640,512]{1,0:T(8,128)(2,1)} %copy-done.8, f32[16,512]{1,0:T(8,128)} %get-tuple-element.138.refs_7_.refs_1_.vectors_ref, ...), custom_call_target="tpu_custom_call", output_to_operand_aliasing={{0}: (4, {}), {1}: (5, {}), {2}: (6, {})} | custom-call | flops 2600000000 | bytes 2600000 | tf_op jit(solution)/shard_map/pallas_call | solution.py:419
  107.3 18.8 %shard_map.335 = (bf16[640,512]{1,0:T(8,128)(2,1)}, f32[640,128]{1,0:T(8,128)}) custom-call(s32[5,11]{1,0:T(8,128)} %pad_add_fusion.slots_ref, bf16[640,512]{1,0:T(8,128)(2,1)} %get-tuple-element.144.query_ref, bf16[5120,512]{1,0:T(8,128)(2,1)} %get-tuple-element.156.key_source, bf16[5120,512]{1,0:T(8,128)(2,1)} %get-tuple-element.157.value_source), custom_call_target="tpu_custom_call" | custom-call | flops 17999998976 | bytes 18000000 | tf_op jit(solution)/shard_map/pallas_call | solution.py:308
  128.5 1.0 collective-permute-done.22
  130.3 21.1 %shard_map.336 = (bf16[640,512]{1,0:T(8,128)(2,1)}, f32[640,512]{1,0:T(8,128)}, bf16[640,512]{1,0:T(8,128)(2,1)}, bf16[640,512]{1,0:T(8,128)(2,1)}, f32[16,512]{...) custom-call(s32[3,32]{1,0:T(4,128)} %pad_add_fusion.1.place_ref, ...), custom_call_target="tpu_custom_call" | custom-call | flops 28000000000 | bytes 28000000 | tf_op jit(solution)/shard_map/pallas_call | solution.py:757
  152.0 2.9 collective-permute-done.23
  154.9 1.9 fusion.1
  157.5 34.3 %shard_map.337 = (bf16[640,512]{1,0:T(8,128)(2,1)}, f32[1024,512]{1,0:T(8,128)}, f32[1024,128]{1,0:T(8,128)}, bf16[5,512,128]{2,1,0:T(8,128)(2,1)}, bf16[5,512,1...) custom-call(s32[5,11]{1,0:T(8,128)} %pad_add_fusion.slots_ref, ...), custom_call_target="tpu_custom_call" | custom-call | flops 32000000000 | bytes 32000000 | tf_op jit(solution)/shard_map/pallas_call | solution.py:327
  191.8 1.1 fusion.6
  192.9 2.2 collective-permute-start.27
  195.1 10.8 %collective-permute-done.27 = bf16[2,176,512]{2,1,0:T(8,128)(2,1)S(1)} collective-permute-done((bf16[2,176,512]{2,1,0:T(8,128)(2,1)S(1)}, bf16[2,176,512]{2,1,0:T(8,128)(2,1)S(1)}, u32[]{:S(2)}, u32[]{:S(2)}) %collective-permute-start.27) | collective-permute-done | bytes 360480 | tf_op jit(solution)/shard_map/ppermute | solution.py:451
  205.8 1.1 fusion.4
  207.2 6.5 %shard_map.338 = (bf16[8,64,512]{2,1,0:T(8,128)(2,1)}, bf16[8,64,512]{2,1,0:T(8,128)(2,1)}, bf16[8,64,512]{2,1,0:T(8,128)(2,1)}, bf16[8,64,512]{2,1,0:T(8,128)(2,1)}) custom-call(s32[32]{0:T(128)} %fusion.30.place_ref, f32[1024,512]{1,0:T(8,128)} %get-tuple-element.200.both_grads_ref, bf16[640,512]{1,0:T(8,128)(2,1)} %get-tuple-element.162.normed_ref, ...), custom_call_target="tpu_custom_call" | custom-call | flops 100000000 | bytes 100000 | tf_op jit(solution)/shard_map/pallas_call | solution.py:757
  213.7 5.2 %collective-permute-done.28 = bf16[2,176,512]{2,1,0:T(8,128)(2,1)S(1)} collective-permute-done((bf16[2,176,512]{2,1,0:T(8,128)(2,1)S(1)}, bf16[2,176,512]{2,1,0:T(8,128)(2,1)S(1)}, u32[]{:S(2)}, u32[]{:S(2)}) %collective-permute-start.28) | collective-permute-done | bytes 360480 | tf_op jit(solution)/shard_map/ppermute | solution.py:451
  219.2 1.2 fusion.3
  221.2 1.8 collective-permute-start.33
  223.7 1.6 convolution_add_fusion.local_ref
  225.3 20.5 %collective-permute-done.31 = bf16[2,176,512]{2,1,0:T(8,128)(2,1)S(1)} collective-permute-done((bf16[2,176,512]{2,1,0:T(8,128)(2,1)S(1)}, bf16[2,176,512]{2,1,0:T(8,128)(2,1)S(1)}, u32[]{:S(2)}, u32[]{:S(2)}) %collective-permute-start.31) | collective-permute-done | bytes 360480 | tf_op jit(solution)/shard_map/ppermute | solution.py:451
  245.9 2.1 collective-permute-start.34
  248.7 1.2 fusion.2
  249.9 18.3 %collective-permute-done.37 = bf16[4,64,512]{2,1,0:T(8,128)(2,1)S(1)} collective-permute-done((bf16[4,64,512]{2,1,0:T(8,128)(2,1)S(1)}, bf16[4,64,512]{2,1,0:T(8,128)(2,1)S(1)}, u32[]{:S(2)}, u32[]{:S(2)}) %collective-permute-start.37) | collective-permute-done | bytes 262176 | tf_op jit(solution)/shard_map/ppermute | solution.py:451
  268.2 1.8 collective-permute-start.38
  270.3 1.9 collective-permute-start.40
  272.5 1.6 collective-permute-start.39
  274.1 2.7 collective-permute-done.42
  276.7 14.3 %collective-permute-done.41 = bf16[64,512]{1,0:T(8,128)(2,1)S(1)} collective-permute-done((bf16[64,512]{1,0:T(8,128)(2,1)S(1)}, bf16[64,512]{1,0:T(8,128)(2,1)S(1)}, u32[]{:S(2)}, u32[]{:S(2)}) %collective-permute-start.41) | collective-permute-done | bytes 65568 | tf_op jit(solution)/shard_map/ppermute | solution.py:451
  299.5 4.7 %shard_map.339 = f32[640,512]{1,0:T(8,128)} custom-call(bf16[640,512]{1,0:T(8,128)(2,1)} %input_ref.3, f32[640,512]{1,0:T(8,128)} %convolution_add_fusion.local_ref, f32[640,512]{1,0:T(8,128)} %get-tuple-element.193.middle_grad_ref, f32[16,512]{1,0:T(8,128)} %get-tuple-element.138.refs_7_.refs_1_.vectors_ref, bf16[5,512,128]{2,1,0:T(8,128)(2,1)} %copy-done.27, ...), custom_call_target="tpu_custom_call" | custom-call | flops 3000000000 | bytes 3000000 | tf_op jit(solution)/shard_map/pallas_call | solution.py:1158
  (241 shorter events, 38.6 us)
Async XLA Ops:
  2.6 19.9 %collective-permute-start.1 = (bf16[80,512]{1,0:T(8,128)(2,1)}, bf16[80,512]{1,0:T(8,128)(2,1)S(1)}, u32[]{:S(2)}, u32[]{:S(2)}) collective-permute-start(bf16[80,512]{1,0:T(8,128)(2,1)} %get-tuple-element.123), channel_id=1, source_target_pairs={{0,4},{1,5},{2,6},{3,7},{4,0},{5,1},{6,2},{7,3},{8,12},{9,13},{10,... | collective-permute-start | bytes 245768 | tf_op jit(solution)/shard_map/ppermute | solution.py:451
  2.9 19.6 %collective-permute-start.2 = (bf16[80,512]{1,0:T(8,128)(2,1)}, bf16[80,512]{1,0:T(8,128)(2,1)S(1)}, u32[]{:S(2)}, u32[]{:S(2)}) collective-permute-start(bf16[80,512]{1,0:T(8,128)(2,1)} %get-tuple-element.123), channel_id=1, source_target_pairs={{0,6},{1,7},{2,0},{3,1},{4,2},{5,3},{6,4},{7,5},{8,14},{9,15},{10,... | collective-permute-start | bytes 245768 | tf_op jit(solution)/shard_map/ppermute | solution.py:451
  3.4 26.6 %collective-permute-start.3 = (bf16[640,512]{1,0:T(8,128)(2,1)}, bf16[640,512]{1,0:T(8,128)(2,1)S(1)}, u32[]{:S(2)}, u32[]{:S(2)}) collective-permute-start(bf16[640,512]{1,0:T(8,128)(2,1)} %input_ref.3), channel_id=1, source_target_pairs={{0,1},{1,0},{2,3},{3,2},{4,5},{5,4},{6,7},{7,6},{8,9},{9,8},{10,11... | collective-permute-start | bytes 1966088 | tf_op jit(solution)/shard_map/ppermute | solution.py:451
  4.9 25.1 %collective-permute-start.4 = (bf16[640,512]{1,0:T(8,128)(2,1)}, bf16[640,512]{1,0:T(8,128)(2,1)S(1)}, u32[]{:S(2)}, u32[]{:S(2)}) collective-permute-start(bf16[640,512]{1,0:T(8,128)(2,1)} %input_ref.3), channel_id=1, source_target_pairs={{0,2},{1,3},{2,4},{3,5},{4,6},{5,7},{6,0},{7,1},{8,10},{9,11},{10,... | collective-permute-start | bytes 1966088 | tf_op jit(solution)/shard_map/ppermute | solution.py:451
  8.3 21.7 %collective-permute-start = (bf16[240,512]{1,0:T(8,128)(2,1)}, bf16[240,512]{1,0:T(8,128)(2,1)S(1)}, u32[]{:S(2)}, u32[]{:S(2)}) collective-permute-start(bf16[240,512]{1,0:T(8,128)(2,1)} %get-tuple-element.124), channel_id=1, source_target_pairs={{0,2},{1,3},{2,4},{3,5},{4,6},{5,7},{6,0},{7,1},{8,10},{9,11},{10,... | collective-permute-start | bytes 737288 | tf_op jit(solution)/shard_map/ppermute | solution.py:451
  30.0 24.1 %copy-start.22 = (bf16[640,512]{1,0:T(8,128)(2,1)}, bf16[640,512]{1,0:T(8,128)(2,1)S(1)}, u32[]{:S(2)}) copy-start(bf16[640,512]{1,0:T(8,128)(2,1)S(1)} %collective-permute-done.4.refs_2_) | copy-start | bytes 1966084
  30.0 23.1 %collective-permute-start.6 = (bf16[640,512]{1,0:T(8,128)(2,1)S(1)}, bf16[640,512]{1,0:T(8,128)(2,1)}, u32[]{:S(2)}, u32[]{:S(2)}) collective-permute-start(bf16[640,512]{1,0:T(8,128)(2,1)S(1)} %collective-permute-done.4.refs_2_), channel_id=1, source_target_pairs={{0,2},{1,3},{2,4},{3,5},{4,6},{5,7},{6,0},{7,1},{8,10},{9,11},{10,... | collective-permute-start | bytes 1966088 | tf_op jit(solution)/shard_map/ppermute | solution.py:451
  31.2 21.9 %collective-permute-start.7 = (bf16[640,512]{1,0:T(8,128)(2,1)S(1)}, bf16[640,512]{1,0:T(8,128)(2,1)S(1)}, u32[]{:S(2)}, u32[]{:S(2)}) collective-permute-start(bf16[640,512]{1,0:T(8,128)(2,1)S(1)} %collective-permute-done.4.refs_2_), channel_id=1, source_target_pairs={{0,1},{1,0},{2,3},{3,2},{4,5},{5,4},{6,7},{7,6},{8,9},{9,8},{10,11... | collective-permute-start | bytes 1966088 | tf_op jit(solution)/shard_map/ppermute | solution.py:451
  31.9 28.8 %copy-start.20 = (bf16[240,512]{1,0:T(8,128)(2,1)S(1)}, bf16[240,512]{1,0:T(8,128)(2,1)}, u32[]{:S(2)}) copy-start(bf16[240,512]{1,0:T(8,128)(2,1)} %get-tuple-element.124) | copy-start | bytes 737284
  32.9 20.2 %collective-permute-start.5 = (bf16[4,80,512]{2,1,0:T(8,128)(2,1)S(1)}, bf16[4,80,512]{2,1,0:T(8,128)(2,1)S(1)}, u32[]{:S(2)}, u32[]{:S(2)}) collective-permute-start(bf16[4,80,512]{2,1,0:T(8,128)(2,1)S(1)} %get-tuple-element.251), channel_id=1, source_target_pairs={{0,1},{1,0},{2,3},{3,2},{4,5},{5,4},{6,7},{7,6},{8,9},{9,8},{10,11... | collective-permute-start | bytes 983048 | tf_op jit(solution)/shard_map/ppermute | solution.py:451
  35.0 14.6 %collective-permute-start.8 = (bf16[160,512]{1,0:T(8,128)(2,1)S(1)}, bf16[160,512]{1,0:T(8,128)(2,1)S(1)}, u32[]{:S(2)}, u32[]{:S(2)}) collective-permute-start(bf16[160,512]{1,0:T(8,128)(2,1)S(1)} %slice.139), channel_id=1, source_target_pairs={{0,2},{1,3},{2,4},{3,5},{4,6},{5,7},{6,0},{7,1},{8,10},{9,11},{10,... | collective-permute-start | bytes 491528 | tf_op jit(solution)/shard_map/ppermute | solution.py:451
  54.1 19.0 %collective-permute-start.9 = (bf16[2,4,80,512]{3,2,1,0:T(8,128)(2,1)S(1)}, bf16[2,4,80,512]{3,2,1,0:T(8,128)(2,1)S(1)}, u32[]{:S(2)}, u32[]{:S(2)}) collective-permute-start(bf16[2,4,80,512]{3,2,1,0:T(8,128)(2,1)S(1)} %get-tuple-element.238), channel_id=1, source_target_pairs={{0,16},{8,24},{16,0},{24,8},{1,17},{9,25},{17,1},{25,9},{2,18},{10... | collective-permute-start | bytes 1966088 | tf_op jit(solution)/shard_map/ppermute | solution.py:451
  54.6 18.4 %collective-permute-start.10 = (bf16[640,512]{1,0:T(8,128)(2,1)}, bf16[640,512]{1,0:T(8,128)(2,1)}, u32[]{:S(2)}, u32[]{:S(2)}) collective-permute-start(bf16[640,512]{1,0:T(8,128)(2,1)} %collective-permute-done.6.refs_4_), channel_id=1, source_target_pairs={{0,2},{1,3},{2,4},{3,5},{4,6},{5,7},{6,0},{7,1},{8,10},{9,11},{10,... | collective-permute-start | bytes 1966088 | tf_op jit(solution)/shard_map/ppermute | solution.py:451
  56.7 16.4 %collective-permute-start.11 = (bf16[640,512]{1,0:T(8,128)(2,1)}, bf16[640,512]{1,0:T(8,128)(2,1)}, u32[]{:S(2)}, u32[]{:S(2)}) collective-permute-start(bf16[640,512]{1,0:T(8,128)(2,1)} %collective-permute-done.6.refs_4_), channel_id=1, source_target_pairs={{0,1},{1,0},{2,3},{3,2},{4,5},{5,4},{6,7},{7,6},{8,9},{9,8},{10,11... | collective-permute-start | bytes 1966088 | tf_op jit(solution)/shard_map/ppermute | solution.py:451
  58.1 15.0 %collective-permute-start.12 = (bf16[160,512]{1,0:T(8,128)(2,1)S(1)}, bf16[160,512]{1,0:T(8,128)(2,1)S(1)}, u32[]{:S(2)}, u32[]{:S(2)}) collective-permute-start(bf16[160,512]{1,0:T(8,128)(2,1)S(1)} %collective-permute-done.8), channel_id=1, source_target_pairs={{0,2},{1,3},{2,4},{3,5},{4,6},{5,7},{6,0},{7,1},{8,10},{9,11},{10,... | collective-permute-start | bytes 491528 | tf_op jit(solution)/shard_map/ppermute | solution.py:451
  73.9 3.2 %collective-permute-start.13 = (bf16[16,80,512]{2,1,0:T(8,128)(2,1)S(1)}, bf16[16,80,512]{2,1,0:T(8,128)(2,1)}, u32[]{:S(2)}, u32[]{:S(2)}) collective-permute-start(bf16[16,80,512]{2,1,0:T(8,128)(2,1)S(1)} %bitcast.144), channel_id=1, source_target_pairs={{0,8},{8,0},{16,24},{24,16},{1,9},{9,1},{17,25},{25,17},{2,10},{10... | collective-permute-start | bytes 3932168 | tf_op jit(solution)/shard_map/ppermute | solution.py:451
  74.7 24.7 %collective-permute-start.16 = (bf16[640,512]{1,0:T(8,128)(2,1)}, bf16[640,512]{1,0:T(8,128)(2,1)S(1)}, u32[]{:S(2)}, u32[]{:S(2)}) collective-permute-start(bf16[640,512]{1,0:T(8,128)(2,1)} %collective-permute-done.10.refs_6_), channel_id=1, source_target_pairs={{0,1},{1,0},{2,3},{3,2},{4,5},{5,4},{6,7},{7,6},{8,9},{9,8},{10,11... | collective-permute-start | bytes 1966088 | tf_op jit(solution)/shard_map/ppermute | solution.py:451
  80.4 19.0 %collective-permute-start.14 = (bf16[4,80,512]{2,1,0:T(8,128)(2,1)S(1)}, bf16[4,80,512]{2,1,0:T(8,128)(2,1)S(1)}, u32[]{:S(2)}, u32[]{:S(2)}) collective-permute-start(bf16[4,80,512]{2,1,0:T(8,128)(2,1)S(1)} %get-tuple-element.247), channel_id=1, source_target_pairs={{0,16},{8,24},{16,0},{24,8},{1,17},{9,25},{17,1},{25,9},{2,18},{10... | collective-permute-start | bytes 983048 | tf_op jit(solution)/shard_map/ppermute | solution.py:451
  82.1 17.4 %collective-permute-start.15 = (bf16[4,80,512]{2,1,0:T(8,128)(2,1)S(1)}, bf16[4,80,512]{2,1,0:T(8,128)(2,1)S(1)}, u32[]{:S(2)}, u32[]{:S(2)}) collective-permute-start(bf16[4,80,512]{2,1,0:T(8,128)(2,1)S(1)} %get-tuple-element.249), channel_id=1, source_target_pairs={{0,1},{1,0},{2,3},{3,2},{4,5},{5,4},{6,7},{7,6},{8,9},{9,8},{10,11... | collective-permute-start | bytes 983048 | tf_op jit(solution)/shard_map/ppermute | solution.py:451
  99.5 26.6 %collective-permute-start.17 = (bf16[2,4,80,512]{3,2,1,0:T(8,128)(2,1)S(1)}, bf16[2,4,80,512]{3,2,1,0:T(8,128)(2,1)S(1)}, u32[]{:S(2)}, u32[]{:S(2)}) collective-permute-start(bf16[2,4,80,512]{3,2,1,0:T(8,128)(2,1)S(1)} %pad_maximum_fusion.3), channel_id=1, source_target_pairs={{0,16},{8,24},{16,0},{24,8},{1,17},{9,25},{17,1},{25,9},{2,18},{10... | collective-permute-start | bytes 1966088 | tf_op jit(solution)/shard_map/ppermute | solution.py:451
  100.8 27.4 %collective-permute-start.19 = (bf16[2,4,80,512]{3,2,1,0:T(8,128)(2,1)S(1)}, bf16[2,4,80,512]{3,2,1,0:T(8,128)(2,1)}, u32[]{:S(2)}, u32[]{:S(2)}) collective-permute-start(bf16[2,4,80,512]{3,2,1,0:T(8,128)(2,1)S(1)} %pad_maximum_fusion.3), channel_id=1, source_target_pairs={{0,8},{8,0},{16,24},{24,16},{1,9},{9,1},{17,25},{25,17},{2,10},{10... | collective-permute-start | bytes 1966088 | tf_op jit(solution)/shard_map/ppermute | solution.py:451
  100.9 25.3 %collective-permute-start.18 = (bf16[2,4,80,512]{3,2,1,0:T(8,128)(2,1)S(1)}, bf16[2,4,80,512]{3,2,1,0:T(8,128)(2,1)}, u32[]{:S(2)}, u32[]{:S(2)}) collective-permute-start(bf16[2,4,80,512]{3,2,1,0:T(8,128)(2,1)S(1)} %pad_maximum_fusion.4), channel_id=1, source_target_pairs={{0,1},{1,0},{2,3},{3,2},{4,5},{5,4},{6,7},{7,6},{8,9},{9,8},{10,11... | collective-permute-start | bytes 1966088 | tf_op jit(solution)/shard_map/ppermute | solution.py:451
  102.7 25.5 %collective-permute-start.21 = (bf16[2,4,80,512]{3,2,1,0:T(8,128)(2,1)S(1)}, bf16[2,4,80,512]{3,2,1,0:T(8,128)(2,1)}, u32[]{:S(2)}, u32[]{:S(2)}) collective-permute-start(bf16[2,4,80,512]{3,2,1,0:T(8,128)(2,1)S(1)} %pad_maximum_fusion.4), channel_id=1, source_target_pairs={{0,8},{8,0},{16,24},{24,16},{1,9},{9,1},{17,25},{25,17},{2,10},{10... | collective-permute-start | bytes 1966088 | tf_op jit(solution)/shard_map/ppermute | solution.py:451
  126.1 2.3 collective-permute-start.20
  126.2 3.2 %collective-permute-start.22 = (bf16[2,4,80,512]{3,2,1,0:T(8,128)(2,1)}, bf16[2,4,80,512]{3,2,1,0:T(8,128)(2,1)S(1)}, u32[]{:S(2)}, u32[]{:S(2)}) collective-permute-start(bf16[2,4,80,512]{3,2,1,0:T(8,128)(2,1)} %collective-permute-done.18), channel_id=1, source_target_pairs={{0,8},{8,0},{16,24},{24,16},{1,9},{9,1},{17,25},{25,17},{2,10},{10... | collective-permute-start | bytes 1966088 | tf_op jit(solution)/shard_map/ppermute | solution.py:451
  151.5 3.4 %collective-permute-start.23 = (bf16[4,2,176,512]{3,2,1,0:T(8,128)(2,1)}, bf16[4,2,176,512]{3,2,1,0:T(8,128)(2,1)S(1)}, u32[]{:S(2)}, u32[]{:S(2)}) collective-permute-start(bf16[4,2,176,512]{3,2,1,0:T(8,128)(2,1)} %bitcast.168), channel_id=1, source_target_pairs={{0,8},{8,0},{16,24},{24,16},{1,9},{9,1},{17,25},{25,17},{2,10},{10... | collective-permute-start | bytes 4325384 | tf_op jit(solution)/shard_map/ppermute | solution.py:451
  151.6 5.4 %collective-permute-start.24 = (bf16[4,2,176,512]{3,2,1,0:T(8,128)(2,1)}, bf16[4,2,176,512]{3,2,1,0:T(8,128)(2,1)S(1)}, u32[]{:S(2)}, u32[]{:S(2)}) collective-permute-start(bf16[4,2,176,512]{3,2,1,0:T(8,128)(2,1)} %bitcast.167), channel_id=1, source_target_pairs={{0,8},{8,0},{16,24},{24,16},{1,9},{9,1},{17,25},{25,17},{2,10},{10... | collective-permute-start | bytes 4325384 | tf_op jit(solution)/shard_map/ppermute | solution.py:451
  157.4 34.4 %collective-permute-start.25 = (bf16[4,2,176,512]{3,2,1,0:T(8,128)(2,1)S(1)}, bf16[4,2,176,512]{3,2,1,0:T(8,128)(2,1)}, u32[]{:S(2)}, u32[]{:S(2)}) collective-permute-start(bf16[4,2,176,512]{3,2,1,0:T(8,128)(2,1)S(1)} %fusion), channel_id=1, source_target_pairs={{0,16},{8,24},{16,0},{24,8},{1,17},{9,25},{17,1},{25,9},{2,18},{10... | collective-permute-start | bytes 4325384 | tf_op jit(solution)/shard_map/ppermute | solution.py:451
  192.9 12.9 %collective-permute-start.27 = (bf16[2,176,512]{2,1,0:T(8,128)(2,1)S(1)}, bf16[2,176,512]{2,1,0:T(8,128)(2,1)S(1)}, u32[]{:S(2)}, u32[]{:S(2)}) collective-permute-start(bf16[2,176,512]{2,1,0:T(8,128)(2,1)S(1)} %fusion.6), channel_id=1, source_target_pairs={{0,6},{1,7},{2,0},{3,1},{4,2},{5,3},{6,4},{7,5},{8,14},{9,15},{10,... | collective-permute-start | bytes 1081352 | tf_op jit(solution)/shard_map/ppermute | solution.py:451
  195.1 18.6 %collective-permute-start.26 = (bf16[5,512,128]{2,1,0:T(8,128)(2,1)}, bf16[5,512,128]{2,1,0:T(8,128)(2,1)S(1)}, u32[]{:S(2)}, u32[]{:S(2)}) collective-permute-start(bf16[5,512,128]{2,1,0:T(8,128)(2,1)} %get-tuple-element.197), channel_id=1, source_target_pairs={{0,1},{1,0},{2,3},{3,2},{4,5},{5,4},{6,7},{7,6},{8,9},{9,8},{10,11... | collective-permute-start | bytes 1966088 | tf_op jit(solution)/shard_map/ppermute | solution.py:451
  207.0 11.9 %collective-permute-start.28 = (bf16[2,176,512]{2,1,0:T(8,128)(2,1)S(1)}, bf16[2,176,512]{2,1,0:T(8,128)(2,1)S(1)}, u32[]{:S(2)}, u32[]{:S(2)}) collective-permute-start(bf16[2,176,512]{2,1,0:T(8,128)(2,1)S(1)} %fusion.4), channel_id=1, source_target_pairs={{0,6},{1,7},{2,0},{3,1},{4,2},{5,3},{6,4},{7,5},{8,14},{9,15},{10,... | collective-permute-start | bytes 1081352 | tf_op jit(solution)/shard_map/ppermute | solution.py:451
  218.9 26.9 %collective-permute-start.29 = (bf16[5,512,128]{2,1,0:T(8,128)(2,1)}, bf16[5,512,128]{2,1,0:T(8,128)(2,1)S(1)}, u32[]{:S(2)}, u32[]{:S(2)}) collective-permute-start(bf16[5,512,128]{2,1,0:T(8,128)(2,1)} %get-tuple-element.208), channel_id=1, source_target_pairs={{0,1},{1,0},{2,3},{3,2},{4,5},{5,4},{6,7},{7,6},{8,9},{9,8},{10,11... | collective-permute-start | bytes 1966088 | tf_op jit(solution)/shard_map/ppermute | solution.py:451
  218.9 2.1 collective-permute-start.32
  219.1 26.7 %collective-permute-start.30 = (bf16[5,512,128]{2,1,0:T(8,128)(2,1)S(1)}, bf16[5,512,128]{2,1,0:T(8,128)(2,1)S(1)}, u32[]{:S(2)}, u32[]{:S(2)}) collective-permute-start(bf16[5,512,128]{2,1,0:T(8,128)(2,1)S(1)} %add_convert_fusion.2), channel_id=1, source_target_pairs={{0,6},{1,7},{2,0},{3,1},{4,2},{5,3},{6,4},{7,5},{8,14},{9,15},{10,... | collective-permute-start | bytes 1966088 | tf_op jit(solution)/shard_map/ppermute | solution.py:451
  220.4 25.4 %collective-permute-start.31 = (bf16[2,176,512]{2,1,0:T(8,128)(2,1)S(1)}, bf16[2,176,512]{2,1,0:T(8,128)(2,1)S(1)}, u32[]{:S(2)}, u32[]{:S(2)}) collective-permute-start(bf16[2,176,512]{2,1,0:T(8,128)(2,1)S(1)} %fusion.3), channel_id=1, source_target_pairs={{0,6},{1,7},{2,0},{3,1},{4,2},{5,3},{6,4},{7,5},{8,14},{9,15},{10,... | collective-permute-start | bytes 1081352 | tf_op jit(solution)/shard_map/ppermute | solution.py:451
  221.2 24.6 %collective-permute-start.33 = (bf16[2,4,64,512]{3,2,1,0:T(8,128)(2,1)S(1)}, bf16[2,4,64,512]{3,2,1,0:T(8,128)(2,1)S(1)}, u32[]{:S(2)}, u32[]{:S(2)}) collective-permute-start(bf16[2,4,64,512]{3,2,1,0:T(8,128)(2,1)S(1)} %add_convert_fusion.5), channel_id=1, source_target_pairs={{0,16},{8,24},{16,0},{24,8},{1,17},{9,25},{17,1},{25,9},{2,18},{10... | collective-permute-start | bytes 1572872 | tf_op jit(solution)/shard_map/ppermute | solution.py:451
  223.6 24.3 %copy-start.10 = (bf16[5,512,128]{2,1,0:T(8,128)(2,1)S(1)}, bf16[5,512,128]{2,1,0:T(8,128)(2,1)}, u32[]{:S(2)}) copy-start(bf16[5,512,128]{2,1,0:T(8,128)(2,1)} %get-tuple-element.215) | copy-start | bytes 1966084
  223.6 24.7 %collective-permute-start.36 = (bf16[2,4,64,512]{3,2,1,0:T(8,128)(2,1)S(1)}, bf16[2,4,64,512]{3,2,1,0:T(8,128)(2,1)S(1)}, u32[]{:S(2)}, u32[]{:S(2)}) collective-permute-start(bf16[2,4,64,512]{3,2,1,0:T(8,128)(2,1)S(1)} %bitcast.172), channel_id=1, source_target_pairs={{0,8},{8,0},{16,24},{24,16},{1,9},{9,1},{17,25},{25,17},{2,10},{10... | collective-permute-start | bytes 1572872 | tf_op jit(solution)/shard_map/ppermute | solution.py:451
  245.9 22.3 %collective-permute-start.34 = (bf16[5,512,128]{2,1,0:T(8,128)(2,1)S(1)}, bf16[5,512,128]{2,1,0:T(8,128)(2,1)S(1)}, u32[]{:S(2)}, u32[]{:S(2)}) collective-permute-start(bf16[5,512,128]{2,1,0:T(8,128)(2,1)S(1)} %copy-done.25), channel_id=1, source_target_pairs={{0,1},{1,0},{2,3},{3,2},{4,5},{5,4},{6,7},{7,6},{8,9},{9,8},{10,11... | collective-permute-start | bytes 1966088 | tf_op jit(solution)/shard_map/ppermute | solution.py:451
  248.2 20.0 %collective-permute-start.35 = (bf16[5,512,128]{2,1,0:T(8,128)(2,1)S(1)}, bf16[5,512,128]{2,1,0:T(8,128)(2,1)S(1)}, u32[]{:S(2)}, u32[]{:S(2)}) collective-permute-start(bf16[5,512,128]{2,1,0:T(8,128)(2,1)S(1)} %add_convert_fusion.1), channel_id=1, source_target_pairs={{0,6},{1,7},{2,0},{3,1},{4,2},{5,3},{6,4},{7,5},{8,14},{9,15},{10,... | collective-permute-start | bytes 1966088 | tf_op jit(solution)/shard_map/ppermute | solution.py:451
  248.6 23.6 %copy-start.9 = (bf16[5,512,128]{2,1,0:T(8,128)(2,1)S(1)}, bf16[5,512,128]{2,1,0:T(8,128)(2,1)}, u32[]{:S(2)}) copy-start(bf16[5,512,128]{2,1,0:T(8,128)(2,1)} %get-tuple-element.222) | copy-start | bytes 1966084
  248.6 19.6 %collective-permute-start.37 = (bf16[4,64,512]{2,1,0:T(8,128)(2,1)S(1)}, bf16[4,64,512]{2,1,0:T(8,128)(2,1)S(1)}, u32[]{:S(2)}, u32[]{:S(2)}) collective-permute-start(bf16[4,64,512]{2,1,0:T(8,128)(2,1)S(1)} %slice_bitcast_fusion.1), channel_id=1, source_target_pairs={{0,1},{1,0},{2,3},{3,2},{4,5},{5,4},{6,7},{7,6},{8,9},{9,8},{10,11... | collective-permute-start | bytes 786440 | tf_op jit(solution)/shard_map/ppermute | solution.py:451
  268.2 30.2 %collective-permute-start.38 = (bf16[5,512,128]{2,1,0:T(8,128)(2,1)S(1)}, bf16[5,512,128]{2,1,0:T(8,128)(2,1)S(1)}, u32[]{:S(2)}, u32[]{:S(2)}) collective-permute-start(bf16[5,512,128]{2,1,0:T(8,128)(2,1)S(1)} %copy-done.23), channel_id=1, source_target_pairs={{0,1},{1,0},{2,3},{3,2},{4,5},{5,4},{6,7},{7,6},{8,9},{9,8},{10,11... | collective-permute-start | bytes 1966088 | tf_op jit(solution)/shard_map/ppermute | solution.py:451
  270.1 6.6 %collective-permute-start.42 = (bf16[64,512]{1,0:T(8,128)(2,1)S(1)}, bf16[64,512]{1,0:T(8,128)(2,1)S(1)}, u32[]{:S(2)}, u32[]{:S(2)}) collective-permute-start(bf16[64,512]{1,0:T(8,128)(2,1)S(1)} %get-tuple-element.253), channel_id=1, source_target_pairs={{0,2},{1,3},{2,4},{3,5},{4,6},{5,7},{6,0},{7,1},{8,10},{9,11},{10,... | collective-permute-start | bytes 196616 | tf_op jit(solution)/shard_map/ppermute | solution.py:451
  270.2 20.8 %collective-permute-start.41 = (bf16[64,512]{1,0:T(8,128)(2,1)S(1)}, bf16[64,512]{1,0:T(8,128)(2,1)S(1)}, u32[]{:S(2)}, u32[]{:S(2)}) collective-permute-start(bf16[64,512]{1,0:T(8,128)(2,1)S(1)} %get-tuple-element.254), channel_id=1, source_target_pairs={{0,4},{1,5},{2,6},{3,7},{4,0},{5,1},{6,2},{7,3},{8,12},{9,13},{10,... | collective-permute-start | bytes 196616 | tf_op jit(solution)/shard_map/ppermute | solution.py:451
  270.3 20.7 %collective-permute-start.40 = (bf16[64,512]{1,0:T(8,128)(2,1)S(1)}, bf16[64,512]{1,0:T(8,128)(2,1)S(1)}, u32[]{:S(2)}, u32[]{:S(2)}) collective-permute-start(bf16[64,512]{1,0:T(8,128)(2,1)S(1)} %get-tuple-element.252), channel_id=1, source_target_pairs={{0,6},{1,7},{2,0},{3,1},{4,2},{5,3},{6,4},{7,5},{8,14},{9,15},{10,... | collective-permute-start | bytes 196616 | tf_op jit(solution)/shard_map/ppermute | solution.py:451
  272.5 26.0 %collective-permute-start.39 = (bf16[5,512,128]{2,1,0:T(8,128)(2,1)S(1)}, bf16[5,512,128]{2,1,0:T(8,128)(2,1)S(1)}, u32[]{:S(2)}, u32[]{:S(2)}) collective-permute-start(bf16[5,512,128]{2,1,0:T(8,128)(2,1)S(1)} %add_convert_fusion), channel_id=1, source_target_pairs={{0,6},{1,7},{2,0},{3,1},{4,2},{5,3},{6,4},{7,5},{8,14},{9,15},{10,... | collective-permute-start | bytes 1966088 | tf_op jit(solution)/shard_map/ppermute | solution.py:451
  276.7 19.7 %collective-permute-start.43 = (bf16[176,512]{1,0:T(8,128)(2,1)S(1)}, bf16[176,512]{1,0:T(8,128)(2,1)S(1)}, u32[]{:S(2)}, u32[]{:S(2)}) collective-permute-start(bf16[176,512]{1,0:T(8,128)(2,1)S(1)} %slice_bitcast_fusion.3), channel_id=1, source_target_pairs={{0,1},{1,0},{2,3},{3,2},{4,5},{5,4},{6,7},{7,6},{8,9},{9,8},{10,11... | collective-permute-start | bytes 540680 | tf_op jit(solution)/shard_map/ppermute | solution.py:451
  (28 other events, 212.0 us)

commit v2 on v1

--- a/solution.py
+++ b/solution.py
@@ -535,12 +535,13 @@
     all_ref[early_count - VECTOR_ROWS : early_count, :] = block.astype(jnp.bfloat16)
 
 
-def unpack_kernel(place_ref, mine_ref, other_ref, query_ref, key_ref, value_ref, gate_ref, vectors_ref):
-    half = mine_ref.shape[0]
-    rows = (mine_ref.shape[1] - VECTOR_ROWS) // 4
+def unpack_kernel(place_ref, *refs):
+    sources, (query_ref, key_ref, value_ref, gate_ref, vectors_ref) = refs[:4], refs[4:]
+    size = sources[0].shape[0]
+    rows = (sources[0].shape[1] - VECTOR_ROWS) // 4
     vectors = jnp.zeros(vectors_ref.shape, jnp.float32)
-    for index in range(2 * half):
-        source = (mine_ref if index < half else other_ref).at[index % half]
+    for index in range(len(sources) * size):
+        source = sources[index // size].at[index % size]
         target = pl.ds(pl.multiple_of(place_ref[index] * rows, rows), rows)
         for part, weight_ref in enumerate((query_ref, key_ref, value_ref, gate_ref)):
             weight_ref[target, :] = source[part * rows : (part + 1) * rows, :]
@@ -586,10 +587,11 @@
     *refs,
 ):
     late_refs, refs = refs[:8], refs[8:]
-    output_ref, middle_grad_ref, attended_grad_ref, gate_pre_ref, block_ref = refs[:5]
-    pack_refs = refs[5:9]
-    output_weight, up_weight, down_weight, carry_weight, hidden, up_pre_grads = refs[9:15]
-    update_grads, normed_second, carry_pre_grads, branch_grads, up_grad, down_grad, square_grads = refs[15:]
+    block_ref, row_targets, pack_targets, refs = refs[0], refs[1:5], refs[5:9], refs[9:]
+    output_weight, up_weight, down_weight, carry_weight, hidden, up_pre_grads = refs[:6]
+    update_grads, normed_second, carry_pre_grads, branch_grads, up_grad, down_grad, square_grads = refs[6:13]
+    row_refs, pack_refs, row_departures, pack_departures = refs[13:17], refs[17:21], refs[21], refs[22]
+    output_ref, middle_grad_ref, attended_grad_ref, gate_pre_ref = row_refs
     unpack_late(
         place_ref,
         late_refs[:4],
@@ -661,6 +663,19 @@
     for part in range(wide):
         block = jnp.where(line == UP_B + part, totals[5][:, part * width : (part + 1) * width], block)
     block_ref[...] = block
+    leaving = []
+
+    def leave(source, target, departure):
+        leaving.append(pltpu.make_async_copy(source, target, departure))
+        leaving[-1].start()
+
+    def packs_leave(group, start, stop):
+        for index, (source, target) in enumerate(zip(pack_refs, pack_targets)):
+            here = (slice(None), slice(start, stop), slice(None))
+            leave(source.at[here], target.at[here], pack_departures.at[group, index])
+
+    for index, (source, target) in enumerate(zip(row_refs, row_targets)):
+        leave(source, target, row_departures.at[index])
 
     target_ref = place_ref.at[2]
     rows = width // (4 * pack_refs[0].shape[0])
@@ -670,10 +685,12 @@
         grad[...] = inner_rows(normed_second[...], up_pre_grads[:, part * width : (part + 1) * width])
         spread_rows(target_ref, grad, pack_refs, place, rows)
         place += rows
+    packs_leave(0, 0, place)
     for part in range(wide):
         here = slice(part * width, (part + 1) * width)
         down_grad[here, :] = inner_rows(hidden[:, here], update_grads[...])
     spread_rows(target_ref, down_grad, pack_refs, place, wide * rows)
+    packs_leave(1, place, place + wide * rows)
     place += wide * rows
     pairs = ((normed_second, carry_pre_grads), (attended_ref, branch_grads), (normed_ref, gate_pre_ref))
     for index, (left_ref, right_ref) in enumerate(pairs):
@@ -681,6 +698,9 @@
         grad[...] = inner_rows(left_ref[...], right_ref[...])
         spread_rows(target_ref, grad, pack_refs, place, rows)
         place += rows
+    packs_leave(2, 2 * wide * rows, place)
+    for copy in leaving:
+        copy.wait()
 
 
 def second_grads_kernel(
@@ -869,8 +889,9 @@
             (early_other, z_three, x_two, late_line[3])
         )
         x_three = axis_x.rotate(z_three, 1)
-        early_all = jnp.stack([early_plane, early_other]).reshape(devices // 2, early_count, width)
-        early_other = axis_core.rotate(early_all, 1)
+        early_parts = [early_plane, early_other]
+        early_parts += [axis_core.rotate(part, 1) for part in early_parts]
+        early_parts = [part.reshape(devices // 4, early_count, width) for part in early_parts]
         input_pieces = [[inputs, x_zero], [z_one, x_one], [z_two, x_two], [z_three, x_three]]
         square = struct(width, width)
         full_query, full_key, full_value, full_gate, vector_rows = local_call(
@@ -878,7 +899,7 @@
             3,
             (square, square, square, square, struct(VECTOR_ROWS, width, dtype=jnp.float32)),
             places,
-            (early_all, early_other),
+            early_parts,
         )
         late_line, full_key = lax.optimization_barrier((late_line, full_key))
         late_half = late_count // 2
@@ -950,28 +971,15 @@
         hidden_width = up_weight.shape[1]
         quarter = struct(devices // 4, first_rows, width)
         tall, short = pltpu.VMEM((rows, hidden_width), low), pltpu.VMEM((rows, width), low)
-        output, middle_grad, attended_grad, gate_pre_grad, block, *first = local_call(
+        wide = (struct(rows, width), struct(rows, width, dtype=jnp.float32), struct(rows, width), struct(rows, width))
+        leaving = wide + (quarter,) * 4
+        block, output, middle_grad, attended_grad, gate_pre_grad, *first = pl.pallas_call(
             middle_kernel,
-            28,
-            (
-                struct(rows, width),
-                struct(rows, width, dtype=jnp.float32),
-                struct(rows, width),
-                struct(rows, width),
-                struct(VECTOR_ROWS, width, dtype=jnp.float32),
-            )
-            + (quarter,) * 4,
-            jnp.stack([places, other_places, targets]),
-            (
-                attended_low,
-                inputs,
-                normed_low,
-                cotangent,
-                full_gate,
-                vector_rows,
-            )
-            + tuple(late_parts),
-            (
+            cost_estimate=about(20),
+            out_shape=(struct(VECTOR_ROWS, width, dtype=jnp.float32),) + leaving,
+            in_specs=[in_smem()] + [in_vmem()] * 14,
+            out_specs=(in_vmem(),) + (anywhere(),) * len(leaving),
+            scratch_shapes=[
                 pltpu.VMEM((width, width), low),
                 pltpu.VMEM((width, hidden_width), low),
                 pltpu.VMEM((hidden_width, width), low),
@@ -985,7 +993,19 @@
                 pltpu.VMEM((hidden_width // width, width, width), jnp.float32),
                 pltpu.VMEM((hidden_width, width), jnp.float32),
                 pltpu.VMEM((3, width, width), jnp.float32),
-            ),
+            ]
+            + [pltpu.VMEM(out.shape, out.dtype) for out in leaving]
+            + [pltpu.SemaphoreType.DMA((4,)), pltpu.SemaphoreType.DMA((3, 4))],
+            compiler_params=pltpu.CompilerParams(vmem_limit_bytes=VMEM_BYTES),
+        )(
+            jnp.stack([places, other_places, targets]),
+            attended_low,
+            inputs,
+            normed_low,
+            cotangent,
+            full_gate,
+            vector_rows,
+            *late_parts,
         )
         first = [pack.reshape(4, 2, first_rows, width) for pack in first]
         first_core = [axis_core.rotate(first[2 + index], -1) for index in range(2)]

time: 308 us -> 303 us (0.984)
    pallas_call x4 -> x3, Pallas kernels: 32.8 us -> 11.5 us  [local_call(): pl.pallas_call(kernel, cost_estimate=about(cost), out_shape=outs, in_spec...]
    pallas_call x0 -> x1, Pallas kernels: none -> 20.6 us  [shards(): pl.pallas_call(middle_kernel, cost_estimate=about(20), out_shape=(struct(...]
    ppermute x44 -> x45, waiting for transfers between devices: 111 us -> 108 us  [rotate(): return lax.ppermute(values, self.name, pairs)]
    ppermute x44 -> x45, starting transfers between devices: 39.3 us -> 40.6 us  [rotate(): return lax.ppermute(values, self.name, pairs)]
  transfers between devices with their start and end apart: 44 -> 45, of which waited for: 16 -> 16; matrix products, arithmetic and copies ran while one was open for 12% -> 13% of each run, Pallas kernels for 27% -> 27%
where the time goes in v2:
time: 303 us; the launch traced here: 299 us
  Pallas kernels  108 us (36%)
  waiting for transfers between devices  108 us (36%)
  starting transfers between devices  40.6 us (13%)
  other arithmetic  26.1 us (9%)
  local copies, waits for them, and re-layouts  12.9 us (4%)
    ppermute x45, waiting for transfers between devices, rotate(): return lax.ppermute(values, self.name, pairs)  108 us
    ppermute x45, starting transfers between devices, rotate(): return lax.ppermute(values, self.name, pairs)  40.6 us
    pallas_call x1, Pallas kernels, attend_backward(): pl.pallas_call(backward_kernel, cost_estimate=about(32), out_shape=(jax.S...  34.7 us
    pallas_call x1, Pallas kernels, shards(): pl.pallas_call(middle_kernel, cost_estimate=about(20), out_shape=(struct(...  20.6 us
    pallas_call x2, Pallas kernels, project(): pl.pallas_call(body, cost_estimate=about(1 + 1.6 * count), out_shape=[who...  18.6 us
    pallas_call x1, Pallas kernels, attend(): pl.pallas_call(forward_kernel, cost_estimate=about(18), out_shape=(jax.Sh...  17.8 us
    pallas_call x3, Pallas kernels, local_call(): pl.pallas_call(kernel, cost_estimate=about(cost), out_shape=outs, in_spec...  11.5 us
    reduce_sum x10, other arithmetic, lookup(): jnp.sum(jnp.where(matches, lookup_table, jnp.int32(0)), axis=-1, dtype=jn...  7.79 us
  transfers between devices with their start and end apart: 45, of which 16 were waited for; matrix products, arithmetic and copies ran while one was open for 13% of the time, Pallas kernels for 27%

profile of v2, /device:TPU:28, one launch (start us, length us, event | category | flops | bytes accessed | tf_op | source)
XLA Modules:
  0.0 299.4 jit_solution(4307119723710697174)
XLA Ops:
  0.7 1.9 shard_map.331
  3.4 1.5 collective-permute-start.3
  4.9 3.4 %collective-permute-start.4 = (bf16[640,512]{1,0:T(8,128)(2,1)}, bf16[640,512]{1,0:T(8,128)(2,1)}, u32[]{:S(2)}, u32[]{:S(2)}) collective-permute-start(bf16[640,512]{1,0:T(8,128)(2,1)} %input_ref.3), channel_id=1, source_target_pairs={{0,2},{1,3},{2,4},{3,5},{4,6},{5,7},{6,0},{7,1},{8,10},{9,11},{10,... | collective-permute-start | bytes 1966088 | tf_op jit(solution)/shard_map/ppermute | solution.py:451
  23.2 6.8 %collective-permute-done = bf16[240,512]{1,0:T(8,128)(2,1)S(1)} collective-permute-done((bf16[240,512]{1,0:T(8,128)(2,1)}, bf16[240,512]{1,0:T(8,128)(2,1)S(1)}, u32[]{:S(2)}, u32[]{:S(2)}) %collective-permute-start) | collective-permute-done | bytes 245792 | tf_op jit(solution)/shard_map/ppermute | solution.py:451
  30.0 1.2 collective-permute-start.6
  32.8 1.4 collective-permute-start.5
  34.9 1.2 add_bitcast_fusion.used_ref
  37.3 12.6 %collective-permute-done.8 = bf16[160,512]{1,0:T(8,128)(2,1)S(1)} collective-permute-done((bf16[160,512]{1,0:T(8,128)(2,1)S(1)}, bf16[160,512]{1,0:T(8,128)(2,1)S(1)}, u32[]{:S(2)}, u32[]{:S(2)}) %collective-permute-start.8) | collective-permute-done | bytes 163872 | tf_op jit(solution)/shard_map/ppermute | solution.py:451
  49.8 3.5 %collective-permute-done.5 = bf16[4,80,512]{2,1,0:T(8,128)(2,1)S(1)} collective-permute-done((bf16[4,80,512]{2,1,0:T(8,128)(2,1)S(1)}, bf16[4,80,512]{2,1,0:T(8,128)(2,1)S(1)}, u32[]{:S(2)}, u32[]{:S(2)}) %collective-permute-start.5) | collective-permute-done | bytes 327712 | tf_op jit(solution)/shard_map/ppermute | solution.py:451
  53.3 2.0 collective-permute-start.10
  55.3 1.4 collective-permute-start.11
  57.5 2.6 collective-permute-start.12
  60.8 11.3 %collective-permute-done.12 = bf16[160,512]{1,0:T(8,128)(2,1)S(1)} collective-permute-done((bf16[160,512]{1,0:T(8,128)(2,1)S(1)}, bf16[160,512]{1,0:T(8,128)(2,1)S(1)}, u32[]{:S(2)}, u32[]{:S(2)}) %collective-permute-start.12) | collective-permute-done | bytes 163872 | tf_op jit(solution)/shard_map/ppermute | solution.py:451
  72.7 1.9 collective-permute-start.17
  75.5 3.1 %shard_map.332 = (bf16[512,512]{1,0:T(8,128)(2,1)}, bf16[512,512]{1,0:T(8,128)(2,1)}, bf16[512,512]{1,0:T(8,128)(2,1)}, bf16[512,512]{1,0:T(8,128)(2,1)}, f32[16,512]{1,0:T(8,128)}) custom-call(s32[32]{0:T(128)} %fusion.30.place_ref, bf16[8,80,512]{2,1,0:T(8,128)(2,1)} %bitcast.146, bf16[8,80,512]{2,1,0:T(8,128)(2,1)} %bitcast.30.refs_1_, ...), custom_call_target="tpu_custom_call" | custom-call | flops 3000000000 | bytes 3000000 | tf_op jit(solution)/shard_map/pallas_call | solution.py:777
  79.4 1.1 collective-permute-start.16
  80.4 14.2 %shard_map.333 = (bf16[5120,512]{1,0:T(8,128)(2,1)}, bf16[5120,512]{1,0:T(8,128)(2,1)}, bf16[5120,512]{1,0:T(8,128)(2,1)}, bf16[640,512]{1,0:T(8,128)(2,1)}, bf16[640,512]{1,0:T(8,128)(2,1)}) custom-call(bf16[640,512]{1,0:T(8,128)(2,1)} %input_ref.3, bf16[640,512]{1,0:T(8,128)(2,1)} %copy-done.17, bf16[640,512]{1,0:T(8,128)(2,1)} %collective-permute-done.4.refs_2_, ...), custom_call_target="tpu_custom_call" | custom-call | flops 12199999488 | bytes 12200000 | tf_op jit(solution)/shard_map/pallas_call | solution.py:419
  94.7 1.1 pad_maximum_fusion.weight_ref
  95.8 1.4 collective-permute-done.16
  98.0 1.8 collective-permute-start.19
  100.0 4.4 %shard_map.334 = (bf16[5120,512]{1,0:T(8,128)(2,1)}, bf16[5120,512]{1,0:T(8,128)(2,1)}, bf16[5120,512]{1,0:T(8,128)(2,1)}) custom-call(bf16[640,512]{1,0:T(8,128)(2,1)} %copy-done.7, f32[16,512]{1,0:T(8,128)} %get-tuple-element.138.refs_7_.refs_1_.vectors_ref, ...), custom_call_target="tpu_custom_call", output_to_operand_aliasing={{0}: (4, {}), {1}: (5, {}), {2}: (6, {})} | custom-call | flops 2600000000 | bytes 2600000 | tf_op jit(solution)/shard_map/pallas_call | solution.py:419
  104.4 17.8 %shard_map.335 = (bf16[640,512]{1,0:T(8,128)(2,1)}, f32[640,128]{1,0:T(8,128)}) custom-call(s32[5,11]{1,0:T(8,128)} %pad_add_fusion.slots_ref, bf16[640,512]{1,0:T(8,128)(2,1)} %get-tuple-element.144.query_ref, bf16[5120,512]{1,0:T(8,128)(2,1)} %get-tuple-element.156.key_source, bf16[5120,512]{1,0:T(8,128)(2,1)} %get-tuple-element.157.value_source), custom_call_target="tpu_custom_call" | custom-call | flops 17999998976 | bytes 18000000 | tf_op jit(solution)/shard_map/pallas_call | solution.py:308
  125.5 20.6 %shard_map.336 = (f32[16,512]{1,0:T(8,128)}, bf16[640,512]{1,0:T(8,128)(2,1)}, f32[640,512]{1,0:T(8,128)}, bf16[640,512]{1,0:T(8,128)(2,1)}, bf16[640,512]{1,0:T...) custom-call(s32[3,32]{1,0:T(4,128)} %pad_add_fusion.1.place_ref, ...), custom_call_target="tpu_custom_call" | custom-call | flops 20000000000 | bytes 20000000 | tf_op jit(solution)/shard_map/pallas_call | solution.py:976
  146.6 2.9 collective-permute-done.24
  149.6 1.9 fusion.1
  152.1 1.4 collective-permute-start.26
  153.5 34.7 %shard_map.337 = (bf16[640,512]{1,0:T(8,128)(2,1)}, f32[1024,512]{1,0:T(8,128)}, f32[1024,128]{1,0:T(8,128)}, bf16[5,512,128]{2,1,0:T(8,128)(2,1)}, bf16[5,512,1...) custom-call(s32[5,11]{1,0:T(8,128)} %pad_add_fusion.slots_ref, ...), custom_call_target="tpu_custom_call" | custom-call | flops 32000000000 | bytes 32000000 | tf_op jit(solution)/shard_map/pallas_call | solution.py:327
  188.2 1.1 fusion.6
  189.4 3.3 %collective-permute-start.27 = (bf16[5,512,128]{2,1,0:T(8,128)(2,1)}, bf16[5,512,128]{2,1,0:T(8,128)(2,1)S(1)}, u32[]{:S(2)}, u32[]{:S(2)}) collective-permute-start(bf16[5,512,128]{2,1,0:T(8,128)(2,1)} %get-tuple-element.197), channel_id=1, source_target_pairs={{0,1},{1,0},{2,3},{3,2},{4,5},{5,4},{6,7},{7,6},{8,9},{9,8},{10,11... | collective-permute-start | bytes 1966088 | tf_op jit(solution)/shard_map/ppermute | solution.py:451
  192.8 8.7 %collective-permute-done.28 = bf16[2,176,512]{2,1,0:T(8,128)(2,1)S(1)} collective-permute-done((bf16[2,176,512]{2,1,0:T(8,128)(2,1)S(1)}, bf16[2,176,512]{2,1,0:T(8,128)(2,1)S(1)}, u32[]{:S(2)}, u32[]{:S(2)}) %collective-permute-start.28) | collective-permute-done | bytes 360480 | tf_op jit(solution)/shard_map/ppermute | solution.py:451
  201.5 1.1 fusion.4
  202.7 6.5 %shard_map.338 = (bf16[8,64,512]{2,1,0:T(8,128)(2,1)}, bf16[8,64,512]{2,1,0:T(8,128)(2,1)}, bf16[8,64,512]{2,1,0:T(8,128)(2,1)}, bf16[8,64,512]{2,1,0:T(8,128)(2,1)}) custom-call(s32[32]{0:T(128)} %fusion.30.place_ref, f32[1024,512]{1,0:T(8,128)} %get-tuple-element.200.both_grads_ref, bf16[640,512]{1,0:T(8,128)(2,1)} %get-tuple-element.162.normed_ref, ...), custom_call_target="tpu_custom_call" | custom-call | flops 100000000 | bytes 100000 | tf_op jit(solution)/shard_map/pallas_call | solution.py:777
  209.2 4.7 %collective-permute-done.29 = bf16[2,176,512]{2,1,0:T(8,128)(2,1)S(1)} collective-permute-done((bf16[2,176,512]{2,1,0:T(8,128)(2,1)S(1)}, bf16[2,176,512]{2,1,0:T(8,128)(2,1)S(1)}, u32[]{:S(2)}, u32[]{:S(2)}) %collective-permute-start.29) | collective-permute-done | bytes 360480 | tf_op jit(solution)/shard_map/ppermute | solution.py:451
  213.9 1.1 collective-permute-start.30
  215.2 1.2 fusion.3
  217.3 1.9 collective-permute-start.34
  219.8 1.6 convolution_add_fusion.local_ref
  221.4 20.5 %collective-permute-done.32 = bf16[2,176,512]{2,1,0:T(8,128)(2,1)S(1)} collective-permute-done((bf16[2,176,512]{2,1,0:T(8,128)(2,1)S(1)}, bf16[2,176,512]{2,1,0:T(8,128)(2,1)S(1)}, u32[]{:S(2)}, u32[]{:S(2)}) %collective-permute-start.32) | collective-permute-done | bytes 360480 | tf_op jit(solution)/shard_map/ppermute | solution.py:451
  241.9 1.0 collective-permute-start.35
  243.6 1.1 collective-permute-start.38
  244.7 1.1 fusion.2
  245.9 18.1 %collective-permute-done.38 = bf16[4,64,512]{2,1,0:T(8,128)(2,1)S(1)} collective-permute-done((bf16[4,64,512]{2,1,0:T(8,128)(2,1)S(1)}, bf16[4,64,512]{2,1,0:T(8,128)(2,1)S(1)}, u32[]{:S(2)}, u32[]{:S(2)}) %collective-permute-start.38) | collective-permute-done | bytes 262176 | tf_op jit(solution)/shard_map/ppermute | solution.py:451
  265.3 1.9 collective-permute-start.41
  267.5 1.6 collective-permute-start.40
  269.0 2.7 collective-permute-done.43
  271.7 1.1 collective-permute-start.44
  272.8 13.2 %collective-permute-done.42 = bf16[64,512]{1,0:T(8,128)(2,1)S(1)} collective-permute-done((bf16[64,512]{1,0:T(8,128)(2,1)S(1)}, bf16[64,512]{1,0:T(8,128)(2,1)S(1)}, u32[]{:S(2)}, u32[]{:S(2)}) %collective-permute-start.42) | collective-permute-done | bytes 65568 | tf_op jit(solution)/shard_map/ppermute | solution.py:451
  294.5 4.7 %shard_map.339 = f32[640,512]{1,0:T(8,128)} custom-call(bf16[640,512]{1,0:T(8,128)(2,1)} %input_ref.3, f32[640,512]{1,0:T(8,128)} %convolution_add_fusion.local_ref, f32[640,512]{1,0:T(8,128)} %get-tuple-element.193.middle_grad_ref, f32[16,512]{1,0:T(8,128)} %get-tuple-element.138.refs_7_.refs_1_.vectors_ref, bf16[5,512,128]{2,1,0:T(8,128)(2,1)} %copy-done.20, ...), custom_call_target="tpu_custom_call" | custom-call | flops 3000000000 | bytes 3000000 | tf_op jit(solution)/shard_map/pallas_call | solution.py:1178
  (230 shorter events, 40.3 us)
Async XLA Ops:
  2.6 20.6 %collective-permute-start.1 = (bf16[80,512]{1,0:T(8,128)(2,1)}, bf16[80,512]{1,0:T(8,128)(2,1)S(1)}, u32[]{:S(2)}, u32[]{:S(2)}) collective-permute-start(bf16[80,512]{1,0:T(8,128)(2,1)} %get-tuple-element.123), channel_id=1, source_target_pairs={{0,4},{1,5},{2,6},{3,7},{4,0},{5,1},{6,2},{7,3},{8,12},{9,13},{10,... | collective-permute-start | bytes 245768 | tf_op jit(solution)/shard_map/ppermute | solution.py:451
  2.9 20.3 %collective-permute-start.2 = (bf16[80,512]{1,0:T(8,128)(2,1)}, bf16[80,512]{1,0:T(8,128)(2,1)S(1)}, u32[]{:S(2)}, u32[]{:S(2)}) collective-permute-start(bf16[80,512]{1,0:T(8,128)(2,1)} %get-tuple-element.123), channel_id=1, source_target_pairs={{0,6},{1,7},{2,0},{3,1},{4,2},{5,3},{6,4},{7,5},{8,14},{9,15},{10,... | collective-permute-start | bytes 245768 | tf_op jit(solution)/shard_map/ppermute | solution.py:451
  3.4 26.6 %collective-permute-start.3 = (bf16[640,512]{1,0:T(8,128)(2,1)}, bf16[640,512]{1,0:T(8,128)(2,1)S(1)}, u32[]{:S(2)}, u32[]{:S(2)}) collective-permute-start(bf16[640,512]{1,0:T(8,128)(2,1)} %input_ref.3), channel_id=1, source_target_pairs={{0,1},{1,0},{2,3},{3,2},{4,5},{5,4},{6,7},{7,6},{8,9},{9,8},{10,11... | collective-permute-start | bytes 1966088 | tf_op jit(solution)/shard_map/ppermute | solution.py:451
  4.9 25.1 %collective-permute-start.4 = (bf16[640,512]{1,0:T(8,128)(2,1)}, bf16[640,512]{1,0:T(8,128)(2,1)}, u32[]{:S(2)}, u32[]{:S(2)}) collective-permute-start(bf16[640,512]{1,0:T(8,128)(2,1)} %input_ref.3), channel_id=1, source_target_pairs={{0,2},{1,3},{2,4},{3,5},{4,6},{5,7},{6,0},{7,1},{8,10},{9,11},{10,... | collective-permute-start | bytes 1966088 | tf_op jit(solution)/shard_map/ppermute | solution.py:451
  8.3 21.7 %collective-permute-start = (bf16[240,512]{1,0:T(8,128)(2,1)}, bf16[240,512]{1,0:T(8,128)(2,1)S(1)}, u32[]{:S(2)}, u32[]{:S(2)}) collective-permute-start(bf16[240,512]{1,0:T(8,128)(2,1)} %get-tuple-element.124), channel_id=1, source_target_pairs={{0,2},{1,3},{2,4},{3,5},{4,6},{5,7},{6,0},{7,1},{8,10},{9,11},{10,... | collective-permute-start | bytes 737288 | tf_op jit(solution)/shard_map/ppermute | solution.py:451
  23.1 37.0 %copy-start.16 = (bf16[240,512]{1,0:T(8,128)(2,1)S(1)}, bf16[240,512]{1,0:T(8,128)(2,1)}, u32[]{:S(2)}) copy-start(bf16[240,512]{1,0:T(8,128)(2,1)} %get-tuple-element.124) | copy-start | bytes 737284
  30.0 30.1 %copy-start.17 = (bf16[640,512]{1,0:T(8,128)(2,1)}, bf16[640,512]{1,0:T(8,128)(2,1)S(1)}, u32[]{:S(2)}) copy-start(bf16[640,512]{1,0:T(8,128)(2,1)S(1)} %collective-permute-done.3.refs_1_) | copy-start | bytes 1966084
  30.0 23.3 %collective-permute-start.6 = (bf16[640,512]{1,0:T(8,128)(2,1)}, bf16[640,512]{1,0:T(8,128)(2,1)}, u32[]{:S(2)}, u32[]{:S(2)}) collective-permute-start(bf16[640,512]{1,0:T(8,128)(2,1)} %collective-permute-done.4.refs_2_), channel_id=1, source_target_pairs={{0,2},{1,3},{2,4},{3,5},{4,6},{5,7},{6,0},{7,1},{8,10},{9,11},{10,... | collective-permute-start | bytes 1966088 | tf_op jit(solution)/shard_map/ppermute | solution.py:451
  31.2 22.1 %collective-permute-start.7 = (bf16[640,512]{1,0:T(8,128)(2,1)}, bf16[640,512]{1,0:T(8,128)(2,1)}, u32[]{:S(2)}, u32[]{:S(2)}) collective-permute-start(bf16[640,512]{1,0:T(8,128)(2,1)} %collective-permute-done.4.refs_2_), channel_id=1, source_target_pairs={{0,1},{1,0},{2,3},{3,2},{4,5},{5,4},{6,7},{7,6},{8,9},{9,8},{10,11... | collective-permute-start | bytes 1966088 | tf_op jit(solution)/shard_map/ppermute | solution.py:451
  32.8 20.5 %collective-permute-start.5 = (bf16[4,80,512]{2,1,0:T(8,128)(2,1)S(1)}, bf16[4,80,512]{2,1,0:T(8,128)(2,1)S(1)}, u32[]{:S(2)}, u32[]{:S(2)}) collective-permute-start(bf16[4,80,512]{2,1,0:T(8,128)(2,1)S(1)} %get-tuple-element.249), channel_id=1, source_target_pairs={{0,1},{1,0},{2,3},{3,2},{4,5},{5,4},{6,7},{7,6},{8,9},{9,8},{10,11... | collective-permute-start | bytes 983048 | tf_op jit(solution)/shard_map/ppermute | solution.py:451
  34.3 15.5 %collective-permute-start.8 = (bf16[160,512]{1,0:T(8,128)(2,1)S(1)}, bf16[160,512]{1,0:T(8,128)(2,1)S(1)}, u32[]{:S(2)}, u32[]{:S(2)}) collective-permute-start(bf16[160,512]{1,0:T(8,128)(2,1)S(1)} %slice.139), channel_id=1, source_target_pairs={{0,2},{1,3},{2,4},{3,5},{4,6},{5,7},{6,0},{7,1},{8,10},{9,11},{10,... | collective-permute-start | bytes 491528 | tf_op jit(solution)/shard_map/ppermute | solution.py:451
  53.3 18.7 %collective-permute-start.10 = (bf16[640,512]{1,0:T(8,128)(2,1)}, bf16[640,512]{1,0:T(8,128)(2,1)}, u32[]{:S(2)}, u32[]{:S(2)}) collective-permute-start(bf16[640,512]{1,0:T(8,128)(2,1)} %collective-permute-done.6.refs_4_), channel_id=1, source_target_pairs={{0,2},{1,3},{2,4},{3,5},{4,6},{5,7},{6,0},{7,1},{8,10},{9,11},{10,... | collective-permute-start | bytes 1966088 | tf_op jit(solution)/shard_map/ppermute | solution.py:451
  55.3 16.7 %collective-permute-start.11 = (bf16[640,512]{1,0:T(8,128)(2,1)}, bf16[640,512]{1,0:T(8,128)(2,1)}, u32[]{:S(2)}, u32[]{:S(2)}) collective-permute-start(bf16[640,512]{1,0:T(8,128)(2,1)} %collective-permute-done.6.refs_4_), channel_id=1, source_target_pairs={{0,1},{1,0},{2,3},{3,2},{4,5},{5,4},{6,7},{7,6},{8,9},{9,8},{10,11... | collective-permute-start | bytes 1966088 | tf_op jit(solution)/shard_map/ppermute | solution.py:451
  56.9 15.2 %collective-permute-start.9 = (bf16[2,4,80,512]{3,2,1,0:T(8,128)(2,1)S(1)}, bf16[2,4,80,512]{3,2,1,0:T(8,128)(2,1)}, u32[]{:S(2)}, u32[]{:S(2)}) collective-permute-start(bf16[2,4,80,512]{3,2,1,0:T(8,128)(2,1)S(1)} %pad_maximum_fusion.1), channel_id=1, source_target_pairs={{0,16},{8,24},{16,0},{24,8},{1,17},{9,25},{17,1},{25,9},{2,18},{10... | collective-permute-start | bytes 1966088 | tf_op jit(solution)/shard_map/ppermute | solution.py:451
  57.5 14.6 %collective-permute-start.12 = (bf16[160,512]{1,0:T(8,128)(2,1)S(1)}, bf16[160,512]{1,0:T(8,128)(2,1)S(1)}, u32[]{:S(2)}, u32[]{:S(2)}) collective-permute-start(bf16[160,512]{1,0:T(8,128)(2,1)S(1)} %collective-permute-done.8), channel_id=1, source_target_pairs={{0,2},{1,3},{2,4},{3,5},{4,6},{5,7},{6,0},{7,1},{8,10},{9,11},{10,... | collective-permute-start | bytes 491528 | tf_op jit(solution)/shard_map/ppermute | solution.py:451
  60.7 13.9 %collective-permute-start.13 = (bf16[2,4,80,512]{3,2,1,0:T(8,128)(2,1)S(1)}, bf16[2,4,80,512]{3,2,1,0:T(8,128)(2,1)S(1)}, u32[]{:S(2)}, u32[]{:S(2)}) collective-permute-start(bf16[2,4,80,512]{3,2,1,0:T(8,128)(2,1)S(1)} %pad_maximum_fusion.1), channel_id=1, source_target_pairs={{0,8},{8,0},{16,24},{24,16},{1,9},{9,1},{17,25},{25,17},{2,10},{10... | collective-permute-start | bytes 1966088 | tf_op jit(solution)/shard_map/ppermute | solution.py:451
  72.1 2.6 collective-permute-start.14
  72.7 23.1 %collective-permute-start.17 = (bf16[640,512]{1,0:T(8,128)(2,1)}, bf16[640,512]{1,0:T(8,128)(2,1)S(1)}, u32[]{:S(2)}, u32[]{:S(2)}) collective-permute-start(bf16[640,512]{1,0:T(8,128)(2,1)} %collective-permute-done.10.refs_6_), channel_id=1, source_target_pairs={{0,1},{1,0},{2,3},{3,2},{4,5},{5,4},{6,7},{7,6},{8,9},{9,8},{10,11... | collective-permute-start | bytes 1966088 | tf_op jit(solution)/shard_map/ppermute | solution.py:451
  78.7 17.1 %collective-permute-start.15 = (bf16[4,80,512]{2,1,0:T(8,128)(2,1)S(1)}, bf16[4,80,512]{2,1,0:T(8,128)(2,1)S(1)}, u32[]{:S(2)}, u32[]{:S(2)}) collective-permute-start(bf16[4,80,512]{2,1,0:T(8,128)(2,1)S(1)} %get-tuple-element.245), channel_id=1, source_target_pairs={{0,16},{8,24},{16,0},{24,8},{1,17},{9,25},{17,1},{25,9},{2,18},{10... | collective-permute-start | bytes 983048 | tf_op jit(solution)/shard_map/ppermute | solution.py:451
  79.4 17.9 %collective-permute-start.16 = (bf16[4,80,512]{2,1,0:T(8,128)(2,1)S(1)}, bf16[4,80,512]{2,1,0:T(8,128)(2,1)S(1)}, u32[]{:S(2)}, u32[]{:S(2)}) collective-permute-start(bf16[4,80,512]{2,1,0:T(8,128)(2,1)S(1)} %get-tuple-element.247), channel_id=1, source_target_pairs={{0,1},{1,0},{2,3},{3,2},{4,5},{5,4},{6,7},{7,6},{8,9},{9,8},{10,11... | collective-permute-start | bytes 983048 | tf_op jit(solution)/shard_map/ppermute | solution.py:451
  97.3 24.9 %collective-permute-start.18 = (bf16[2,4,80,512]{3,2,1,0:T(8,128)(2,1)S(1)}, bf16[2,4,80,512]{3,2,1,0:T(8,128)(2,1)}, u32[]{:S(2)}, u32[]{:S(2)}) collective-permute-start(bf16[2,4,80,512]{3,2,1,0:T(8,128)(2,1)S(1)} %pad_maximum_fusion.2), channel_id=1, source_target_pairs={{0,16},{8,24},{16,0},{24,8},{1,17},{9,25},{17,1},{25,9},{2,18},{10... | collective-permute-start | bytes 1966088 | tf_op jit(solution)/shard_map/ppermute | solution.py:451
  97.9 26.5 %collective-permute-start.20 = (bf16[2,4,80,512]{3,2,1,0:T(8,128)(2,1)S(1)}, bf16[2,4,80,512]{3,2,1,0:T(8,128)(2,1)}, u32[]{:S(2)}, u32[]{:S(2)}) collective-permute-start(bf16[2,4,80,512]{3,2,1,0:T(8,128)(2,1)S(1)} %pad_maximum_fusion.2), channel_id=1, source_target_pairs={{0,8},{8,0},{16,24},{24,16},{1,9},{9,1},{17,25},{25,17},{2,10},{10... | collective-permute-start | bytes 1966088 | tf_op jit(solution)/shard_map/ppermute | solution.py:451
  98.0 24.3 %collective-permute-start.19 = (bf16[2,4,80,512]{3,2,1,0:T(8,128)(2,1)S(1)}, bf16[2,4,80,512]{3,2,1,0:T(8,128)(2,1)S(1)}, u32[]{:S(2)}, u32[]{:S(2)}) collective-permute-start(bf16[2,4,80,512]{3,2,1,0:T(8,128)(2,1)S(1)} %pad_maximum_fusion.3), channel_id=1, source_target_pairs={{0,1},{1,0},{2,3},{3,2},{4,5},{5,4},{6,7},{7,6},{8,9},{9,8},{10,11... | collective-permute-start | bytes 1966088 | tf_op jit(solution)/shard_map/ppermute | solution.py:451
  99.8 24.6 %collective-permute-start.22 = (bf16[2,4,80,512]{3,2,1,0:T(8,128)(2,1)S(1)}, bf16[2,4,80,512]{3,2,1,0:T(8,128)(2,1)}, u32[]{:S(2)}, u32[]{:S(2)}) collective-permute-start(bf16[2,4,80,512]{3,2,1,0:T(8,128)(2,1)S(1)} %pad_maximum_fusion.3), channel_id=1, source_target_pairs={{0,8},{8,0},{16,24},{24,16},{1,9},{9,1},{17,25},{25,17},{2,10},{10... | collective-permute-start | bytes 1966088 | tf_op jit(solution)/shard_map/ppermute | solution.py:451
  122.3 2.4 collective-permute-start.21
  122.4 3.1 %collective-permute-start.23 = (bf16[2,4,80,512]{3,2,1,0:T(8,128)(2,1)S(1)}, bf16[2,4,80,512]{3,2,1,0:T(8,128)(2,1)}, u32[]{:S(2)}, u32[]{:S(2)}) collective-permute-start(bf16[2,4,80,512]{3,2,1,0:T(8,128)(2,1)S(1)} %collective-permute-done.19), channel_id=1, source_target_pairs={{0,8},{8,0},{16,24},{24,16},{1,9},{9,1},{17,25},{25,17},{2,10},{10... | collective-permute-start | bytes 1966088 | tf_op jit(solution)/shard_map/ppermute | solution.py:451
  146.1 3.5 %collective-permute-start.24 = (bf16[4,2,176,512]{3,2,1,0:T(8,128)(2,1)}, bf16[4,2,176,512]{3,2,1,0:T(8,128)(2,1)S(1)}, u32[]{:S(2)}, u32[]{:S(2)}) collective-permute-start(bf16[4,2,176,512]{3,2,1,0:T(8,128)(2,1)} %bitcast.166), channel_id=1, source_target_pairs={{0,8},{8,0},{16,24},{24,16},{1,9},{9,1},{17,25},{25,17},{2,10},{10... | collective-permute-start | bytes 4325384 | tf_op jit(solution)/shard_map/ppermute | solution.py:451
  146.3 5.3 %collective-permute-start.25 = (bf16[4,2,176,512]{3,2,1,0:T(8,128)(2,1)}, bf16[4,2,176,512]{3,2,1,0:T(8,128)(2,1)S(1)}, u32[]{:S(2)}, u32[]{:S(2)}) collective-permute-start(bf16[4,2,176,512]{3,2,1,0:T(8,128)(2,1)} %bitcast.165), channel_id=1, source_target_pairs={{0,8},{8,0},{16,24},{24,16},{1,9},{9,1},{17,25},{25,17},{2,10},{10... | collective-permute-start | bytes 4325384 | tf_op jit(solution)/shard_map/ppermute | solution.py:451
  152.1 36.2 %collective-permute-start.26 = (bf16[4,2,176,512]{3,2,1,0:T(8,128)(2,1)S(1)}, bf16[4,2,176,512]{3,2,1,0:T(8,128)(2,1)}, u32[]{:S(2)}, u32[]{:S(2)}) collective-permute-start(bf16[4,2,176,512]{3,2,1,0:T(8,128)(2,1)S(1)} %fusion), channel_id=1, source_target_pairs={{0,16},{8,24},{16,0},{24,8},{1,17},{9,25},{17,1},{25,9},{2,18},{10... | collective-permute-start | bytes 4325384 | tf_op jit(solution)/shard_map/ppermute | solution.py:451
  189.3 12.2 %collective-permute-start.28 = (bf16[2,176,512]{2,1,0:T(8,128)(2,1)S(1)}, bf16[2,176,512]{2,1,0:T(8,128)(2,1)S(1)}, u32[]{:S(2)}, u32[]{:S(2)}) collective-permute-start(bf16[2,176,512]{2,1,0:T(8,128)(2,1)S(1)} %fusion.6), channel_id=1, source_target_pairs={{0,6},{1,7},{2,0},{3,1},{4,2},{5,3},{6,4},{7,5},{8,14},{9,15},{10,... | collective-permute-start | bytes 1081352 | tf_op jit(solution)/shard_map/ppermute | solution.py:451
  189.4 19.7 %collective-permute-start.27 = (bf16[5,512,128]{2,1,0:T(8,128)(2,1)}, bf16[5,512,128]{2,1,0:T(8,128)(2,1)S(1)}, u32[]{:S(2)}, u32[]{:S(2)}) collective-permute-start(bf16[5,512,128]{2,1,0:T(8,128)(2,1)} %get-tuple-element.197), channel_id=1, source_target_pairs={{0,1},{1,0},{2,3},{3,2},{4,5},{5,4},{6,7},{7,6},{8,9},{9,8},{10,11... | collective-permute-start | bytes 1966088 | tf_op jit(solution)/shard_map/ppermute | solution.py:451
  202.6 11.3 %collective-permute-start.29 = (bf16[2,176,512]{2,1,0:T(8,128)(2,1)S(1)}, bf16[2,176,512]{2,1,0:T(8,128)(2,1)S(1)}, u32[]{:S(2)}, u32[]{:S(2)}) collective-permute-start(bf16[2,176,512]{2,1,0:T(8,128)(2,1)S(1)} %fusion.4), channel_id=1, source_target_pairs={{0,6},{1,7},{2,0},{3,1},{4,2},{5,3},{6,4},{7,5},{8,14},{9,15},{10,... | collective-permute-start | bytes 1081352 | tf_op jit(solution)/shard_map/ppermute | solution.py:451
  213.9 28.0 %collective-permute-start.30 = (bf16[5,512,128]{2,1,0:T(8,128)(2,1)}, bf16[5,512,128]{2,1,0:T(8,128)(2,1)S(1)}, u32[]{:S(2)}, u32[]{:S(2)}) collective-permute-start(bf16[5,512,128]{2,1,0:T(8,128)(2,1)} %get-tuple-element.208), channel_id=1, source_target_pairs={{0,1},{1,0},{2,3},{3,2},{4,5},{5,4},{6,7},{7,6},{8,9},{9,8},{10,11... | collective-permute-start | bytes 1966088 | tf_op jit(solution)/shard_map/ppermute | solution.py:451
  215.0 2.1 collective-permute-start.33
  215.2 26.7 %collective-permute-start.31 = (bf16[5,512,128]{2,1,0:T(8,128)(2,1)S(1)}, bf16[5,512,128]{2,1,0:T(8,128)(2,1)S(1)}, u32[]{:S(2)}, u32[]{:S(2)}) collective-permute-start(bf16[5,512,128]{2,1,0:T(8,128)(2,1)S(1)} %add_convert_fusion.2), channel_id=1, source_target_pairs={{0,6},{1,7},{2,0},{3,1},{4,2},{5,3},{6,4},{7,5},{8,14},{9,15},{10,... | collective-permute-start | bytes 1966088 | tf_op jit(solution)/shard_map/ppermute | solution.py:451
  216.5 25.4 %collective-permute-start.32 = (bf16[2,176,512]{2,1,0:T(8,128)(2,1)S(1)}, bf16[2,176,512]{2,1,0:T(8,128)(2,1)S(1)}, u32[]{:S(2)}, u32[]{:S(2)}) collective-permute-start(bf16[2,176,512]{2,1,0:T(8,128)(2,1)S(1)} %fusion.3), channel_id=1, source_target_pairs={{0,6},{1,7},{2,0},{3,1},{4,2},{5,3},{6,4},{7,5},{8,14},{9,15},{10,... | collective-permute-start | bytes 1081352 | tf_op jit(solution)/shard_map/ppermute | solution.py:451
  217.3 24.6 %collective-permute-start.34 = (bf16[2,4,64,512]{3,2,1,0:T(8,128)(2,1)S(1)}, bf16[2,4,64,512]{3,2,1,0:T(8,128)(2,1)S(1)}, u32[]{:S(2)}, u32[]{:S(2)}) collective-permute-start(bf16[2,4,64,512]{3,2,1,0:T(8,128)(2,1)S(1)} %add_convert_fusion.5), channel_id=1, source_target_pairs={{0,16},{8,24},{16,0},{24,8},{1,17},{9,25},{17,1},{25,9},{2,18},{10... | collective-permute-start | bytes 1572872 | tf_op jit(solution)/shard_map/ppermute | solution.py:451
  219.7 23.6 %collective-permute-start.37 = (bf16[2,4,64,512]{3,2,1,0:T(8,128)(2,1)S(1)}, bf16[2,4,64,512]{3,2,1,0:T(8,128)(2,1)S(1)}, u32[]{:S(2)}, u32[]{:S(2)}) collective-permute-start(bf16[2,4,64,512]{3,2,1,0:T(8,128)(2,1)S(1)} %bitcast.170), channel_id=1, source_target_pairs={{0,8},{8,0},{16,24},{24,16},{1,9},{9,1},{17,25},{25,17},{2,10},{10... | collective-permute-start | bytes 1572872 | tf_op jit(solution)/shard_map/ppermute | solution.py:451
  241.9 22.0 %collective-permute-start.35 = (bf16[5,512,128]{2,1,0:T(8,128)(2,1)S(1)}, bf16[5,512,128]{2,1,0:T(8,128)(2,1)S(1)}, u32[]{:S(2)}, u32[]{:S(2)}) collective-permute-start(bf16[5,512,128]{2,1,0:T(8,128)(2,1)S(1)} %copy-done.19), channel_id=1, source_target_pairs={{0,1},{1,0},{2,3},{3,2},{4,5},{5,4},{6,7},{7,6},{8,9},{9,8},{10,11... | collective-permute-start | bytes 1966088 | tf_op jit(solution)/shard_map/ppermute | solution.py:451
  243.2 20.8 %collective-permute-start.36 = (bf16[5,512,128]{2,1,0:T(8,128)(2,1)S(1)}, bf16[5,512,128]{2,1,0:T(8,128)(2,1)S(1)}, u32[]{:S(2)}, u32[]{:S(2)}) collective-permute-start(bf16[5,512,128]{2,1,0:T(8,128)(2,1)S(1)} %add_convert_fusion.1), channel_id=1, source_target_pairs={{0,6},{1,7},{2,0},{3,1},{4,2},{5,3},{6,4},{7,5},{8,14},{9,15},{10,... | collective-permute-start | bytes 1966088 | tf_op jit(solution)/shard_map/ppermute | solution.py:451
  243.6 23.6 %copy-start.8 = (bf16[5,512,128]{2,1,0:T(8,128)(2,1)S(1)}, bf16[5,512,128]{2,1,0:T(8,128)(2,1)}, u32[]{:S(2)}) copy-start(bf16[5,512,128]{2,1,0:T(8,128)(2,1)} %get-tuple-element.222) | copy-start | bytes 1966084
  243.6 20.4 %collective-permute-start.38 = (bf16[4,64,512]{2,1,0:T(8,128)(2,1)S(1)}, bf16[4,64,512]{2,1,0:T(8,128)(2,1)S(1)}, u32[]{:S(2)}, u32[]{:S(2)}) collective-permute-start(bf16[4,64,512]{2,1,0:T(8,128)(2,1)S(1)} %slice_bitcast_fusion.1), channel_id=1, source_target_pairs={{0,1},{1,0},{2,3},{3,2},{4,5},{5,4},{6,7},{7,6},{8,9},{9,8},{10,11... | collective-permute-start | bytes 786440 | tf_op jit(solution)/shard_map/ppermute | solution.py:451
  264.0 29.4 %collective-permute-start.39 = (bf16[5,512,128]{2,1,0:T(8,128)(2,1)S(1)}, bf16[5,512,128]{2,1,0:T(8,128)(2,1)S(1)}, u32[]{:S(2)}, u32[]{:S(2)}) collective-permute-start(bf16[5,512,128]{2,1,0:T(8,128)(2,1)S(1)} %copy-done.18), channel_id=1, source_target_pairs={{0,1},{1,0},{2,3},{3,2},{4,5},{5,4},{6,7},{7,6},{8,9},{9,8},{10,11... | collective-permute-start | bytes 1966088 | tf_op jit(solution)/shard_map/ppermute | solution.py:451
  265.1 6.6 %collective-permute-start.43 = (bf16[64,512]{1,0:T(8,128)(2,1)S(1)}, bf16[64,512]{1,0:T(8,128)(2,1)S(1)}, u32[]{:S(2)}, u32[]{:S(2)}) collective-permute-start(bf16[64,512]{1,0:T(8,128)(2,1)S(1)} %get-tuple-element.251), channel_id=1, source_target_pairs={{0,2},{1,3},{2,4},{3,5},{4,6},{5,7},{6,0},{7,1},{8,10},{9,11},{10,... | collective-permute-start | bytes 196616 | tf_op jit(solution)/shard_map/ppermute | solution.py:451
  265.2 20.8 %collective-permute-start.42 = (bf16[64,512]{1,0:T(8,128)(2,1)S(1)}, bf16[64,512]{1,0:T(8,128)(2,1)S(1)}, u32[]{:S(2)}, u32[]{:S(2)}) collective-permute-start(bf16[64,512]{1,0:T(8,128)(2,1)S(1)} %get-tuple-element.252), channel_id=1, source_target_pairs={{0,4},{1,5},{2,6},{3,7},{4,0},{5,1},{6,2},{7,3},{8,12},{9,13},{10,... | collective-permute-start | bytes 196616 | tf_op jit(solution)/shard_map/ppermute | solution.py:451
  265.3 20.7 %collective-permute-start.41 = (bf16[64,512]{1,0:T(8,128)(2,1)S(1)}, bf16[64,512]{1,0:T(8,128)(2,1)S(1)}, u32[]{:S(2)}, u32[]{:S(2)}) collective-permute-start(bf16[64,512]{1,0:T(8,128)(2,1)S(1)} %get-tuple-element.250), channel_id=1, source_target_pairs={{0,6},{1,7},{2,0},{3,1},{4,2},{5,3},{6,4},{7,5},{8,14},{9,15},{10,... | collective-permute-start | bytes 196616 | tf_op jit(solution)/shard_map/ppermute | solution.py:451
  267.5 26.0 %collective-permute-start.40 = (bf16[5,512,128]{2,1,0:T(8,128)(2,1)S(1)}, bf16[5,512,128]{2,1,0:T(8,128)(2,1)S(1)}, u32[]{:S(2)}, u32[]{:S(2)}) collective-permute-start(bf16[5,512,128]{2,1,0:T(8,128)(2,1)S(1)} %add_convert_fusion), channel_id=1, source_target_pairs={{0,6},{1,7},{2,0},{3,1},{4,2},{5,3},{6,4},{7,5},{8,14},{9,15},{10,... | collective-permute-start | bytes 1966088 | tf_op jit(solution)/shard_map/ppermute | solution.py:451
  271.7 19.7 %collective-permute-start.44 = (bf16[176,512]{1,0:T(8,128)(2,1)S(1)}, bf16[176,512]{1,0:T(8,128)(2,1)S(1)}, u32[]{:S(2)}, u32[]{:S(2)}) collective-permute-start(bf16[176,512]{1,0:T(8,128)(2,1)S(1)} %slice_bitcast_fusion.3), channel_id=1, source_target_pairs={{0,1},{1,0},{2,3},{3,2},{4,5},{5,4},{6,7},{7,6},{8,9},{9,8},{10,11... | collective-permute-start | bytes 540680 | tf_op jit(solution)/shard_map/ppermute | solution.py:451
  (23 other events, 191.7 us)

commit v3 on v2

--- a/solution.py
+++ b/solution.py
@@ -150,6 +150,41 @@
         return carry
 
     lax.fori_loop(0, count, one_slot, 0)
+
+
+def last_forward_kernel(
+    slots_ref,
+    query_ref,
+    piece_ref,
+    vectors_ref,
+    key_weight_ref,
+    value_weight_ref,
+    *refs,
+):
+    mixed_ref, logsum_ref = refs[3:5]
+    targets = refs[5:8]
+    key_here, value_here, bias_ref, arrivals, made, departures = refs[8:]
+    gain = vectors_ref[GAIN_ONE : GAIN_ONE + 1, :]
+    shift = vectors_ref[SHIFT_ONE : SHIFT_ONE + 1, :]
+    rows = piece_ref.shape[0]
+    first = targets[0].shape[0] - rows
+
+    def leave(kind):
+        return pltpu.make_async_copy(made.at[kind], targets[kind].at[first : first + rows, :], departures.at[kind])
+
+    normed = normalize(piece_ref[...].astype(jnp.float32), gain, shift).astype(jnp.bfloat16)
+    made[1] = matmul(normed, key_weight_ref[...]).astype(jnp.bfloat16)
+    leave(1).start()
+    made[2] = matmul(normed, value_weight_ref[...]).astype(jnp.bfloat16)
+    leave(2).start()
+    made[0] = normed
+    leave(0).start()
+    leave(1).wait()
+    leave(2).wait()
+    forward_kernel(
+        slots_ref, query_ref, targets[1], targets[2], mixed_ref, logsum_ref, key_here, value_here, bias_ref, arrivals
+    )
+    leave(0).wait()
 
 
 def backward_kernel(
@@ -317,6 +352,32 @@
         scratch_shapes=level_scratch(width) + [pltpu.SemaphoreType.DMA((2, 2, DEPTH))],
         compiler_params=pltpu.CompilerParams(vmem_limit_bytes=VMEM_BYTES),
     )(slots, query_rows, key_group, value_group)
+
+
+def project_and_attend(slots, query_rows, piece, vectors, key_weight, value_weight, carried):
+    rows, width = query_rows.shape
+    whole = jax.ShapeDtypeStruct(carried[0].shape, jnp.bfloat16)
+    return pl.pallas_call(
+        last_forward_kernel,
+        cost_estimate=about(20),
+        out_shape=(
+            jax.ShapeDtypeStruct((rows, width), jnp.bfloat16),
+            jax.ShapeDtypeStruct((rows, PAIR), jnp.float32),
+            whole,
+            whole,
+            whole,
+        ),
+        in_specs=[in_smem()] + [in_vmem()] * 5 + [anywhere()] * 3,
+        out_specs=(in_vmem(), in_vmem(), anywhere(), anywhere(), anywhere()),
+        scratch_shapes=level_scratch(width)
+        + [
+            pltpu.SemaphoreType.DMA((2, 2, DEPTH)),
+            pltpu.VMEM((3, rows, width), jnp.bfloat16),
+            pltpu.SemaphoreType.DMA((3,)),
+        ],
+        input_output_aliases={6: 2, 7: 3, 8: 4},
+        compiler_params=pltpu.CompilerParams(vmem_limit_bytes=VMEM_BYTES),
+    )(slots, query_rows, piece, vectors, key_weight, value_weight, *carried)
 
 
 def attend_backward(tables, query_rows, key_group, value_group, logsum, mixed, mixed_grad, normed_group, both_weight):
@@ -757,6 +818,30 @@
     for pack_ref in pack_refs:
         for index in range(pack_ref.shape[0]):
             pack_ref[index, 3 * rows :, :] = block
+
+
+def own_kernel(device_ref, arrived_ref, kept_ref, *refs):
+    second_refs, weight_refs, line_refs = refs[:4], refs[4:12], refs[12:]
+    width = arrived_ref.shape[1]
+    first = arrived_ref[...].astype(jnp.float32) + kept_ref[...].astype(jnp.float32)
+    second = sum(ref[...].astype(jnp.float32) for ref in second_refs)
+    start = 0
+    source = first
+    for index, ref in enumerate(weight_refs):
+        if index == 5:
+            start, source = 0, second
+        rows = ref.shape[0]
+        for column in range(0, ref.shape[1], width):
+            ref[:, column : column + width] = source[start : start + rows, :]
+            start += rows
+    lines = second[start:, :]
+    place = lax.broadcasted_iota(jnp.int32, lines.shape, 0)
+    for index, ref in enumerate(line_refs):
+        count = ref.shape[1]
+        offset = device_ref[0] * count
+        line = jnp.where(place == index + offset // width, lines, jnp.float32(0.0))
+        line = jnp.broadcast_to(jnp.sum(line, axis=0, keepdims=True), (8, width))
+        ref[...] = pltpu.roll(line, (width - offset % width) % width, 1)[:1, :count]
 
 
 def input_grad_kernel(input_ref, local_ref, middle_grad_ref, vectors_ref, *refs):
@@ -950,14 +1035,17 @@
         late_y = jnp.stack([late_y, late_y_other])
         late_x_other = axis_y.rotate(late_x, 1)
         late_y_other = axis_x.rotate(late_y, 1)
-        carried = project([x_three], vector_rows, full_key, full_value, group_rows, near, carried)
+        attended_low, logsum, *carried = project_and_attend(
+            slots, query_low, x_three, vector_rows, full_key, full_value, carried
+        )
     normed_group, key_group, value_group = carried
 
     gate_b, down_b, carry_b, gain_one, shift_one, gain_two, shift_two = [vector_rows[line] for line in range(UP_B)]
     up_b = vector_rows[UP_B : UP_B + up_weight.shape[1] // width].reshape(-1)
 
     values_in = inputs.astype(jnp.float32)
-    attended_low, logsum = attend(slots, query_low, key_group, value_group)
+    if not direct:
+        attended_low, logsum = attend(slots, query_low, key_group, value_group)
 
     if direct:
         attended_low, late_x_other, late_y_other = lax.optimization_barrier((attended_low, late_x_other, late_y_other))
@@ -1110,14 +1198,14 @@
         second_arrived = axis_y.rotate(add_low(second_core[1], second[1]), -1)
         x_two = axis_x.rotate(tied(shared_parts[5], x_three), -1)
         z_three = axis_z.rotate(add_low(x_three, shared_parts[6]), -1)
-        first_z = axis_z.rotate(add_low(first_z, first_y(1)), -1)
-        x_two, z_three, first_z, second_arrived = barrier((x_two, z_three, first_z, second_arrived))
+        x_two, z_three, second_arrived = barrier((x_two, z_three, second_arrived))
 
         second_y = add_low(second_arrived, second_keep)
         second_x = axis_x.rotate(second_y[1], -1)
         x_one = axis_x.rotate(tied(shared_parts[3], x_two), -1)
         z_two = axis_z.rotate(add_three(x_two, shared_parts[4], z_three), -1)
-        x_one, z_two, second_x = barrier((x_one, z_two, second_x))
+        first_z = axis_z.rotate(add_low(tied(first_z, x_two), first_y(1)), -1)
+        x_one, z_two, second_x, first_z = barrier((x_one, z_two, second_x, first_z))
 
         first_half = add_low(first_z, first_y(0))
         first_x = axis_x.rotate(tied(first_half[1], x_one), -1)
@@ -1126,9 +1214,6 @@
         x_zero = axis_x.rotate(tied(shared_parts[1], x_one), -1)
         z_one = axis_z.rotate(add_three(x_one, shared_parts[2], z_two), -1)
         shared = (x_zero, z_one, shared_parts[0])
-        first_sum = first_x.astype(jnp.float32) + first_half[0].astype(jnp.float32)
-        second_sum = sum(piece.astype(jnp.float32) for piece in [second_half[0]] + second_z)
-        weight_sum = jnp.concatenate([first_sum, second_sum])
     else:
         grad_key = jnp.transpose(both_grads[:width])
         grad_value = jnp.transpose(both_grads[width:])
@@ -1168,12 +1253,6 @@
 
         shared = (ring_scatter(over_x, axis_z),)
 
-    def own(start, piece):
-        rows = piece.shape[0]
-        parts = piece.shape[1] // width
-        blocks = [weight_sum[start + part * rows : start + (part + 1) * rows] for part in range(parts)]
-        return joined(blocks, 1), start + parts * rows
-
     local_grad = against(query_rows_grad, full_query) + against(gate_pre_grad, full_gate)
     input_grad = pl.pallas_call(
         input_grad_kernel,
@@ -1182,20 +1261,43 @@
         compiler_params=pltpu.CompilerParams(vmem_limit_bytes=VMEM_BYTES),
     )(inputs, local_grad, middle_grad, vector_rows, *shared)
 
-    place = 0
-    own_up, place = own(place, up_weight)
-    own_down, place = own(place, down_weight)
-    own_carry, place = own(place, carry_weight)
-    own_output, place = own(place, output_weight)
-    own_gate, place = own(place, gate_weight)
-    own_query, place = own(place, query_weight)
-    own_key, place = own(place, key_weight)
-    own_value, place = own(place, value_weight)
-    vector_out = []
-    for index, vector in enumerate(vectors):
-        count = vector.shape[0]
-        lines = weight_sum[place + index : place + index + count * devices // width].reshape(-1)
-        vector_out.append(lax.dynamic_slice_in_dim(lines, device * count, count))
+    if direct:
+        input_grad, first_x, second_z = lax.optimization_barrier((input_grad, first_x, second_z))
+        square = struct(rows_each, width, dtype=jnp.float32)
+        tall = struct(down_weight.shape[0], width, dtype=jnp.float32)
+        broad = struct(rows_each, up_weight.shape[1], dtype=jnp.float32)
+        weight_outs = (broad, tall, square, square, square, square, square, square)
+        line_outs = tuple(struct(1, vector.shape[0], dtype=jnp.float32) for vector in vectors)
+        own_grads = local_call(
+            own_kernel,
+            2,
+            weight_outs + line_outs,
+            device.reshape(1),
+            (first_x, first_half[0], second_half[0], *second_z),
+        )
+        own_up, own_down, own_carry, own_output, own_gate, own_query, own_key, own_value = own_grads[:8]
+        vector_out = [line.reshape(-1) for line in own_grads[8:]]
+    else:
+        def own(start, piece):
+            rows = piece.shape[0]
+            parts = piece.shape[1] // width
+            blocks = [weight_sum[start + part * rows : start + (part + 1) * rows] for part in range(parts)]
+            return joined(blocks, 1), start + parts * rows
+
+        place = 0
+        own_up, place = own(place, up_weight)
+        own_down, place = own(place, down_weight)
+        own_carry, place = own(place, carry_weight)
+        own_output, place = own(place, output_weight)
+        own_gate, place = own(place, gate_weight)
+        own_query, place = own(place, query_weight)
+        own_key, place = own(place, key_weight)
+        own_value, place = own(place, value_weight)
+        vector_out = []
+        for index, vector in enumerate(vectors):
+            count = vector.shape[0]
+            lines = weight_sum[place + index : place + index + count * devices // width].reshape(-1)
+            vector_out.append(lax.dynamic_slice_in_dim(lines, device * count, count))
     gate_bg, down_bg, carry_bg, gain_one_g, shift_one_g, gain_two_g, shift_two_g, up_bg = vector_out
     return (
         output,

time: 303 us -> 295 us (0.974)
  local copies, waits for them, and re-layouts: 12.9 us -> 7.5 us
    dynamic_slice x8 -> x0, local copies, waits for them, and re-layouts: 4.65 us -> none  [shards(): vector_out.append(lax.dynamic_slice_in_dim(lines, device * count, count))]
    pallas_call x2 -> x1, Pallas kernels: 18.6 us -> 14.2 us  [project(): pl.pallas_call(body, cost_estimate=about(1 + 1.6 * count), out_shape=[who...]
    pallas_call x3 -> x4, Pallas kernels: 11.5 us -> 13.6 us  [local_call(): pl.pallas_call(kernel, cost_estimate=about(cost), out_shape=outs, in_spec...]
  transfers between devices with their start and end apart: 45 -> 45, of which waited for: 16 -> 19; matrix products, arithmetic and copies ran while one was open for 13% -> 10% of each run, Pallas kernels for 27% -> 28%
where the time goes in v3:
time: 295 us; the launch traced here: 291 us
  waiting for transfers between devices  109 us (37%)
  Pallas kernels  107 us (36%)
  starting transfers between devices  38.1 us (13%)
  other arithmetic  25.3 us (9%)
  local copies, waits for them, and re-layouts  7.5 us (3%)
    ppermute x45, waiting for transfers between devices, rotate(): return lax.ppermute(values, self.name, pairs)  109 us
    ppermute x45, starting transfers between devices, rotate(): return lax.ppermute(values, self.name, pairs)  38.1 us
    pallas_call x1, Pallas kernels, attend_backward(): pl.pallas_call(backward_kernel, cost_estimate=about(32), out_shape=(jax.S...  33.6 us
    pallas_call x1, Pallas kernels, shards(): pl.pallas_call(middle_kernel, cost_estimate=about(20), out_shape=(struct(...  20.6 us
    pallas_call x1, Pallas kernels, project_and_attend(): pl.pallas_call(last_forward_kernel, cost_estimate=about(20), out_shape=(j...  20.3 us
    pallas_call x1, Pallas kernels, project(): pl.pallas_call(body, cost_estimate=about(1 + 1.6 * count), out_shape=[who...  14.2 us
    pallas_call x4, Pallas kernels, local_call(): pl.pallas_call(kernel, cost_estimate=about(cost), out_shape=outs, in_spec...  13.6 us
    reduce_sum x10, other arithmetic, lookup(): jnp.sum(jnp.where(matches, lookup_table, jnp.int32(0)), axis=-1, dtype=jn...  7.79 us
  transfers between devices with their start and end apart: 45, of which 19 were waited for; matrix products, arithmetic and copies ran while one was open for 10% of the time, Pallas kernels for 28%

profile of v3, /device:TPU:28, one launch (start us, length us, event | category | flops | bytes accessed | tf_op | source)
XLA Modules:
  0.0 291.2 jit_solution(16716654217368295363)
XLA Ops:
  0.7 2.0 shard_map.331
  3.4 3.0 %collective-permute-start.4 = (bf16[640,512]{1,0:T(8,128)(2,1)}, bf16[640,512]{1,0:T(8,128)(2,1)S(1)}, u32[]{:S(2)}, u32[]{:S(2)}) collective-permute-start(bf16[640,512]{1,0:T(8,128)(2,1)} %input_ref.3), channel_id=1, source_target_pairs={{0,2},{1,3},{2,4},{3,5},{4,6},{5,7},{6,0},{7,1},{8,10},{9,11},{10,... | collective-permute-start | bytes 1966088 | tf_op jit(solution)/shard_map/ppermute | solution.py:512
  6.5 1.5 collective-permute-start.3
  8.0 1.0 collective-permute-start
  23.3 5.9 %collective-permute-done = bf16[240,512]{1,0:T(8,128)(2,1)S(1)} collective-permute-done((bf16[240,512]{1,0:T(8,128)(2,1)}, bf16[240,512]{1,0:T(8,128)(2,1)S(1)}, u32[]{:S(2)}, u32[]{:S(2)}) %collective-permute-start) | collective-permute-done | bytes 245792 | tf_op jit(solution)/shard_map/ppermute | solution.py:512
  29.2 1.6 collective-permute-start.7
  30.7 2.6 collective-permute-start.6
  35.2 1.2 add_bitcast_fusion.used_ref
  37.5 12.9 %collective-permute-done.8 = bf16[160,512]{1,0:T(8,128)(2,1)S(1)} collective-permute-done((bf16[160,512]{1,0:T(8,128)(2,1)S(1)}, bf16[160,512]{1,0:T(8,128)(2,1)S(1)}, u32[]{:S(2)}, u32[]{:S(2)}) %collective-permute-start.8) | collective-permute-done | bytes 163872 | tf_op jit(solution)/shard_map/ppermute | solution.py:512
  50.4 2.1 collective-permute-done.5
  52.5 1.5 collective-permute-start.11
  54.0 2.7 collective-permute-start.10
  58.4 14.8 %collective-permute-done.12 = bf16[160,512]{1,0:T(8,128)(2,1)S(1)} collective-permute-done((bf16[160,512]{1,0:T(8,128)(2,1)S(1)}, bf16[160,512]{1,0:T(8,128)(2,1)S(1)}, u32[]{:S(2)}, u32[]{:S(2)}) %collective-permute-start.12) | collective-permute-done | bytes 163872 | tf_op jit(solution)/shard_map/ppermute | solution.py:512
  74.3 1.3 collective-permute-done.14
  75.6 3.1 %shard_map.332 = (bf16[512,512]{1,0:T(8,128)(2,1)}, bf16[512,512]{1,0:T(8,128)(2,1)}, bf16[512,512]{1,0:T(8,128)(2,1)}, bf16[512,512]{1,0:T(8,128)(2,1)}, f32[16,512]{1,0:T(8,128)}) custom-call(s32[32]{0:T(128)} %fusion.28.place_ref, bf16[8,80,512]{2,1,0:T(8,128)(2,1)} %bitcast.131, bf16[8,80,512]{2,1,0:T(8,128)(2,1)} %bitcast.30.refs_1_, ...), custom_call_target="tpu_custom_call" | custom-call | flops 3000000000 | bytes 3000000 | tf_op jit(solution)/shard_map/pallas_call | solution.py:862
  78.9 1.1 collective-permute-start.16
  80.6 14.2 %shard_map.333 = (bf16[5120,512]{1,0:T(8,128)(2,1)}, bf16[5120,512]{1,0:T(8,128)(2,1)}, bf16[5120,512]{1,0:T(8,128)(2,1)}, bf16[640,512]{1,0:T(8,128)(2,1)}, bf16[640,512]{1,0:T(8,128)(2,1)}) custom-call(bf16[640,512]{1,0:T(8,128)(2,1)} %input_ref.3, bf16[640,512]{1,0:T(8,128)(2,1)} %copy-done.17, bf16[640,512]{1,0:T(8,128)(2,1)} %copy-done.16, ...), custom_call_target="tpu_custom_call" | custom-call | flops 12199999488 | bytes 12200000 | tf_op jit(solution)/shard_map/pallas_call | solution.py:480
  94.8 1.1 pad_maximum_fusion.weight_ref
  96.0 2.1 collective-permute-done.16
  99.9 20.3 %shard_map.334 = (bf16[640,512]{1,0:T(8,128)(2,1)}, f32[640,128]{1,0:T(8,128)}, bf16[5120,512]{1,0:T(8,128)(2,1)}, bf16[5120,512]{1,0:T(8,128)(2,1)}, bf16[5120,512]{1,0:T(8,128)(2,1)}) custom-call(s32[5,11]{1,0:T(8,128)} %pad_add_fusion.slots_ref, ...), custom_call_target="tpu_custom_call", output_to_operand_aliasing={{2}: (6, {}), {3}: (7, {}), {4}: (8, {})} | custom-call | flops 20000000000 | bytes 20000000 | tf_op jit(solution)/shard_map/pallas_call | solution.py:360
  124.2 20.6 %shard_map.335 = (f32[16,512]{1,0:T(8,128)}, bf16[640,512]{1,0:T(8,128)(2,1)}, f32[640,512]{1,0:T(8,128)}, bf16[640,512]{1,0:T(8,128)(2,1)}, bf16[640,512]{1,0:T...) custom-call(s32[3,32]{1,0:T(4,128)} %pad_add_fusion.1.place_ref, ...), custom_call_target="tpu_custom_call" | custom-call | flops 20000000000 | bytes 20000000 | tf_op jit(solution)/shard_map/pallas_call | solution.py:1064
  145.4 2.9 %collective-permute-done.24 = bf16[4,2,176,512]{3,2,1,0:T(8,128)(2,1)S(1)} collective-permute-done((bf16[4,2,176,512]{3,2,1,0:T(8,128)(2,1)}, bf16[4,2,176,512]{3,2,1,0:T(8,128)(2,1)S(1)}, u32[]{:S(2)}, u32[]{:S(2)}) %collective-permute-start.24) | collective-permute-done | bytes 1441824 | tf_op jit(solution)/shard_map/ppermute | solution.py:512
  148.3 1.9 fusion.1
  150.8 1.7 collective-permute-start.26
  152.5 33.6 %shard_map.336 = (bf16[640,512]{1,0:T(8,128)(2,1)}, f32[1024,512]{1,0:T(8,128)}, f32[1024,128]{1,0:T(8,128)}, bf16[5,512,128]{2,1,0:T(8,128)(2,1)}, bf16[5,512,1...) custom-call(s32[5,11]{1,0:T(8,128)} %pad_add_fusion.slots_ref, ...), custom_call_target="tpu_custom_call" | custom-call | flops 32000000000 | bytes 32000000 | tf_op jit(solution)/shard_map/pallas_call | solution.py:388
  186.1 1.1 fusion.6
  187.2 1.1 collective-permute-start.28
  188.3 2.8 collective-permute-start.27
  191.1 10.2 %collective-permute-done.28 = bf16[2,176,512]{2,1,0:T(8,128)(2,1)S(1)} collective-permute-done((bf16[2,176,512]{2,1,0:T(8,128)(2,1)S(1)}, bf16[2,176,512]{2,1,0:T(8,128)(2,1)S(1)}, u32[]{:S(2)}, u32[]{:S(2)}) %collective-permute-start.28) | collective-permute-done | bytes 360480 | tf_op jit(solution)/shard_map/ppermute | solution.py:512
  201.3 1.1 fusion.4
  202.5 6.5 %shard_map.337 = (bf16[8,64,512]{2,1,0:T(8,128)(2,1)}, bf16[8,64,512]{2,1,0:T(8,128)(2,1)}, bf16[8,64,512]{2,1,0:T(8,128)(2,1)}, bf16[8,64,512]{2,1,0:T(8,128)(2,1)}) custom-call(s32[32]{0:T(128)} %fusion.28.place_ref, f32[1024,512]{1,0:T(8,128)} %get-tuple-element.222.both_grads_ref, bf16[640,512]{1,0:T(8,128)(2,1)} %get-tuple-element.182.normed_ref, ...), custom_call_target="tpu_custom_call" | custom-call | flops 100000000 | bytes 100000 | tf_op jit(solution)/shard_map/pallas_call | solution.py:862
  209.1 5.5 %collective-permute-done.29 = bf16[2,176,512]{2,1,0:T(8,128)(2,1)S(1)} collective-permute-done((bf16[2,176,512]{2,1,0:T(8,128)(2,1)S(1)}, bf16[2,176,512]{2,1,0:T(8,128)(2,1)S(1)}, u32[]{:S(2)}, u32[]{:S(2)}) %collective-permute-start.29) | collective-permute-done | bytes 360480 | tf_op jit(solution)/shard_map/ppermute | solution.py:512
  215.2 1.6 collective-permute-done.32
  218.1 13.6 %collective-permute-done.30 = bf16[5,512,128]{2,1,0:T(8,128)(2,1)S(1)} collective-permute-done((bf16[5,512,128]{2,1,0:T(8,128)(2,1)S(1)}, bf16[5,512,128]{2,1,0:T(8,128)(2,1)S(1)}, u32[]{:S(2)}, u32[]{:S(2)}) %collective-permute-start.30) | collective-permute-done | bytes 655392 | tf_op jit(solution)/shard_map/ppermute | solution.py:512
  231.8 2.3 collective-permute-done.31
  234.0 1.1 fusion.3
  235.3 1.8 collective-permute-start.34
  238.5 1.6 convolution_add_fusion.local_ref
  240.2 17.1 %collective-permute-done.37 = bf16[4,64,512]{2,1,0:T(8,128)(2,1)S(1)} collective-permute-done((bf16[4,64,512]{2,1,0:T(8,128)(2,1)S(1)}, bf16[4,64,512]{2,1,0:T(8,128)(2,1)S(1)}, u32[]{:S(2)}, u32[]{:S(2)}) %collective-permute-start.37) | collective-permute-done | bytes 262176 | tf_op jit(solution)/shard_map/ppermute | solution.py:512
  257.2 3.8 %collective-permute-done.35 = bf16[5,512,128]{2,1,0:T(8,128)(2,1)S(1)} collective-permute-done((bf16[5,512,128]{2,1,0:T(8,128)(2,1)S(1)}, bf16[5,512,128]{2,1,0:T(8,128)(2,1)S(1)}, u32[]{:S(2)}, u32[]{:S(2)}) %collective-permute-start.35) | collective-permute-done | bytes 655392 | tf_op jit(solution)/shard_map/ppermute | solution.py:512
  261.0 1.1 fusion.2
  262.2 1.5 collective-permute-start.39
  265.4 3.8 %collective-permute-start.44 = (bf16[64,512]{1,0:T(8,128)(2,1)S(1)}, bf16[64,512]{1,0:T(8,128)(2,1)S(1)}, u32[]{:S(2)}, u32[]{:S(2)}) collective-permute-start(bf16[64,512]{1,0:T(8,128)(2,1)S(1)} %get-tuple-element.290), channel_id=1, source_target_pairs={{0,2},{1,3},{2,4},{3,5},{4,6},{5,7},{6,0},{7,1},{8,10},{9,11},{10,... | collective-permute-start | bytes 196616 | tf_op jit(solution)/shard_map/ppermute | solution.py:512
  269.8 7.9 %collective-permute-done.39.refs_0_ = bf16[5,512,128]{2,1,0:T(8,128)(2,1)S(1)} collective-permute-done((bf16[5,512,128]{2,1,0:T(8,128)(2,1)S(1)}, bf16[5,512,128]{2,1,0:T(8,128)(2,1)S(1)}, u32[]{:S(2)}, u32[]{:S(2)}) %collective-permute-start.39) | collective-permute-done | bytes 655392 | tf_op jit(solution)/shard_map/ppermute | solution.py:512
  277.6 1.1 collective-permute-start.41
  278.7 4.0 %collective-permute-done.40.refs_1_ = bf16[5,512,128]{2,1,0:T(8,128)(2,1)S(1)} collective-permute-done((bf16[5,512,128]{2,1,0:T(8,128)(2,1)S(1)}, bf16[5,512,128]{2,1,0:T(8,128)(2,1)S(1)}, u32[]{:S(2)}, u32[]{:S(2)}) %collective-permute-start.40) | collective-permute-done | bytes 655392 | tf_op jit(solution)/shard_map/ppermute | solution.py:512
  283.5 4.7 %shard_map.338 = f32[640,512]{1,0:T(8,128)} custom-call(bf16[640,512]{1,0:T(8,128)(2,1)} %input_ref.3, f32[640,512]{1,0:T(8,128)} %convolution_add_fusion.local_ref, f32[640,512]{1,0:T(8,128)} %get-tuple-element.215.middle_grad_ref, f32[16,512]{1,0:T(8,128)} %get-tuple-element.160.refs_7_.vectors_ref, bf16[5,512,128]{2,1,0:T(8,128)(2,1)} %copy-done.24, ...), custom_call_target="tpu_custom_call" | custom-call | flops 3000000000 | bytes 3000000 | tf_op jit(solution)/shard_map/pallas_call | solution.py:1257
  288.9 2.0 shard_map.339
  (226 shorter events, 35.7 us)
Async XLA Ops:
  2.6 20.6 %collective-permute-start.2 = (bf16[80,512]{1,0:T(8,128)(2,1)}, bf16[80,512]{1,0:T(8,128)(2,1)S(1)}, u32[]{:S(2)}, u32[]{:S(2)}) collective-permute-start(bf16[80,512]{1,0:T(8,128)(2,1)} %get-tuple-element.145), channel_id=1, source_target_pairs={{0,6},{1,7},{2,0},{3,1},{4,2},{5,3},{6,4},{7,5},{8,14},{9,15},{10,... | collective-permute-start | bytes 245768 | tf_op jit(solution)/shard_map/ppermute | solution.py:512
  3.1 20.2 %collective-permute-start.1 = (bf16[80,512]{1,0:T(8,128)(2,1)}, bf16[80,512]{1,0:T(8,128)(2,1)S(1)}, u32[]{:S(2)}, u32[]{:S(2)}) collective-permute-start(bf16[80,512]{1,0:T(8,128)(2,1)} %get-tuple-element.145), channel_id=1, source_target_pairs={{0,4},{1,5},{2,6},{3,7},{4,0},{5,1},{6,2},{7,3},{8,12},{9,13},{10,... | collective-permute-start | bytes 245768 | tf_op jit(solution)/shard_map/ppermute | solution.py:512
  3.4 25.7 %collective-permute-start.4 = (bf16[640,512]{1,0:T(8,128)(2,1)}, bf16[640,512]{1,0:T(8,128)(2,1)S(1)}, u32[]{:S(2)}, u32[]{:S(2)}) collective-permute-start(bf16[640,512]{1,0:T(8,128)(2,1)} %input_ref.3), channel_id=1, source_target_pairs={{0,2},{1,3},{2,4},{3,5},{4,6},{5,7},{6,0},{7,1},{8,10},{9,11},{10,... | collective-permute-start | bytes 1966088 | tf_op jit(solution)/shard_map/ppermute | solution.py:512
  6.5 22.7 %collective-permute-start.3 = (bf16[640,512]{1,0:T(8,128)(2,1)}, bf16[640,512]{1,0:T(8,128)(2,1)S(1)}, u32[]{:S(2)}, u32[]{:S(2)}) collective-permute-start(bf16[640,512]{1,0:T(8,128)(2,1)} %input_ref.3), channel_id=1, source_target_pairs={{0,1},{1,0},{2,3},{3,2},{4,5},{5,4},{6,7},{7,6},{8,9},{9,8},{10,11... | collective-permute-start | bytes 1966088 | tf_op jit(solution)/shard_map/ppermute | solution.py:512
  8.0 21.2 %collective-permute-start = (bf16[240,512]{1,0:T(8,128)(2,1)}, bf16[240,512]{1,0:T(8,128)(2,1)S(1)}, u32[]{:S(2)}, u32[]{:S(2)}) collective-permute-start(bf16[240,512]{1,0:T(8,128)(2,1)} %get-tuple-element.146), channel_id=1, source_target_pairs={{0,2},{1,3},{2,4},{3,5},{4,6},{5,7},{6,0},{7,1},{8,10},{9,11},{10,... | collective-permute-start | bytes 737288 | tf_op jit(solution)/shard_map/ppermute | solution.py:512
  23.1 34.5 %copy-start.15 = (bf16[240,512]{1,0:T(8,128)(2,1)S(1)}, bf16[240,512]{1,0:T(8,128)(2,1)}, u32[]{:S(2)}) copy-start(bf16[240,512]{1,0:T(8,128)(2,1)} %get-tuple-element.146) | copy-start | bytes 737284
  29.2 28.5 %copy-start.16 = (bf16[640,512]{1,0:T(8,128)(2,1)}, bf16[640,512]{1,0:T(8,128)(2,1)S(1)}, u32[]{:S(2)}) copy-start(bf16[640,512]{1,0:T(8,128)(2,1)S(1)} %collective-permute-done.4.refs_2_) | copy-start | bytes 1966084
  29.2 28.5 %copy-start.17 = (bf16[640,512]{1,0:T(8,128)(2,1)}, bf16[640,512]{1,0:T(8,128)(2,1)S(1)}, u32[]{:S(2)}) copy-start(bf16[640,512]{1,0:T(8,128)(2,1)S(1)} %collective-permute-done.3.refs_1_) | copy-start | bytes 1966084
  29.2 23.3 %collective-permute-start.7 = (bf16[640,512]{1,0:T(8,128)(2,1)S(1)}, bf16[640,512]{1,0:T(8,128)(2,1)}, u32[]{:S(2)}, u32[]{:S(2)}) collective-permute-start(bf16[640,512]{1,0:T(8,128)(2,1)S(1)} %collective-permute-done.4.refs_2_), channel_id=1, source_target_pairs={{0,1},{1,0},{2,3},{3,2},{4,5},{5,4},{6,7},{7,6},{8,9},{9,8},{10,11... | collective-permute-start | bytes 1966088 | tf_op jit(solution)/shard_map/ppermute | solution.py:512
  30.7 21.8 %collective-permute-start.6 = (bf16[640,512]{1,0:T(8,128)(2,1)S(1)}, bf16[640,512]{1,0:T(8,128)(2,1)}, u32[]{:S(2)}, u32[]{:S(2)}) collective-permute-start(bf16[640,512]{1,0:T(8,128)(2,1)S(1)} %collective-permute-done.4.refs_2_), channel_id=1, source_target_pairs={{0,2},{1,3},{2,4},{3,5},{4,6},{5,7},{6,0},{7,1},{8,10},{9,11},{10,... | collective-permute-start | bytes 1966088 | tf_op jit(solution)/shard_map/ppermute | solution.py:512
  34.3 18.2 %collective-permute-start.5 = (bf16[4,80,512]{2,1,0:T(8,128)(2,1)S(1)}, bf16[4,80,512]{2,1,0:T(8,128)(2,1)S(1)}, u32[]{:S(2)}, u32[]{:S(2)}) collective-permute-start(bf16[4,80,512]{2,1,0:T(8,128)(2,1)S(1)} %get-tuple-element.288), channel_id=1, source_target_pairs={{0,1},{1,0},{2,3},{3,2},{4,5},{5,4},{6,7},{7,6},{8,9},{9,8},{10,11... | collective-permute-start | bytes 983048 | tf_op jit(solution)/shard_map/ppermute | solution.py:512
  34.9 15.5 %collective-permute-start.8 = (bf16[160,512]{1,0:T(8,128)(2,1)S(1)}, bf16[160,512]{1,0:T(8,128)(2,1)S(1)}, u32[]{:S(2)}, u32[]{:S(2)}) collective-permute-start(bf16[160,512]{1,0:T(8,128)(2,1)S(1)} %slice.82), channel_id=1, source_target_pairs={{0,2},{1,3},{2,4},{3,5},{4,6},{5,7},{6,0},{7,1},{8,10},{9,11},{10,... | collective-permute-start | bytes 491528 | tf_op jit(solution)/shard_map/ppermute | solution.py:512
  52.5 20.6 %collective-permute-start.11 = (bf16[640,512]{1,0:T(8,128)(2,1)}, bf16[640,512]{1,0:T(8,128)(2,1)}, u32[]{:S(2)}, u32[]{:S(2)}) collective-permute-start(bf16[640,512]{1,0:T(8,128)(2,1)} %collective-permute-done.6.refs_4_), channel_id=1, source_target_pairs={{0,1},{1,0},{2,3},{3,2},{4,5},{5,4},{6,7},{7,6},{8,9},{9,8},{10,11... | collective-permute-start | bytes 1966088 | tf_op jit(solution)/shard_map/ppermute | solution.py:512
  54.0 19.1 %collective-permute-start.10 = (bf16[640,512]{1,0:T(8,128)(2,1)}, bf16[640,512]{1,0:T(8,128)(2,1)}, u32[]{:S(2)}, u32[]{:S(2)}) collective-permute-start(bf16[640,512]{1,0:T(8,128)(2,1)} %collective-permute-done.6.refs_4_), channel_id=1, source_target_pairs={{0,2},{1,3},{2,4},{3,5},{4,6},{5,7},{6,0},{7,1},{8,10},{9,11},{10,... | collective-permute-start | bytes 1966088 | tf_op jit(solution)/shard_map/ppermute | solution.py:512
  56.8 16.3 %collective-permute-start.9 = (bf16[2,4,80,512]{3,2,1,0:T(8,128)(2,1)S(1)}, bf16[2,4,80,512]{3,2,1,0:T(8,128)(2,1)}, u32[]{:S(2)}, u32[]{:S(2)}) collective-permute-start(bf16[2,4,80,512]{3,2,1,0:T(8,128)(2,1)S(1)} %pad_maximum_fusion.1), channel_id=1, source_target_pairs={{0,16},{8,24},{16,0},{24,8},{1,17},{9,25},{17,1},{25,9},{2,18},{10... | collective-permute-start | bytes 1966088 | tf_op jit(solution)/shard_map/ppermute | solution.py:512
  57.4 15.7 %collective-permute-start.12 = (bf16[160,512]{1,0:T(8,128)(2,1)S(1)}, bf16[160,512]{1,0:T(8,128)(2,1)S(1)}, u32[]{:S(2)}, u32[]{:S(2)}) collective-permute-start(bf16[160,512]{1,0:T(8,128)(2,1)S(1)} %collective-permute-done.8), channel_id=1, source_target_pairs={{0,2},{1,3},{2,4},{3,5},{4,6},{5,7},{6,0},{7,1},{8,10},{9,11},{10,... | collective-permute-start | bytes 491528 | tf_op jit(solution)/shard_map/ppermute | solution.py:512
  58.3 16.0 %collective-permute-start.13 = (bf16[2,4,80,512]{3,2,1,0:T(8,128)(2,1)S(1)}, bf16[2,4,80,512]{3,2,1,0:T(8,128)(2,1)S(1)}, u32[]{:S(2)}, u32[]{:S(2)}) collective-permute-start(bf16[2,4,80,512]{3,2,1,0:T(8,128)(2,1)S(1)} %pad_maximum_fusion.1), channel_id=1, source_target_pairs={{0,8},{8,0},{16,24},{24,16},{1,9},{9,1},{17,25},{25,17},{2,10},{10... | collective-permute-start | bytes 1966088 | tf_op jit(solution)/shard_map/ppermute | solution.py:512
  73.1 2.5 collective-permute-start.14
  73.8 22.2 %collective-permute-start.17 = (bf16[640,512]{1,0:T(8,128)(2,1)}, bf16[640,512]{1,0:T(8,128)(2,1)S(1)}, u32[]{:S(2)}, u32[]{:S(2)}) collective-permute-start(bf16[640,512]{1,0:T(8,128)(2,1)} %collective-permute-done.10.refs_6_), channel_id=1, source_target_pairs={{0,1},{1,0},{2,3},{3,2},{4,5},{5,4},{6,7},{7,6},{8,9},{9,8},{10,11... | collective-permute-start | bytes 1966088 | tf_op jit(solution)/shard_map/ppermute | solution.py:512
  78.9 19.2 %collective-permute-start.16 = (bf16[4,80,512]{2,1,0:T(8,128)(2,1)S(1)}, bf16[4,80,512]{2,1,0:T(8,128)(2,1)S(1)}, u32[]{:S(2)}, u32[]{:S(2)}) collective-permute-start(bf16[4,80,512]{2,1,0:T(8,128)(2,1)S(1)} %get-tuple-element.286), channel_id=1, source_target_pairs={{0,1},{1,0},{2,3},{3,2},{4,5},{5,4},{6,7},{7,6},{8,9},{9,8},{10,11... | collective-permute-start | bytes 983048 | tf_op jit(solution)/shard_map/ppermute | solution.py:512
  80.0 18.1 %collective-permute-start.15 = (bf16[4,80,512]{2,1,0:T(8,128)(2,1)S(1)}, bf16[4,80,512]{2,1,0:T(8,128)(2,1)S(1)}, u32[]{:S(2)}, u32[]{:S(2)}) collective-permute-start(bf16[4,80,512]{2,1,0:T(8,128)(2,1)S(1)} %get-tuple-element.284), channel_id=1, source_target_pairs={{0,16},{8,24},{16,0},{24,8},{1,17},{9,25},{17,1},{25,9},{2,18},{10... | collective-permute-start | bytes 983048 | tf_op jit(solution)/shard_map/ppermute | solution.py:512
  98.2 24.6 %collective-permute-start.22 = (bf16[2,4,80,512]{3,2,1,0:T(8,128)(2,1)S(1)}, bf16[2,4,80,512]{3,2,1,0:T(8,128)(2,1)S(1)}, u32[]{:S(2)}, u32[]{:S(2)}) collective-permute-start(bf16[2,4,80,512]{3,2,1,0:T(8,128)(2,1)S(1)} %pad_maximum_fusion.3), channel_id=1, source_target_pairs={{0,8},{8,0},{16,24},{24,16},{1,9},{9,1},{17,25},{25,17},{2,10},{10... | collective-permute-start | bytes 1966088 | tf_op jit(solution)/shard_map/ppermute | solution.py:512
  98.3 22.0 %collective-permute-start.19 = (bf16[2,4,80,512]{3,2,1,0:T(8,128)(2,1)S(1)}, bf16[2,4,80,512]{3,2,1,0:T(8,128)(2,1)}, u32[]{:S(2)}, u32[]{:S(2)}) collective-permute-start(bf16[2,4,80,512]{3,2,1,0:T(8,128)(2,1)S(1)} %pad_maximum_fusion.3), channel_id=1, source_target_pairs={{0,1},{1,0},{2,3},{3,2},{4,5},{5,4},{6,7},{7,6},{8,9},{9,8},{10,11... | collective-permute-start | bytes 1966088 | tf_op jit(solution)/shard_map/ppermute | solution.py:512
  99.0 23.8 %collective-permute-start.20 = (bf16[2,4,80,512]{3,2,1,0:T(8,128)(2,1)S(1)}, bf16[2,4,80,512]{3,2,1,0:T(8,128)(2,1)S(1)}, u32[]{:S(2)}, u32[]{:S(2)}) collective-permute-start(bf16[2,4,80,512]{3,2,1,0:T(8,128)(2,1)S(1)} %pad_maximum_fusion.2), channel_id=1, source_target_pairs={{0,8},{8,0},{16,24},{24,16},{1,9},{9,1},{17,25},{25,17},{2,10},{10... | collective-permute-start | bytes 1966088 | tf_op jit(solution)/shard_map/ppermute | solution.py:512
  99.2 21.1 %collective-permute-start.18 = (bf16[2,4,80,512]{3,2,1,0:T(8,128)(2,1)S(1)}, bf16[2,4,80,512]{3,2,1,0:T(8,128)(2,1)}, u32[]{:S(2)}, u32[]{:S(2)}) collective-permute-start(bf16[2,4,80,512]{3,2,1,0:T(8,128)(2,1)S(1)} %pad_maximum_fusion.2), channel_id=1, source_target_pairs={{0,16},{8,24},{16,0},{24,8},{1,17},{9,25},{17,1},{25,9},{2,18},{10... | collective-permute-start | bytes 1966088 | tf_op jit(solution)/shard_map/ppermute | solution.py:512
  120.3 3.0 %collective-permute-start.21 = (bf16[2,4,80,512]{3,2,1,0:T(8,128)(2,1)}, bf16[2,4,80,512]{3,2,1,0:T(8,128)(2,1)}, u32[]{:S(2)}, u32[]{:S(2)}) collective-permute-start(bf16[2,4,80,512]{3,2,1,0:T(8,128)(2,1)} %collective-permute-done.18), channel_id=1, source_target_pairs={{0,8},{8,0},{16,24},{24,16},{1,9},{9,1},{17,25},{25,17},{2,10},{10... | collective-permute-start | bytes 1966088 | tf_op jit(solution)/shard_map/ppermute | solution.py:512
  121.2 3.0 %collective-permute-start.23 = (bf16[2,4,80,512]{3,2,1,0:T(8,128)(2,1)}, bf16[2,4,80,512]{3,2,1,0:T(8,128)(2,1)}, u32[]{:S(2)}, u32[]{:S(2)}) collective-permute-start(bf16[2,4,80,512]{3,2,1,0:T(8,128)(2,1)} %collective-permute-done.19), channel_id=1, source_target_pairs={{0,8},{8,0},{16,24},{24,16},{1,9},{9,1},{17,25},{25,17},{2,10},{10... | collective-permute-start | bytes 1966088 | tf_op jit(solution)/shard_map/ppermute | solution.py:512
  144.8 3.5 %collective-permute-start.24 = (bf16[4,2,176,512]{3,2,1,0:T(8,128)(2,1)}, bf16[4,2,176,512]{3,2,1,0:T(8,128)(2,1)S(1)}, u32[]{:S(2)}, u32[]{:S(2)}) collective-permute-start(bf16[4,2,176,512]{3,2,1,0:T(8,128)(2,1)} %bitcast.150), channel_id=1, source_target_pairs={{0,8},{8,0},{16,24},{24,16},{1,9},{9,1},{17,25},{25,17},{2,10},{10... | collective-permute-start | bytes 4325384 | tf_op jit(solution)/shard_map/ppermute | solution.py:512
  145.2 5.1 %collective-permute-start.25 = (bf16[4,2,176,512]{3,2,1,0:T(8,128)(2,1)}, bf16[4,2,176,512]{3,2,1,0:T(8,128)(2,1)S(1)}, u32[]{:S(2)}, u32[]{:S(2)}) collective-permute-start(bf16[4,2,176,512]{3,2,1,0:T(8,128)(2,1)} %bitcast.149), channel_id=1, source_target_pairs={{0,8},{8,0},{16,24},{24,16},{1,9},{9,1},{17,25},{25,17},{2,10},{10... | collective-permute-start | bytes 4325384 | tf_op jit(solution)/shard_map/ppermute | solution.py:512
  150.8 35.3 %collective-permute-start.26 = (bf16[4,2,176,512]{3,2,1,0:T(8,128)(2,1)S(1)}, bf16[4,2,176,512]{3,2,1,0:T(8,128)(2,1)}, u32[]{:S(2)}, u32[]{:S(2)}) collective-permute-start(bf16[4,2,176,512]{3,2,1,0:T(8,128)(2,1)S(1)} %fusion), channel_id=1, source_target_pairs={{0,16},{8,24},{16,0},{24,8},{1,17},{9,25},{17,1},{25,9},{2,18},{10... | collective-permute-start | bytes 4325384 | tf_op jit(solution)/shard_map/ppermute | solution.py:512
  187.2 14.2 %collective-permute-start.28 = (bf16[2,176,512]{2,1,0:T(8,128)(2,1)S(1)}, bf16[2,176,512]{2,1,0:T(8,128)(2,1)S(1)}, u32[]{:S(2)}, u32[]{:S(2)}) collective-permute-start(bf16[2,176,512]{2,1,0:T(8,128)(2,1)S(1)} %fusion.6), channel_id=1, source_target_pairs={{0,6},{1,7},{2,0},{3,1},{4,2},{5,3},{6,4},{7,5},{8,14},{9,15},{10,... | collective-permute-start | bytes 1081352 | tf_op jit(solution)/shard_map/ppermute | solution.py:512
  188.3 20.8 %collective-permute-start.27 = (bf16[5,512,128]{2,1,0:T(8,128)(2,1)}, bf16[5,512,128]{2,1,0:T(8,128)(2,1)S(1)}, u32[]{:S(2)}, u32[]{:S(2)}) collective-permute-start(bf16[5,512,128]{2,1,0:T(8,128)(2,1)} %get-tuple-element.219), channel_id=1, source_target_pairs={{0,1},{1,0},{2,3},{3,2},{4,5},{5,4},{6,7},{7,6},{8,9},{9,8},{10,11... | collective-permute-start | bytes 1966088 | tf_op jit(solution)/shard_map/ppermute | solution.py:512
  202.5 12.2 %collective-permute-start.29 = (bf16[2,176,512]{2,1,0:T(8,128)(2,1)S(1)}, bf16[2,176,512]{2,1,0:T(8,128)(2,1)S(1)}, u32[]{:S(2)}, u32[]{:S(2)}) collective-permute-start(bf16[2,176,512]{2,1,0:T(8,128)(2,1)S(1)} %fusion.4), channel_id=1, source_target_pairs={{0,6},{1,7},{2,0},{3,1},{4,2},{5,3},{6,4},{7,5},{8,14},{9,15},{10,... | collective-permute-start | bytes 1081352 | tf_op jit(solution)/shard_map/ppermute | solution.py:512
  214.6 2.1 collective-permute-start.32
  214.6 17.1 %collective-permute-start.30 = (bf16[5,512,128]{2,1,0:T(8,128)(2,1)S(1)}, bf16[5,512,128]{2,1,0:T(8,128)(2,1)S(1)}, u32[]{:S(2)}, u32[]{:S(2)}) collective-permute-start(bf16[5,512,128]{2,1,0:T(8,128)(2,1)S(1)} %copy-done.23), channel_id=1, source_target_pairs={{0,1},{1,0},{2,3},{3,2},{4,5},{5,4},{6,7},{7,6},{8,9},{9,8},{10,11... | collective-permute-start | bytes 1966088 | tf_op jit(solution)/shard_map/ppermute | solution.py:512
  214.9 19.1 %collective-permute-start.31 = (bf16[5,512,128]{2,1,0:T(8,128)(2,1)S(1)}, bf16[5,512,128]{2,1,0:T(8,128)(2,1)S(1)}, u32[]{:S(2)}, u32[]{:S(2)}) collective-permute-start(bf16[5,512,128]{2,1,0:T(8,128)(2,1)S(1)} %add_convert_fusion.2), channel_id=1, source_target_pairs={{0,6},{1,7},{2,0},{3,1},{4,2},{5,3},{6,4},{7,5},{8,14},{9,15},{10,... | collective-permute-start | bytes 1966088 | tf_op jit(solution)/shard_map/ppermute | solution.py:512
  216.9 17.1 %collective-permute-start.33 = (bf16[2,4,64,512]{3,2,1,0:T(8,128)(2,1)S(1)}, bf16[2,4,64,512]{3,2,1,0:T(8,128)(2,1)S(1)}, u32[]{:S(2)}, u32[]{:S(2)}) collective-permute-start(bf16[2,4,64,512]{3,2,1,0:T(8,128)(2,1)S(1)} %add_convert_fusion.5), channel_id=1, source_target_pairs={{0,16},{8,24},{16,0},{24,8},{1,17},{9,25},{17,1},{25,9},{2,18},{10... | collective-permute-start | bytes 1572872 | tf_op jit(solution)/shard_map/ppermute | solution.py:512
  218.1 19.3 %collective-permute-start.36 = (bf16[2,4,64,512]{3,2,1,0:T(8,128)(2,1)S(1)}, bf16[2,4,64,512]{3,2,1,0:T(8,128)(2,1)S(1)}, u32[]{:S(2)}, u32[]{:S(2)}) collective-permute-start(bf16[2,4,64,512]{3,2,1,0:T(8,128)(2,1)S(1)} %bitcast.154), channel_id=1, source_target_pairs={{0,8},{8,0},{16,24},{24,16},{1,9},{9,1},{17,25},{25,17},{2,10},{10... | collective-permute-start | bytes 1572872 | tf_op jit(solution)/shard_map/ppermute | solution.py:512
  235.2 22.0 %collective-permute-start.38 = (bf16[2,176,512]{2,1,0:T(8,128)(2,1)S(1)}, bf16[2,176,512]{2,1,0:T(8,128)(2,1)S(1)}, u32[]{:S(2)}, u32[]{:S(2)}) collective-permute-start(bf16[2,176,512]{2,1,0:T(8,128)(2,1)S(1)} %fusion.3), channel_id=1, source_target_pairs={{0,6},{1,7},{2,0},{3,1},{4,2},{5,3},{6,4},{7,5},{8,14},{9,15},{10,... | collective-permute-start | bytes 1081352 | tf_op jit(solution)/shard_map/ppermute | solution.py:512
  235.3 22.0 %collective-permute-start.34 = (bf16[5,512,128]{2,1,0:T(8,128)(2,1)S(1)}, bf16[5,512,128]{2,1,0:T(8,128)(2,1)S(1)}, u32[]{:S(2)}, u32[]{:S(2)}) collective-permute-start(bf16[5,512,128]{2,1,0:T(8,128)(2,1)S(1)} %copy-done.19), channel_id=1, source_target_pairs={{0,1},{1,0},{2,3},{3,2},{4,5},{5,4},{6,7},{7,6},{8,9},{9,8},{10,11... | collective-permute-start | bytes 1966088 | tf_op jit(solution)/shard_map/ppermute | solution.py:512
  237.3 23.7 %collective-permute-start.35 = (bf16[5,512,128]{2,1,0:T(8,128)(2,1)S(1)}, bf16[5,512,128]{2,1,0:T(8,128)(2,1)S(1)}, u32[]{:S(2)}, u32[]{:S(2)}) collective-permute-start(bf16[5,512,128]{2,1,0:T(8,128)(2,1)S(1)} %add_convert_fusion.1), channel_id=1, source_target_pairs={{0,6},{1,7},{2,0},{3,1},{4,2},{5,3},{6,4},{7,5},{8,14},{9,15},{10,... | collective-permute-start | bytes 1966088 | tf_op jit(solution)/shard_map/ppermute | solution.py:512
  237.7 19.6 %collective-permute-start.37 = (bf16[4,64,512]{2,1,0:T(8,128)(2,1)S(1)}, bf16[4,64,512]{2,1,0:T(8,128)(2,1)S(1)}, u32[]{:S(2)}, u32[]{:S(2)}) collective-permute-start(bf16[4,64,512]{2,1,0:T(8,128)(2,1)S(1)} %slice_bitcast_fusion.1), channel_id=1, source_target_pairs={{0,1},{1,0},{2,3},{3,2},{4,5},{5,4},{6,7},{7,6},{8,9},{9,8},{10,11... | collective-permute-start | bytes 786440 | tf_op jit(solution)/shard_map/ppermute | solution.py:512
  262.2 15.5 %collective-permute-start.39 = (bf16[5,512,128]{2,1,0:T(8,128)(2,1)S(1)}, bf16[5,512,128]{2,1,0:T(8,128)(2,1)S(1)}, u32[]{:S(2)}, u32[]{:S(2)}) collective-permute-start(bf16[5,512,128]{2,1,0:T(8,128)(2,1)S(1)} %copy-done.18), channel_id=1, source_target_pairs={{0,1},{1,0},{2,3},{3,2},{4,5},{5,4},{6,7},{7,6},{8,9},{9,8},{10,11... | collective-permute-start | bytes 1966088 | tf_op jit(solution)/shard_map/ppermute | solution.py:512
  263.9 18.8 %collective-permute-start.40 = (bf16[5,512,128]{2,1,0:T(8,128)(2,1)S(1)}, bf16[5,512,128]{2,1,0:T(8,128)(2,1)S(1)}, u32[]{:S(2)}, u32[]{:S(2)}) collective-permute-start(bf16[5,512,128]{2,1,0:T(8,128)(2,1)S(1)} %add_convert_fusion), channel_id=1, source_target_pairs={{0,6},{1,7},{2,0},{3,1},{4,2},{5,3},{6,4},{7,5},{8,14},{9,15},{10,... | collective-permute-start | bytes 1966088 | tf_op jit(solution)/shard_map/ppermute | solution.py:512
  265.4 22.8 %collective-permute-start.44 = (bf16[64,512]{1,0:T(8,128)(2,1)S(1)}, bf16[64,512]{1,0:T(8,128)(2,1)S(1)}, u32[]{:S(2)}, u32[]{:S(2)}) collective-permute-start(bf16[64,512]{1,0:T(8,128)(2,1)S(1)} %get-tuple-element.290), channel_id=1, source_target_pairs={{0,2},{1,3},{2,4},{3,5},{4,6},{5,7},{6,0},{7,1},{8,10},{9,11},{10,... | collective-permute-start | bytes 196616 | tf_op jit(solution)/shard_map/ppermute | solution.py:512
  269.2 19.0 %collective-permute-start.43 = (bf16[64,512]{1,0:T(8,128)(2,1)S(1)}, bf16[64,512]{1,0:T(8,128)(2,1)S(1)}, u32[]{:S(2)}, u32[]{:S(2)}) collective-permute-start(bf16[64,512]{1,0:T(8,128)(2,1)S(1)} %get-tuple-element.291), channel_id=1, source_target_pairs={{0,4},{1,5},{2,6},{3,7},{4,0},{5,1},{6,2},{7,3},{8,12},{9,13},{10,... | collective-permute-start | bytes 196616 | tf_op jit(solution)/shard_map/ppermute | solution.py:512
  269.2 19.0 %collective-permute-start.42 = (bf16[64,512]{1,0:T(8,128)(2,1)S(1)}, bf16[64,512]{1,0:T(8,128)(2,1)S(1)}, u32[]{:S(2)}, u32[]{:S(2)}) collective-permute-start(bf16[64,512]{1,0:T(8,128)(2,1)S(1)} %get-tuple-element.292), channel_id=1, source_target_pairs={{0,6},{1,7},{2,0},{3,1},{4,2},{5,3},{6,4},{7,5},{8,14},{9,15},{10,... | collective-permute-start | bytes 196616 | tf_op jit(solution)/shard_map/ppermute | solution.py:512
  277.6 10.6 %collective-permute-start.41 = (bf16[176,512]{1,0:T(8,128)(2,1)S(1)}, bf16[176,512]{1,0:T(8,128)(2,1)S(1)}, u32[]{:S(2)}, u32[]{:S(2)}) collective-permute-start(bf16[176,512]{1,0:T(8,128)(2,1)S(1)} %get-tuple-element.249), channel_id=1, source_target_pairs={{0,1},{1,0},{2,3},{3,2},{4,5},{5,4},{6,7},{7,6},{8,9},{9,8},{10,11... | collective-permute-start | bytes 540680 | tf_op jit(solution)/shard_map/ppermute | solution.py:512
  (29 other events, 235.0 us)

commit v4 on v3

--- a/solution.py
+++ b/solution.py
@@ -81,13 +81,16 @@
     return jnp.where(lane < HD, rows[:half], rows[half:])
 
 
-def make_bias(levels, bias_ref):
-    row = lax.broadcasted_iota(jnp.int32, (BLK, DEPTH * BLK), 0)
-    col = lax.broadcasted_iota(jnp.int32, (BLK, DEPTH * BLK), 1)
-    limit = jnp.where(col < BLK, row + 1, levels * BLK)
-    bias = jnp.where(col < limit, jnp.float32(0.0), jnp.float32(NEGATIVE))
-    bias_ref[:BLK, :] = bias
-    bias_ref[BLK:, :] = bias
+def make_bias(bias_ref):
+    row = lax.broadcasted_iota(jnp.int32, bias_ref.shape, 0) % BLK
+    col = lax.broadcasted_iota(jnp.int32, bias_ref.shape, 1)
+    bias_ref[...] = jnp.where(col <= row, jnp.float32(0.0), jnp.float32(NEGATIVE))
+
+
+def masked(scores, levels, bias_ref):
+    col = lax.broadcasted_iota(jnp.int32, (1, (DEPTH - 1) * BLK), 1)
+    line = jnp.where(col < (levels - 1) * BLK, jnp.float32(0.0), jnp.float32(NEGATIVE))
+    return jnp.concatenate([scores[:, :BLK] + bias_ref[...], scores[:, BLK:] + line], axis=1)
 
 
 class Levels:
@@ -126,10 +129,10 @@
     count = query_ref.shape[0] // BLK
     levels = Levels(slots_ref, (key_source, value_source), (key_here, value_here), arrivals)
     levels.start(0)
+    make_bias(bias_ref)
 
     def one_slot(slot, carry):
         rows = pl.ds(pl.multiple_of(slot * BLK, BLK), BLK)
-        make_bias(slots_ref[slot, DEPTH], bias_ref)
         levels.step(slot, count)
         turn = slot % 2
         lane = lax.broadcasted_iota(jnp.int32, (BLK, PAIR), 1)
@@ -137,7 +140,7 @@
         for pair in range(width // PAIR):
             cols = slice(pair * PAIR, (pair + 1) * PAIR)
             stacked = stack_heads(query_ref[rows, cols])
-            scores = against(stacked, key_here[turn, :, cols]) + bias_ref[...]
+            scores = masked(against(stacked, key_here[turn, :, cols]), slots_ref[slot, DEPTH], bias_ref)
             highest = jnp.max(scores, axis=-1, keepdims=True)
             raised = jnp.exp(scores - highest)
             total = jnp.sum(raised, axis=-1, keepdims=True)
@@ -238,12 +241,12 @@
             target = shared_refs[slot // count].at[slot % count]
             pltpu.make_async_copy(zero_block, target, departures.at[slot]).start()
 
+    make_bias(bias_ref)
     key_sums[...] = jnp.zeros_like(key_sums)
     value_sums[...] = jnp.zeros_like(value_sums)
 
     def one_slot(slot, carry):
         rows = pl.ds(pl.multiple_of(slot * BLK, BLK), BLK)
-        make_bias(slots_ref[slot, DEPTH], bias_ref)
         levels.step(slot, count)
         turn = slot % 2
         for pair in range(width // PAIR):
@@ -257,7 +260,7 @@
                 [logsum_ref[rows, 2 * pair : 2 * pair + 1], logsum_ref[rows, 2 * pair + 1 : 2 * pair + 2]], axis=0
             )
             key_rows = key_here[turn, :, cols]
-            shares = jnp.exp(against(stacked, key_rows) + bias_ref[...] - logsum)
+            shares = jnp.exp(masked(against(stacked, key_rows), slots_ref[slot, DEPTH], bias_ref) - logsum)
             share_grad = against(grad_stacked, value_here[turn, :, cols])
             score_grad = (shares * (share_grad - row_dot)).astype(jnp.bfloat16)
             query_grad = unstack_heads(matmul(score_grad, key_rows)) * (HD ** (-0.5))
@@ -334,7 +337,7 @@
     return [
         pltpu.VMEM((2, DEPTH * BLK, width), jnp.bfloat16),
         pltpu.VMEM((2, DEPTH * BLK, width), jnp.bfloat16),
-        pltpu.VMEM((2 * BLK, DEPTH * BLK), jnp.float32),
+        pltpu.VMEM((2 * BLK, BLK), jnp.float32),
     ]
 
 

time: 295 us -> 294 us (level)
  waiting for transfers between devices: 109 us -> 106 us
    ppermute x45, waiting for transfers between devices: 109 us -> 106 us  [rotate(): return lax.ppermute(values, self.name, pairs)]
  transfers between devices with their start and end apart: 45 -> 45, of which waited for: 19 -> 20; matrix products, arithmetic and copies ran while one was open for 10% -> 11% of each run, Pallas kernels for 28% -> 28%
where the time goes in v4:
time: 294 us; the launch traced here: 288 us
  waiting for transfers between devices  106 us (36%)
  Pallas kernels  105 us (36%)
  starting transfers between devices  40.3 us (14%)
  other arithmetic  25.3 us (9%)
  local copies, waits for them, and re-layouts  7.5 us (3%)
    ppermute x45, waiting for transfers between devices, rotate(): return lax.ppermute(values, self.name, pairs)  106 us
    ppermute x45, starting transfers between devices, rotate(): return lax.ppermute(values, self.name, pairs)  40.3 us
    pallas_call x1, Pallas kernels, attend_backward(): pl.pallas_call(backward_kernel, cost_estimate=about(32), out_shape=(jax.S...  31.8 us
    pallas_call x1, Pallas kernels, shards(): pl.pallas_call(middle_kernel, cost_estimate=about(20), out_shape=(struct(...  20.6 us
    pallas_call x1, Pallas kernels, project_and_attend(): pl.pallas_call(last_forward_kernel, cost_estimate=about(20), out_shape=(j...  20.3 us
    pallas_call x1, Pallas kernels, project(): pl.pallas_call(body, cost_estimate=about(1 + 1.6 * count), out_shape=[who...  14.2 us
    pallas_call x4, Pallas kernels, local_call(): pl.pallas_call(kernel, cost_estimate=about(cost), out_shape=outs, in_spec...  13.6 us
    reduce_sum x10, other arithmetic, lookup(): jnp.sum(jnp.where(matches, lookup_table, jnp.int32(0)), axis=-1, dtype=jn...  7.79 us
  transfers between devices with their start and end apart: 45, of which 20 were waited for; matrix products, arithmetic and copies ran while one was open for 11% of the time, Pallas kernels for 28%

profile of v4, /device:TPU:28, one launch (start us, length us, event | category | flops | bytes accessed | tf_op | source)
XLA Modules:
  0.0 288.1 jit_solution(5592509948046895560)
XLA Ops:
  0.7 2.0 shard_map.331
  3.4 3.0 %collective-permute-start.4 = (bf16[640,512]{1,0:T(8,128)(2,1)}, bf16[640,512]{1,0:T(8,128)(2,1)S(1)}, u32[]{:S(2)}, u32[]{:S(2)}) collective-permute-start(bf16[640,512]{1,0:T(8,128)(2,1)} %input_ref.3), channel_id=1, source_target_pairs={{0,2},{1,3},{2,4},{3,5},{4,6},{5,7},{6,0},{7,1},{8,10},{9,11},{10,... | collective-permute-start | bytes 1966088 | tf_op jit(solution)/shard_map/ppermute | solution.py:515
  6.5 1.5 collective-permute-start.3
  8.0 1.0 collective-permute-start
  23.3 5.9 %collective-permute-done = bf16[240,512]{1,0:T(8,128)(2,1)S(1)} collective-permute-done((bf16[240,512]{1,0:T(8,128)(2,1)}, bf16[240,512]{1,0:T(8,128)(2,1)S(1)}, u32[]{:S(2)}, u32[]{:S(2)}) %collective-permute-start) | collective-permute-done | bytes 245792 | tf_op jit(solution)/shard_map/ppermute | solution.py:515
  29.2 1.6 collective-permute-start.7
  30.7 2.6 collective-permute-start.6
  35.2 1.2 add_bitcast_fusion.used_ref
  37.5 12.9 %collective-permute-done.8 = bf16[160,512]{1,0:T(8,128)(2,1)S(1)} collective-permute-done((bf16[160,512]{1,0:T(8,128)(2,1)S(1)}, bf16[160,512]{1,0:T(8,128)(2,1)S(1)}, u32[]{:S(2)}, u32[]{:S(2)}) %collective-permute-start.8) | collective-permute-done | bytes 163872 | tf_op jit(solution)/shard_map/ppermute | solution.py:515
  50.4 2.1 collective-permute-done.5
  52.5 1.5 collective-permute-start.11
  54.0 2.7 collective-permute-start.10
  58.4 14.8 %collective-permute-done.12 = bf16[160,512]{1,0:T(8,128)(2,1)S(1)} collective-permute-done((bf16[160,512]{1,0:T(8,128)(2,1)S(1)}, bf16[160,512]{1,0:T(8,128)(2,1)S(1)}, u32[]{:S(2)}, u32[]{:S(2)}) %collective-permute-start.12) | collective-permute-done | bytes 163872 | tf_op jit(solution)/shard_map/ppermute | solution.py:515
  74.3 1.3 collective-permute-done.14
  75.6 3.1 %shard_map.332 = (bf16[512,512]{1,0:T(8,128)(2,1)}, bf16[512,512]{1,0:T(8,128)(2,1)}, bf16[512,512]{1,0:T(8,128)(2,1)}, bf16[512,512]{1,0:T(8,128)(2,1)}, f32[16,512]{1,0:T(8,128)}) custom-call(s32[32]{0:T(128)} %fusion.28.place_ref, bf16[8,80,512]{2,1,0:T(8,128)(2,1)} %bitcast.131, bf16[8,80,512]{2,1,0:T(8,128)(2,1)} %bitcast.30.refs_1_, ...), custom_call_target="tpu_custom_call" | custom-call | flops 3000000000 | bytes 3000000 | tf_op jit(solution)/shard_map/pallas_call | solution.py:865
  78.9 1.1 collective-permute-start.16
  80.6 14.2 %shard_map.333 = (bf16[5120,512]{1,0:T(8,128)(2,1)}, bf16[5120,512]{1,0:T(8,128)(2,1)}, bf16[5120,512]{1,0:T(8,128)(2,1)}, bf16[640,512]{1,0:T(8,128)(2,1)}, bf16[640,512]{1,0:T(8,128)(2,1)}) custom-call(bf16[640,512]{1,0:T(8,128)(2,1)} %input_ref.3, bf16[640,512]{1,0:T(8,128)(2,1)} %copy-done.17, bf16[640,512]{1,0:T(8,128)(2,1)} %copy-done.16, ...), custom_call_target="tpu_custom_call" | custom-call | flops 12199999488 | bytes 12200000 | tf_op jit(solution)/shard_map/pallas_call | solution.py:483
  94.8 1.1 pad_maximum_fusion.weight_ref
  96.0 2.1 collective-permute-done.16
  99.9 20.3 %shard_map.334 = (bf16[640,512]{1,0:T(8,128)(2,1)}, f32[640,128]{1,0:T(8,128)}, bf16[5120,512]{1,0:T(8,128)(2,1)}, bf16[5120,512]{1,0:T(8,128)(2,1)}, bf16[5120,512]{1,0:T(8,128)(2,1)}) custom-call(s32[5,11]{1,0:T(8,128)} %pad_add_fusion.slots_ref, ...), custom_call_target="tpu_custom_call", output_to_operand_aliasing={{2}: (6, {}), {3}: (7, {}), {4}: (8, {})} | custom-call | flops 20000000000 | bytes 20000000 | tf_op jit(solution)/shard_map/pallas_call | solution.py:363
  123.7 20.6 %shard_map.335 = (f32[16,512]{1,0:T(8,128)}, bf16[640,512]{1,0:T(8,128)(2,1)}, f32[640,512]{1,0:T(8,128)}, bf16[640,512]{1,0:T(8,128)(2,1)}, bf16[640,512]{1,0:T...) custom-call(s32[3,32]{1,0:T(4,128)} %pad_add_fusion.1.place_ref, ...), custom_call_target="tpu_custom_call" | custom-call | flops 20000000000 | bytes 20000000 | tf_op jit(solution)/shard_map/pallas_call | solution.py:1067
  144.8 2.9 %collective-permute-done.24 = bf16[4,2,176,512]{3,2,1,0:T(8,128)(2,1)S(1)} collective-permute-done((bf16[4,2,176,512]{3,2,1,0:T(8,128)(2,1)}, bf16[4,2,176,512]{3,2,1,0:T(8,128)(2,1)S(1)}, u32[]{:S(2)}, u32[]{:S(2)}) %collective-permute-start.24) | collective-permute-done | bytes 1441824 | tf_op jit(solution)/shard_map/ppermute | solution.py:515
  147.7 1.9 fusion.1
  150.3 1.4 collective-permute-start.26
  151.6 31.8 %shard_map.336 = (bf16[640,512]{1,0:T(8,128)(2,1)}, f32[1024,512]{1,0:T(8,128)}, f32[1024,128]{1,0:T(8,128)}, bf16[5,512,128]{2,1,0:T(8,128)(2,1)}, bf16[5,512,1...) custom-call(s32[5,11]{1,0:T(8,128)} %pad_add_fusion.slots_ref, ...), custom_call_target="tpu_custom_call" | custom-call | flops 32000000000 | bytes 32000000 | tf_op jit(solution)/shard_map/pallas_call | solution.py:391
  184.1 1.1 fusion.6
  185.1 3.3 %collective-permute-start.28 = (bf16[2,176,512]{2,1,0:T(8,128)(2,1)S(1)}, bf16[2,176,512]{2,1,0:T(8,128)(2,1)S(1)}, u32[]{:S(2)}, u32[]{:S(2)}) collective-permute-start(bf16[2,176,512]{2,1,0:T(8,128)(2,1)S(1)} %fusion.6), channel_id=1, source_target_pairs={{0,6},{1,7},{2,0},{3,1},{4,2},{5,3},{6,4},{7,5},{8,14},{9,15},{10,... | collective-permute-start | bytes 1081352 | tf_op jit(solution)/shard_map/ppermute | solution.py:515
  188.5 1.2 collective-permute-start.27
  189.7 9.7 %collective-permute-done.28 = bf16[2,176,512]{2,1,0:T(8,128)(2,1)S(1)} collective-permute-done((bf16[2,176,512]{2,1,0:T(8,128)(2,1)S(1)}, bf16[2,176,512]{2,1,0:T(8,128)(2,1)S(1)}, u32[]{:S(2)}, u32[]{:S(2)}) %collective-permute-start.28) | collective-permute-done | bytes 360480 | tf_op jit(solution)/shard_map/ppermute | solution.py:515
  199.4 1.1 fusion.4
  200.6 6.5 %shard_map.337 = (bf16[8,64,512]{2,1,0:T(8,128)(2,1)}, bf16[8,64,512]{2,1,0:T(8,128)(2,1)}, bf16[8,64,512]{2,1,0:T(8,128)(2,1)}, bf16[8,64,512]{2,1,0:T(8,128)(2,1)}) custom-call(s32[32]{0:T(128)} %fusion.28.place_ref, f32[1024,512]{1,0:T(8,128)} %get-tuple-element.222.both_grads_ref, bf16[640,512]{1,0:T(8,128)(2,1)} %get-tuple-element.182.normed_ref, ...), custom_call_target="tpu_custom_call" | custom-call | flops 100000000 | bytes 100000 | tf_op jit(solution)/shard_map/pallas_call | solution.py:865
  207.1 4.4 %collective-permute-done.29 = bf16[2,176,512]{2,1,0:T(8,128)(2,1)S(1)} collective-permute-done((bf16[2,176,512]{2,1,0:T(8,128)(2,1)S(1)}, bf16[2,176,512]{2,1,0:T(8,128)(2,1)S(1)}, u32[]{:S(2)}, u32[]{:S(2)}) %collective-permute-start.29) | collective-permute-done | bytes 360480 | tf_op jit(solution)/shard_map/ppermute | solution.py:515
  213.9 1.4 collective-permute-start.33
  215.8 12.9 %collective-permute-done.30 = bf16[5,512,128]{2,1,0:T(8,128)(2,1)S(1)} collective-permute-done((bf16[5,512,128]{2,1,0:T(8,128)(2,1)S(1)}, bf16[5,512,128]{2,1,0:T(8,128)(2,1)S(1)}, u32[]{:S(2)}, u32[]{:S(2)}) %collective-permute-start.30) | collective-permute-done | bytes 655392 | tf_op jit(solution)/shard_map/ppermute | solution.py:515
  228.7 2.4 collective-permute-done.31
  231.1 1.1 fusion.3
  232.3 1.7 collective-permute-start.34
  235.5 1.6 convolution_add_fusion.local_ref
  237.1 16.9 %collective-permute-done.37 = bf16[4,64,512]{2,1,0:T(8,128)(2,1)S(1)} collective-permute-done((bf16[4,64,512]{2,1,0:T(8,128)(2,1)S(1)}, bf16[4,64,512]{2,1,0:T(8,128)(2,1)S(1)}, u32[]{:S(2)}, u32[]{:S(2)}) %collective-permute-start.37) | collective-permute-done | bytes 262176 | tf_op jit(solution)/shard_map/ppermute | solution.py:515
  253.9 3.8 %collective-permute-done.35 = bf16[5,512,128]{2,1,0:T(8,128)(2,1)S(1)} collective-permute-done((bf16[5,512,128]{2,1,0:T(8,128)(2,1)S(1)}, bf16[5,512,128]{2,1,0:T(8,128)(2,1)S(1)}, u32[]{:S(2)}, u32[]{:S(2)}) %collective-permute-start.35) | collective-permute-done | bytes 655392 | tf_op jit(solution)/shard_map/ppermute | solution.py:515
  257.8 1.1 fusion.2
  258.9 1.7 collective-permute-start.39
  262.3 3.8 %collective-permute-start.44 = (bf16[64,512]{1,0:T(8,128)(2,1)S(1)}, bf16[64,512]{1,0:T(8,128)(2,1)S(1)}, u32[]{:S(2)}, u32[]{:S(2)}) collective-permute-start(bf16[64,512]{1,0:T(8,128)(2,1)S(1)} %get-tuple-element.290), channel_id=1, source_target_pairs={{0,2},{1,3},{2,4},{3,5},{4,6},{5,7},{6,0},{7,1},{8,10},{9,11},{10,... | collective-permute-start | bytes 196616 | tf_op jit(solution)/shard_map/ppermute | solution.py:515
  266.7 7.3 %collective-permute-done.39.refs_0_ = bf16[5,512,128]{2,1,0:T(8,128)(2,1)S(1)} collective-permute-done((bf16[5,512,128]{2,1,0:T(8,128)(2,1)S(1)}, bf16[5,512,128]{2,1,0:T(8,128)(2,1)S(1)}, u32[]{:S(2)}, u32[]{:S(2)}) %collective-permute-start.39) | collective-permute-done | bytes 655392 | tf_op jit(solution)/shard_map/ppermute | solution.py:515
  274.0 1.6 collective-permute-start.41
  275.6 4.0 %collective-permute-done.40.refs_1_ = bf16[5,512,128]{2,1,0:T(8,128)(2,1)S(1)} collective-permute-done((bf16[5,512,128]{2,1,0:T(8,128)(2,1)S(1)}, bf16[5,512,128]{2,1,0:T(8,128)(2,1)S(1)}, u32[]{:S(2)}, u32[]{:S(2)}) %collective-permute-start.40) | collective-permute-done | bytes 655392 | tf_op jit(solution)/shard_map/ppermute | solution.py:515
  280.5 4.7 %shard_map.338 = f32[640,512]{1,0:T(8,128)} custom-call(bf16[640,512]{1,0:T(8,128)(2,1)} %input_ref.3, f32[640,512]{1,0:T(8,128)} %convolution_add_fusion.local_ref, f32[640,512]{1,0:T(8,128)} %get-tuple-element.215.middle_grad_ref, f32[16,512]{1,0:T(8,128)} %get-tuple-element.160.refs_7_.vectors_ref, bf16[5,512,128]{2,1,0:T(8,128)(2,1)} %copy-done.24, ...), custom_call_target="tpu_custom_call" | custom-call | flops 3000000000 | bytes 3000000 | tf_op jit(solution)/shard_map/pallas_call | solution.py:1260
  285.9 2.0 shard_map.339
  (226 shorter events, 36.8 us)
Async XLA Ops:
  2.6 20.6 %collective-permute-start.2 = (bf16[80,512]{1,0:T(8,128)(2,1)}, bf16[80,512]{1,0:T(8,128)(2,1)S(1)}, u32[]{:S(2)}, u32[]{:S(2)}) collective-permute-start(bf16[80,512]{1,0:T(8,128)(2,1)} %get-tuple-element.145), channel_id=1, source_target_pairs={{0,6},{1,7},{2,0},{3,1},{4,2},{5,3},{6,4},{7,5},{8,14},{9,15},{10,... | collective-permute-start | bytes 245768 | tf_op jit(solution)/shard_map/ppermute | solution.py:515
  3.1 20.2 %collective-permute-start.1 = (bf16[80,512]{1,0:T(8,128)(2,1)}, bf16[80,512]{1,0:T(8,128)(2,1)S(1)}, u32[]{:S(2)}, u32[]{:S(2)}) collective-permute-start(bf16[80,512]{1,0:T(8,128)(2,1)} %get-tuple-element.145), channel_id=1, source_target_pairs={{0,4},{1,5},{2,6},{3,7},{4,0},{5,1},{6,2},{7,3},{8,12},{9,13},{10,... | collective-permute-start | bytes 245768 | tf_op jit(solution)/shard_map/ppermute | solution.py:515
  3.4 25.7 %collective-permute-start.4 = (bf16[640,512]{1,0:T(8,128)(2,1)}, bf16[640,512]{1,0:T(8,128)(2,1)S(1)}, u32[]{:S(2)}, u32[]{:S(2)}) collective-permute-start(bf16[640,512]{1,0:T(8,128)(2,1)} %input_ref.3), channel_id=1, source_target_pairs={{0,2},{1,3},{2,4},{3,5},{4,6},{5,7},{6,0},{7,1},{8,10},{9,11},{10,... | collective-permute-start | bytes 1966088 | tf_op jit(solution)/shard_map/ppermute | solution.py:515
  6.5 22.7 %collective-permute-start.3 = (bf16[640,512]{1,0:T(8,128)(2,1)}, bf16[640,512]{1,0:T(8,128)(2,1)S(1)}, u32[]{:S(2)}, u32[]{:S(2)}) collective-permute-start(bf16[640,512]{1,0:T(8,128)(2,1)} %input_ref.3), channel_id=1, source_target_pairs={{0,1},{1,0},{2,3},{3,2},{4,5},{5,4},{6,7},{7,6},{8,9},{9,8},{10,11... | collective-permute-start | bytes 1966088 | tf_op jit(solution)/shard_map/ppermute | solution.py:515
  8.0 21.2 %collective-permute-start = (bf16[240,512]{1,0:T(8,128)(2,1)}, bf16[240,512]{1,0:T(8,128)(2,1)S(1)}, u32[]{:S(2)}, u32[]{:S(2)}) collective-permute-start(bf16[240,512]{1,0:T(8,128)(2,1)} %get-tuple-element.146), channel_id=1, source_target_pairs={{0,2},{1,3},{2,4},{3,5},{4,6},{5,7},{6,0},{7,1},{8,10},{9,11},{10,... | collective-permute-start | bytes 737288 | tf_op jit(solution)/shard_map/ppermute | solution.py:515
  23.1 34.5 %copy-start.15 = (bf16[240,512]{1,0:T(8,128)(2,1)S(1)}, bf16[240,512]{1,0:T(8,128)(2,1)}, u32[]{:S(2)}) copy-start(bf16[240,512]{1,0:T(8,128)(2,1)} %get-tuple-element.146) | copy-start | bytes 737284
  29.2 28.5 %copy-start.16 = (bf16[640,512]{1,0:T(8,128)(2,1)}, bf16[640,512]{1,0:T(8,128)(2,1)S(1)}, u32[]{:S(2)}) copy-start(bf16[640,512]{1,0:T(8,128)(2,1)S(1)} %collective-permute-done.4.refs_2_) | copy-start | bytes 1966084
  29.2 28.5 %copy-start.17 = (bf16[640,512]{1,0:T(8,128)(2,1)}, bf16[640,512]{1,0:T(8,128)(2,1)S(1)}, u32[]{:S(2)}) copy-start(bf16[640,512]{1,0:T(8,128)(2,1)S(1)} %collective-permute-done.3.refs_1_) | copy-start | bytes 1966084
  29.2 23.3 %collective-permute-start.7 = (bf16[640,512]{1,0:T(8,128)(2,1)S(1)}, bf16[640,512]{1,0:T(8,128)(2,1)}, u32[]{:S(2)}, u32[]{:S(2)}) collective-permute-start(bf16[640,512]{1,0:T(8,128)(2,1)S(1)} %collective-permute-done.4.refs_2_), channel_id=1, source_target_pairs={{0,1},{1,0},{2,3},{3,2},{4,5},{5,4},{6,7},{7,6},{8,9},{9,8},{10,11... | collective-permute-start | bytes 1966088 | tf_op jit(solution)/shard_map/ppermute | solution.py:515
  30.7 21.8 %collective-permute-start.6 = (bf16[640,512]{1,0:T(8,128)(2,1)S(1)}, bf16[640,512]{1,0:T(8,128)(2,1)}, u32[]{:S(2)}, u32[]{:S(2)}) collective-permute-start(bf16[640,512]{1,0:T(8,128)(2,1)S(1)} %collective-permute-done.4.refs_2_), channel_id=1, source_target_pairs={{0,2},{1,3},{2,4},{3,5},{4,6},{5,7},{6,0},{7,1},{8,10},{9,11},{10,... | collective-permute-start | bytes 1966088 | tf_op jit(solution)/shard_map/ppermute | solution.py:515
  34.3 18.2 %collective-permute-start.5 = (bf16[4,80,512]{2,1,0:T(8,128)(2,1)S(1)}, bf16[4,80,512]{2,1,0:T(8,128)(2,1)S(1)}, u32[]{:S(2)}, u32[]{:S(2)}) collective-permute-start(bf16[4,80,512]{2,1,0:T(8,128)(2,1)S(1)} %get-tuple-element.288), channel_id=1, source_target_pairs={{0,1},{1,0},{2,3},{3,2},{4,5},{5,4},{6,7},{7,6},{8,9},{9,8},{10,11... | collective-permute-start | bytes 983048 | tf_op jit(solution)/shard_map/ppermute | solution.py:515
  34.9 15.5 %collective-permute-start.8 = (bf16[160,512]{1,0:T(8,128)(2,1)S(1)}, bf16[160,512]{1,0:T(8,128)(2,1)S(1)}, u32[]{:S(2)}, u32[]{:S(2)}) collective-permute-start(bf16[160,512]{1,0:T(8,128)(2,1)S(1)} %slice.82), channel_id=1, source_target_pairs={{0,2},{1,3},{2,4},{3,5},{4,6},{5,7},{6,0},{7,1},{8,10},{9,11},{10,... | collective-permute-start | bytes 491528 | tf_op jit(solution)/shard_map/ppermute | solution.py:515
  52.5 20.6 %collective-permute-start.11 = (bf16[640,512]{1,0:T(8,128)(2,1)}, bf16[640,512]{1,0:T(8,128)(2,1)}, u32[]{:S(2)}, u32[]{:S(2)}) collective-permute-start(bf16[640,512]{1,0:T(8,128)(2,1)} %collective-permute-done.6.refs_4_), channel_id=1, source_target_pairs={{0,1},{1,0},{2,3},{3,2},{4,5},{5,4},{6,7},{7,6},{8,9},{9,8},{10,11... | collective-permute-start | bytes 1966088 | tf_op jit(solution)/shard_map/ppermute | solution.py:515
  54.0 19.1 %collective-permute-start.10 = (bf16[640,512]{1,0:T(8,128)(2,1)}, bf16[640,512]{1,0:T(8,128)(2,1)}, u32[]{:S(2)}, u32[]{:S(2)}) collective-permute-start(bf16[640,512]{1,0:T(8,128)(2,1)} %collective-permute-done.6.refs_4_), channel_id=1, source_target_pairs={{0,2},{1,3},{2,4},{3,5},{4,6},{5,7},{6,0},{7,1},{8,10},{9,11},{10,... | collective-permute-start | bytes 1966088 | tf_op jit(solution)/shard_map/ppermute | solution.py:515
  56.8 16.3 %collective-permute-start.9 = (bf16[2,4,80,512]{3,2,1,0:T(8,128)(2,1)S(1)}, bf16[2,4,80,512]{3,2,1,0:T(8,128)(2,1)}, u32[]{:S(2)}, u32[]{:S(2)}) collective-permute-start(bf16[2,4,80,512]{3,2,1,0:T(8,128)(2,1)S(1)} %pad_maximum_fusion.1), channel_id=1, source_target_pairs={{0,16},{8,24},{16,0},{24,8},{1,17},{9,25},{17,1},{25,9},{2,18},{10... | collective-permute-start | bytes 1966088 | tf_op jit(solution)/shard_map/ppermute | solution.py:515
  57.4 15.7 %collective-permute-start.12 = (bf16[160,512]{1,0:T(8,128)(2,1)S(1)}, bf16[160,512]{1,0:T(8,128)(2,1)S(1)}, u32[]{:S(2)}, u32[]{:S(2)}) collective-permute-start(bf16[160,512]{1,0:T(8,128)(2,1)S(1)} %collective-permute-done.8), channel_id=1, source_target_pairs={{0,2},{1,3},{2,4},{3,5},{4,6},{5,7},{6,0},{7,1},{8,10},{9,11},{10,... | collective-permute-start | bytes 491528 | tf_op jit(solution)/shard_map/ppermute | solution.py:515
  58.3 16.0 %collective-permute-start.13 = (bf16[2,4,80,512]{3,2,1,0:T(8,128)(2,1)S(1)}, bf16[2,4,80,512]{3,2,1,0:T(8,128)(2,1)S(1)}, u32[]{:S(2)}, u32[]{:S(2)}) collective-permute-start(bf16[2,4,80,512]{3,2,1,0:T(8,128)(2,1)S(1)} %pad_maximum_fusion.1), channel_id=1, source_target_pairs={{0,8},{8,0},{16,24},{24,16},{1,9},{9,1},{17,25},{25,17},{2,10},{10... | collective-permute-start | bytes 1966088 | tf_op jit(solution)/shard_map/ppermute | solution.py:515
  73.1 2.5 collective-permute-start.14
  73.8 22.2 %collective-permute-start.17 = (bf16[640,512]{1,0:T(8,128)(2,1)}, bf16[640,512]{1,0:T(8,128)(2,1)S(1)}, u32[]{:S(2)}, u32[]{:S(2)}) collective-permute-start(bf16[640,512]{1,0:T(8,128)(2,1)} %collective-permute-done.10.refs_6_), channel_id=1, source_target_pairs={{0,1},{1,0},{2,3},{3,2},{4,5},{5,4},{6,7},{7,6},{8,9},{9,8},{10,11... | collective-permute-start | bytes 1966088 | tf_op jit(solution)/shard_map/ppermute | solution.py:515
  78.9 19.2 %collective-permute-start.16 = (bf16[4,80,512]{2,1,0:T(8,128)(2,1)S(1)}, bf16[4,80,512]{2,1,0:T(8,128)(2,1)S(1)}, u32[]{:S(2)}, u32[]{:S(2)}) collective-permute-start(bf16[4,80,512]{2,1,0:T(8,128)(2,1)S(1)} %get-tuple-element.286), channel_id=1, source_target_pairs={{0,1},{1,0},{2,3},{3,2},{4,5},{5,4},{6,7},{7,6},{8,9},{9,8},{10,11... | collective-permute-start | bytes 983048 | tf_op jit(solution)/shard_map/ppermute | solution.py:515
  80.0 18.1 %collective-permute-start.15 = (bf16[4,80,512]{2,1,0:T(8,128)(2,1)S(1)}, bf16[4,80,512]{2,1,0:T(8,128)(2,1)S(1)}, u32[]{:S(2)}, u32[]{:S(2)}) collective-permute-start(bf16[4,80,512]{2,1,0:T(8,128)(2,1)S(1)} %get-tuple-element.284), channel_id=1, source_target_pairs={{0,16},{8,24},{16,0},{24,8},{1,17},{9,25},{17,1},{25,9},{2,18},{10... | collective-permute-start | bytes 983048 | tf_op jit(solution)/shard_map/ppermute | solution.py:515
  98.2 24.1 %collective-permute-start.22 = (bf16[2,4,80,512]{3,2,1,0:T(8,128)(2,1)S(1)}, bf16[2,4,80,512]{3,2,1,0:T(8,128)(2,1)S(1)}, u32[]{:S(2)}, u32[]{:S(2)}) collective-permute-start(bf16[2,4,80,512]{3,2,1,0:T(8,128)(2,1)S(1)} %pad_maximum_fusion.3), channel_id=1, source_target_pairs={{0,8},{8,0},{16,24},{24,16},{1,9},{9,1},{17,25},{25,17},{2,10},{10... | collective-permute-start | bytes 1966088 | tf_op jit(solution)/shard_map/ppermute | solution.py:515
  98.3 21.9 %collective-permute-start.19 = (bf16[2,4,80,512]{3,2,1,0:T(8,128)(2,1)S(1)}, bf16[2,4,80,512]{3,2,1,0:T(8,128)(2,1)}, u32[]{:S(2)}, u32[]{:S(2)}) collective-permute-start(bf16[2,4,80,512]{3,2,1,0:T(8,128)(2,1)S(1)} %pad_maximum_fusion.3), channel_id=1, source_target_pairs={{0,1},{1,0},{2,3},{3,2},{4,5},{5,4},{6,7},{7,6},{8,9},{9,8},{10,11... | collective-permute-start | bytes 1966088 | tf_op jit(solution)/shard_map/ppermute | solution.py:515
  99.0 23.3 %collective-permute-start.20 = (bf16[2,4,80,512]{3,2,1,0:T(8,128)(2,1)S(1)}, bf16[2,4,80,512]{3,2,1,0:T(8,128)(2,1)S(1)}, u32[]{:S(2)}, u32[]{:S(2)}) collective-permute-start(bf16[2,4,80,512]{3,2,1,0:T(8,128)(2,1)S(1)} %pad_maximum_fusion.2), channel_id=1, source_target_pairs={{0,8},{8,0},{16,24},{24,16},{1,9},{9,1},{17,25},{25,17},{2,10},{10... | collective-permute-start | bytes 1966088 | tf_op jit(solution)/shard_map/ppermute | solution.py:515
  99.2 21.0 %collective-permute-start.18 = (bf16[2,4,80,512]{3,2,1,0:T(8,128)(2,1)S(1)}, bf16[2,4,80,512]{3,2,1,0:T(8,128)(2,1)}, u32[]{:S(2)}, u32[]{:S(2)}) collective-permute-start(bf16[2,4,80,512]{3,2,1,0:T(8,128)(2,1)S(1)} %pad_maximum_fusion.2), channel_id=1, source_target_pairs={{0,16},{8,24},{16,0},{24,8},{1,17},{9,25},{17,1},{25,9},{2,18},{10... | collective-permute-start | bytes 1966088 | tf_op jit(solution)/shard_map/ppermute | solution.py:515
  120.2 2.5 collective-permute-start.21
  120.3 3.3 %collective-permute-start.23 = (bf16[2,4,80,512]{3,2,1,0:T(8,128)(2,1)}, bf16[2,4,80,512]{3,2,1,0:T(8,128)(2,1)}, u32[]{:S(2)}, u32[]{:S(2)}) collective-permute-start(bf16[2,4,80,512]{3,2,1,0:T(8,128)(2,1)} %collective-permute-done.19), channel_id=1, source_target_pairs={{0,8},{8,0},{16,24},{24,16},{1,9},{9,1},{17,25},{25,17},{2,10},{10... | collective-permute-start | bytes 1966088 | tf_op jit(solution)/shard_map/ppermute | solution.py:515
  144.2 3.5 %collective-permute-start.24 = (bf16[4,2,176,512]{3,2,1,0:T(8,128)(2,1)}, bf16[4,2,176,512]{3,2,1,0:T(8,128)(2,1)S(1)}, u32[]{:S(2)}, u32[]{:S(2)}) collective-permute-start(bf16[4,2,176,512]{3,2,1,0:T(8,128)(2,1)} %bitcast.150), channel_id=1, source_target_pairs={{0,8},{8,0},{16,24},{24,16},{1,9},{9,1},{17,25},{25,17},{2,10},{10... | collective-permute-start | bytes 4325384 | tf_op jit(solution)/shard_map/ppermute | solution.py:515
  144.4 5.4 %collective-permute-start.25 = (bf16[4,2,176,512]{3,2,1,0:T(8,128)(2,1)}, bf16[4,2,176,512]{3,2,1,0:T(8,128)(2,1)S(1)}, u32[]{:S(2)}, u32[]{:S(2)}) collective-permute-start(bf16[4,2,176,512]{3,2,1,0:T(8,128)(2,1)} %bitcast.149), channel_id=1, source_target_pairs={{0,8},{8,0},{16,24},{24,16},{1,9},{9,1},{17,25},{25,17},{2,10},{10... | collective-permute-start | bytes 4325384 | tf_op jit(solution)/shard_map/ppermute | solution.py:515
  150.3 33.8 %collective-permute-start.26 = (bf16[4,2,176,512]{3,2,1,0:T(8,128)(2,1)S(1)}, bf16[4,2,176,512]{3,2,1,0:T(8,128)(2,1)}, u32[]{:S(2)}, u32[]{:S(2)}) collective-permute-start(bf16[4,2,176,512]{3,2,1,0:T(8,128)(2,1)S(1)} %fusion), channel_id=1, source_target_pairs={{0,16},{8,24},{16,0},{24,8},{1,17},{9,25},{17,1},{25,9},{2,18},{10... | collective-permute-start | bytes 4325384 | tf_op jit(solution)/shard_map/ppermute | solution.py:515
  185.1 14.2 %collective-permute-start.28 = (bf16[2,176,512]{2,1,0:T(8,128)(2,1)S(1)}, bf16[2,176,512]{2,1,0:T(8,128)(2,1)S(1)}, u32[]{:S(2)}, u32[]{:S(2)}) collective-permute-start(bf16[2,176,512]{2,1,0:T(8,128)(2,1)S(1)} %fusion.6), channel_id=1, source_target_pairs={{0,6},{1,7},{2,0},{3,1},{4,2},{5,3},{6,4},{7,5},{8,14},{9,15},{10,... | collective-permute-start | bytes 1081352 | tf_op jit(solution)/shard_map/ppermute | solution.py:515
  188.5 18.6 %collective-permute-start.27 = (bf16[5,512,128]{2,1,0:T(8,128)(2,1)}, bf16[5,512,128]{2,1,0:T(8,128)(2,1)S(1)}, u32[]{:S(2)}, u32[]{:S(2)}) collective-permute-start(bf16[5,512,128]{2,1,0:T(8,128)(2,1)} %get-tuple-element.219), channel_id=1, source_target_pairs={{0,1},{1,0},{2,3},{3,2},{4,5},{5,4},{6,7},{7,6},{8,9},{9,8},{10,11... | collective-permute-start | bytes 1966088 | tf_op jit(solution)/shard_map/ppermute | solution.py:515
  200.5 11.0 %collective-permute-start.29 = (bf16[2,176,512]{2,1,0:T(8,128)(2,1)S(1)}, bf16[2,176,512]{2,1,0:T(8,128)(2,1)S(1)}, u32[]{:S(2)}, u32[]{:S(2)}) collective-permute-start(bf16[2,176,512]{2,1,0:T(8,128)(2,1)S(1)} %fusion.4), channel_id=1, source_target_pairs={{0,6},{1,7},{2,0},{3,1},{4,2},{5,3},{6,4},{7,5},{8,14},{9,15},{10,... | collective-permute-start | bytes 1081352 | tf_op jit(solution)/shard_map/ppermute | solution.py:515
  211.6 2.1 collective-permute-start.32
  211.6 17.1 %collective-permute-start.30 = (bf16[5,512,128]{2,1,0:T(8,128)(2,1)S(1)}, bf16[5,512,128]{2,1,0:T(8,128)(2,1)S(1)}, u32[]{:S(2)}, u32[]{:S(2)}) collective-permute-start(bf16[5,512,128]{2,1,0:T(8,128)(2,1)S(1)} %copy-done.23), channel_id=1, source_target_pairs={{0,1},{1,0},{2,3},{3,2},{4,5},{5,4},{6,7},{7,6},{8,9},{9,8},{10,11... | collective-permute-start | bytes 1966088 | tf_op jit(solution)/shard_map/ppermute | solution.py:515
  212.2 18.9 %collective-permute-start.31 = (bf16[5,512,128]{2,1,0:T(8,128)(2,1)S(1)}, bf16[5,512,128]{2,1,0:T(8,128)(2,1)S(1)}, u32[]{:S(2)}, u32[]{:S(2)}) collective-permute-start(bf16[5,512,128]{2,1,0:T(8,128)(2,1)S(1)} %add_convert_fusion.2), channel_id=1, source_target_pairs={{0,6},{1,7},{2,0},{3,1},{4,2},{5,3},{6,4},{7,5},{8,14},{9,15},{10,... | collective-permute-start | bytes 1966088 | tf_op jit(solution)/shard_map/ppermute | solution.py:515
  213.9 17.2 %collective-permute-start.33 = (bf16[2,4,64,512]{3,2,1,0:T(8,128)(2,1)S(1)}, bf16[2,4,64,512]{3,2,1,0:T(8,128)(2,1)S(1)}, u32[]{:S(2)}, u32[]{:S(2)}) collective-permute-start(bf16[2,4,64,512]{3,2,1,0:T(8,128)(2,1)S(1)} %add_convert_fusion.5), channel_id=1, source_target_pairs={{0,16},{8,24},{16,0},{24,8},{1,17},{9,25},{17,1},{25,9},{2,18},{10... | collective-permute-start | bytes 1572872 | tf_op jit(solution)/shard_map/ppermute | solution.py:515
  215.8 18.6 %collective-permute-start.36 = (bf16[2,4,64,512]{3,2,1,0:T(8,128)(2,1)S(1)}, bf16[2,4,64,512]{3,2,1,0:T(8,128)(2,1)S(1)}, u32[]{:S(2)}, u32[]{:S(2)}) collective-permute-start(bf16[2,4,64,512]{3,2,1,0:T(8,128)(2,1)S(1)} %bitcast.154), channel_id=1, source_target_pairs={{0,8},{8,0},{16,24},{24,16},{1,9},{9,1},{17,25},{25,17},{2,10},{10... | collective-permute-start | bytes 1572872 | tf_op jit(solution)/shard_map/ppermute | solution.py:515
  232.2 21.7 %collective-permute-start.38 = (bf16[2,176,512]{2,1,0:T(8,128)(2,1)S(1)}, bf16[2,176,512]{2,1,0:T(8,128)(2,1)S(1)}, u32[]{:S(2)}, u32[]{:S(2)}) collective-permute-start(bf16[2,176,512]{2,1,0:T(8,128)(2,1)S(1)} %fusion.3), channel_id=1, source_target_pairs={{0,6},{1,7},{2,0},{3,1},{4,2},{5,3},{6,4},{7,5},{8,14},{9,15},{10,... | collective-permute-start | bytes 1081352 | tf_op jit(solution)/shard_map/ppermute | solution.py:515
  232.3 21.7 %collective-permute-start.34 = (bf16[5,512,128]{2,1,0:T(8,128)(2,1)S(1)}, bf16[5,512,128]{2,1,0:T(8,128)(2,1)S(1)}, u32[]{:S(2)}, u32[]{:S(2)}) collective-permute-start(bf16[5,512,128]{2,1,0:T(8,128)(2,1)S(1)} %copy-done.19), channel_id=1, source_target_pairs={{0,1},{1,0},{2,3},{3,2},{4,5},{5,4},{6,7},{7,6},{8,9},{9,8},{10,11... | collective-permute-start | bytes 1966088 | tf_op jit(solution)/shard_map/ppermute | solution.py:515
  234.3 23.5 %collective-permute-start.35 = (bf16[5,512,128]{2,1,0:T(8,128)(2,1)S(1)}, bf16[5,512,128]{2,1,0:T(8,128)(2,1)S(1)}, u32[]{:S(2)}, u32[]{:S(2)}) collective-permute-start(bf16[5,512,128]{2,1,0:T(8,128)(2,1)S(1)} %add_convert_fusion.1), channel_id=1, source_target_pairs={{0,6},{1,7},{2,0},{3,1},{4,2},{5,3},{6,4},{7,5},{8,14},{9,15},{10,... | collective-permute-start | bytes 1966088 | tf_op jit(solution)/shard_map/ppermute | solution.py:515
  234.6 19.3 %collective-permute-start.37 = (bf16[4,64,512]{2,1,0:T(8,128)(2,1)S(1)}, bf16[4,64,512]{2,1,0:T(8,128)(2,1)S(1)}, u32[]{:S(2)}, u32[]{:S(2)}) collective-permute-start(bf16[4,64,512]{2,1,0:T(8,128)(2,1)S(1)} %slice_bitcast_fusion.1), channel_id=1, source_target_pairs={{0,1},{1,0},{2,3},{3,2},{4,5},{5,4},{6,7},{7,6},{8,9},{9,8},{10,11... | collective-permute-start | bytes 786440 | tf_op jit(solution)/shard_map/ppermute | solution.py:515
  258.9 15.1 %collective-permute-start.39 = (bf16[5,512,128]{2,1,0:T(8,128)(2,1)S(1)}, bf16[5,512,128]{2,1,0:T(8,128)(2,1)S(1)}, u32[]{:S(2)}, u32[]{:S(2)}) collective-permute-start(bf16[5,512,128]{2,1,0:T(8,128)(2,1)S(1)} %copy-done.18), channel_id=1, source_target_pairs={{0,1},{1,0},{2,3},{3,2},{4,5},{5,4},{6,7},{7,6},{8,9},{9,8},{10,11... | collective-permute-start | bytes 1966088 | tf_op jit(solution)/shard_map/ppermute | solution.py:515
  260.8 18.8 %collective-permute-start.40 = (bf16[5,512,128]{2,1,0:T(8,128)(2,1)S(1)}, bf16[5,512,128]{2,1,0:T(8,128)(2,1)S(1)}, u32[]{:S(2)}, u32[]{:S(2)}) collective-permute-start(bf16[5,512,128]{2,1,0:T(8,128)(2,1)S(1)} %add_convert_fusion), channel_id=1, source_target_pairs={{0,6},{1,7},{2,0},{3,1},{4,2},{5,3},{6,4},{7,5},{8,14},{9,15},{10,... | collective-permute-start | bytes 1966088 | tf_op jit(solution)/shard_map/ppermute | solution.py:515
  262.3 22.8 %collective-permute-start.44 = (bf16[64,512]{1,0:T(8,128)(2,1)S(1)}, bf16[64,512]{1,0:T(8,128)(2,1)S(1)}, u32[]{:S(2)}, u32[]{:S(2)}) collective-permute-start(bf16[64,512]{1,0:T(8,128)(2,1)S(1)} %get-tuple-element.290), channel_id=1, source_target_pairs={{0,2},{1,3},{2,4},{3,5},{4,6},{5,7},{6,0},{7,1},{8,10},{9,11},{10,... | collective-permute-start | bytes 196616 | tf_op jit(solution)/shard_map/ppermute | solution.py:515
  266.1 19.0 %collective-permute-start.43 = (bf16[64,512]{1,0:T(8,128)(2,1)S(1)}, bf16[64,512]{1,0:T(8,128)(2,1)S(1)}, u32[]{:S(2)}, u32[]{:S(2)}) collective-permute-start(bf16[64,512]{1,0:T(8,128)(2,1)S(1)} %get-tuple-element.291), channel_id=1, source_target_pairs={{0,4},{1,5},{2,6},{3,7},{4,0},{5,1},{6,2},{7,3},{8,12},{9,13},{10,... | collective-permute-start | bytes 196616 | tf_op jit(solution)/shard_map/ppermute | solution.py:515
  266.1 19.0 %collective-permute-start.42 = (bf16[64,512]{1,0:T(8,128)(2,1)S(1)}, bf16[64,512]{1,0:T(8,128)(2,1)S(1)}, u32[]{:S(2)}, u32[]{:S(2)}) collective-permute-start(bf16[64,512]{1,0:T(8,128)(2,1)S(1)} %get-tuple-element.292), channel_id=1, source_target_pairs={{0,6},{1,7},{2,0},{3,1},{4,2},{5,3},{6,4},{7,5},{8,14},{9,15},{10,... | collective-permute-start | bytes 196616 | tf_op jit(solution)/shard_map/ppermute | solution.py:515
  274.0 11.2 %collective-permute-start.41 = (bf16[176,512]{1,0:T(8,128)(2,1)S(1)}, bf16[176,512]{1,0:T(8,128)(2,1)S(1)}, u32[]{:S(2)}, u32[]{:S(2)}) collective-permute-start(bf16[176,512]{1,0:T(8,128)(2,1)S(1)} %get-tuple-element.249), channel_id=1, source_target_pairs={{0,1},{1,0},{2,3},{3,2},{4,5},{5,4},{6,7},{7,6},{8,9},{9,8},{10,11... | collective-permute-start | bytes 540680 | tf_op jit(solution)/shard_map/ppermute | solution.py:515
  (29 other events, 234.4 us)
